TPU v7x, 256 devices: a whole 4x4x8 slice. The times are simulated.
256 devices in a mesh: group: 4 (over y_hi, core), space: 64 (over y_lo, z, x).
Axes of the slice: x: 4, y: 4 (y_hi: 2, y_lo: 2; y = y_hi * 2 + y_lo), z: 8, core: 2. Of those that a mesh axis runs over, the one named last changes fastest.
Arguments:
- initial: float32 [512, 256, 128], P('space'), may hold values from -6 to 6
- source: float32 [512, 256, 128], P('space'), may hold values from -3 to 3
- table: float32 [8, 6], replicated, may hold values from 0 to 1
- pairs: int32 [4, 2], P('group'), may hold values from 0 to 7, as said below
- owner: int32 [256], replicated, may hold values from 0 to 255, each once
Outputs:
- mean: float32 [512, 256, 128], P(None, ('group', 'space'))
- variance: float32 [512, 256, 128], P(None, ('group', 'space'))
- first: float32 [6, 512, 256, 128], P(None, None, ('group', 'space'))
- total: float32 [6, 512, 256, 128], P(None, None, ('group', 'space'))
Inputs may be any that keep to these rules, and one draw needn't show every extreme that they name: Every row of table appears exactly once in pairs. `owner`: every server slab position appears exactly once.
All inputs are finite; a program needn't handle non-finite values.
Results may differ from a plain program's by a relative error of at most 0.0003.
Values sent between devices are 32-bit elements; how exact they have to be, the bound alone decides.
No kernel may reach another device: no remote copies, remote signals or barrier semaphores. Data moves between devices by JAX's collectives and lax.ppermute only.
A program may use at most 128 MiB of HBM per device.

v0:
```python
import jax
import jax.numpy as jnp
from jax import lax
from jax.sharding import PartitionSpec as P

STEPS = 3


def extended_2(cells, sides, width):
    for axis, dim in sides:
        count = lax.axis_size(axis)
        ends = count - 1
        head = lax.slice_in_dim(cells, 0, width, axis=dim)
        tail = lax.slice_in_dim(cells, cells.shape[dim] - width, cells.shape[dim], axis=dim)
        cells = jnp.concatenate(
            [
                lax.ppermute(tail, axis, [(i, (i + 1) % count) for i in range(ends)]),
                cells,
                lax.ppermute(head, axis, [((i + 1) % count, i) for i in range(ends)]),
            ],
            axis=dim,
        )
    return cells


def run_params(table, pairs):
    labels = jnp.arange(table.shape[0], dtype=jnp.int32)
    pick_first = (pairs[:, 0][:, None] == labels[None, :]).astype(jnp.float32)
    pick_second = (pairs[:, 1][:, None] == labels[None, :]).astype(jnp.float32)
    first_draw = jnp.dot(pick_first, table, precision=lax.Precision.HIGHEST)
    second_draw = jnp.dot(pick_second, table, precision=lax.Precision.HIGHEST)
    frozen = jnp.eye(table.shape[1], dtype=jnp.int32) > 0
    mixed = jnp.where(frozen[None], second_draw[:, None, :], first_draw[:, None, :])
    return jnp.concatenate([first_draw[:, None], second_draw[:, None], mixed], axis=1)


def coefficients(unit):
    return (
        0.03 + 0.12 * unit[..., 0],
        0.3 * unit[..., 1] - 0.15,
        0.3 * unit[..., 2] - 0.15,
        0.3 * unit[..., 3] - 0.15,
        0.02 + 0.2 * unit[..., 4],
        0.5 + 1.5 * unit[..., 5],
    )


def advance(extended, source, coeffs):
    diffusion, speed_x, speed_y, speed_z, decay, strength = coeffs
    inner = extended[..., 1:-1, :, :]
    widths = [(0, 0)] * (inner.ndim - 2) + [(1, 1), (1, 1)]
    padded = jnp.pad(inner, widths)
    east = extended[..., 2:, :, :]
    west = extended[..., :-2, :, :]
    north = padded[..., 2:, 1:-1]
    south = padded[..., :-2, 1:-1]
    upper = padded[..., 1:-1, 2:]
    lower = padded[..., 1:-1, :-2]
    laplace = east + west + north + south + upper + lower - 6.0 * inner
    transport = speed_x * (east - west) + speed_y * (north - south) + speed_z * (upper - lower)
    return inner + diffusion * laplace - 0.5 * transport - decay * inner + strength * source


def local(initial, source, table, pairs, owner):
    params = run_params(table, pairs)
    local_groups, runs, unused = params.shape
    count = local_groups * runs
    flat = params.reshape(count, params.shape[2])
    coeffs = tuple((value[:, None, None, None] for value in coefficients(flat)))
    tile_x, rows_y, cells_z = initial.shape
    fields = jnp.broadcast_to(initial[None], (count, tile_x, rows_y, cells_z))
    for moment in range(STEPS):
        extended = extended_2(fields, (("space", 1),), 1)
        fields = advance(extended, source, coeffs)
    group_count = lax.axis_size("group")
    space_count = lax.axis_size("space")
    servers = group_count * space_count
    slab_rows = rows_y // servers
    blocks = fields.reshape(count, tile_x, servers, slab_rows, cells_z)
    inverse = jnp.zeros((servers,), jnp.int32).at[owner].set(jnp.arange(servers, dtype=jnp.int32))
    ordered = jnp.take(blocks, inverse, axis=2).reshape(count, tile_x, rows_y, cells_z)
    arrived = lax.all_to_all(
        lax.all_to_all(ordered, "group", split_axis=2, concat_axis=0, tiled=True),
        "space",
        split_axis=2,
        concat_axis=1,
        tiled=True,
    )
    samples = arrived.reshape((-1, runs) + arrived.shape[1:])
    group_total = samples.shape[0]
    runs_a = samples[:, 0]
    runs_b = samples[:, 1]
    mixed_runs = samples[:, 2:]
    gap = runs_a[:, None] - mixed_runs
    mean = jnp.sum(runs_a + runs_b, axis=0) / (2.0 * group_total)
    variance = (
        jnp.sum(runs_a * runs_a + runs_b * runs_b, axis=0) / (2.0 * group_total) - mean * mean
    )
    first = -jnp.sum(runs_b[:, None] * gap, axis=0) / (1.0 * group_total)
    total = jnp.sum(gap * gap, axis=0) / (2.0 * group_total)
    return (mean, variance, first, total)


def solution(mesh):
    placed = (P("space", None, None), P("space", None, None), P(), P("group", None), P())
    return jax.shard_map(
        local,
        mesh=mesh,
        in_specs=placed,
        out_specs=(
            P(None, ("group", "space"), None),
            P(None, ("group", "space"), None),
            P(None, None, ("group", "space"), None),
            P(None, None, ("group", "space"), None),
        ),
        check_vma=False,
    )
```

profile of v0, /device:TPU:6, one launch (start us, length us, event | category | flops | bytes accessed | tf_op | source)
XLA Modules:
  0.0 490.6 jit_solution(10781842721426973846)
XLA Ops:
  0.7 1.0 slice_bitcast_fusion.3
  2.2 2.7 collective-permute-start
  5.5 5.2 %collective-permute-start.1 = (f32[8,1,256,128]{3,1,2,0:T(1,128)S(1)}, f32[8,1,256,128]{3,1,2,0:T(1,128)S(1)}, u32[]{:S(2)}, u32[]{:S(2)}) collective-permute-start(f32[8,1,256,128]{3,1,2,0:T(1,128)S(1)} %broadcast_in_dim.71), channel_id=1, source_target_pairs={{0,1},{1,2},{2,3},{3,4},{4,5},{5,6},{6,7},{7,8},{8,9},{9,10},{10,1... | collective-permute-start | bytes 3145736 | tf_op jit(solution)/shard_map/ppermute | solution.py:17
  10.7 1.3 broadcast_multiply_fusion.1
  12.0 1.8 copy.14
  13.9 1.8 copy.16
  18.7 12.4 %collective-permute-done = f32[8,1,256,128]{3,1,2,0:T(1,128)S(1)} collective-permute-done((f32[8,1,256,128]{3,1,2,0:T(1,128)S(1)}, f32[8,1,256,128]{3,1,2,0:T(1,128)S(1)}, u32[]{:S(2)}, u32[]{:S(2)}) %collective-permute-start) | collective-permute-done | bytes 1048608 | tf_op jit(solution)/shard_map/ppermute | solution.py:19
  31.1 1.7 collective-permute-done.1
  34.4 11.4 %multiply_add_fusion.2 = f32[8,8,256,128]{3,1,2,0:T(8,128)S(1)} fusion(f32[8,8,256,128]{3,1,2,0:T(8,128)S(1)} %broadcast_in_dim.65, f32[8,1,256,128]{3,1,2,0:T(1,128)} %copy-done.5, f32[8,1,256,128]{3,1,2,0:T(1,128)} %copy-done.4, f32[8,256,128]{2,0,1:T(8,128)S(1)} %copy.16, f32[8]{0:T(128)S(1)} %get-tuple-element.9, f32[8]{0:T(128)S(1)} %get-tuple-element.10, ...), kind=kLoop, calls=%fused_computation.16 | loop fusion | flops 50331648 | bytes 20971712 | tf_op jit(solution)/shard_map/add | solution.py:61
  45.8 3.3 fusion.33
  49.1 1.9 collective-permute-start.2
  51.0 6.5 %collective-permute-start.3 = (f32[8,1,256,128]{3,1,2,0:T(1,128)}, f32[8,1,256,128]{3,1,2,0:T(1,128)S(1)}, u32[]{:S(2)}, u32[]{:S(2)}) collective-permute-start(f32[8,1,256,128]{3,1,2,0:T(1,128)} %get-tuple-element.18), channel_id=1, source_target_pairs={{0,1},{1,2},{2,3},{3,4},{4,5},{5,6},{6,7},{7,8},{8,9},{9,10},{10,1... | collective-permute-start | bytes 3145736 | tf_op jit(solution)/shard_map/ppermute | solution.py:17
  57.5 20.2 %collective-permute-done.2 = f32[8,1,256,128]{3,1,2,0:T(1,128)S(1)} collective-permute-done((f32[8,1,256,128]{3,1,2,0:T(1,128)}, f32[8,1,256,128]{3,1,2,0:T(1,128)S(1)}, u32[]{:S(2)}, u32[]{:S(2)}) %collective-permute-start.2) | collective-permute-done | bytes 1048608 | tf_op jit(solution)/shard_map/ppermute | solution.py:19
  77.8 1.3 collective-permute-done.3
  79.1 22.9 %multiply_add_fusion.1 = f32[8,8,256,128]{3,1,2,0:T(8,128)S(1)} fusion(f32[8,8,256,128]{3,1,2,0:T(8,128)} %copy-done.3, f32[8,1,256,128]{3,1,2,0:T(1,128)S(1)} %collective-permute-done.2, f32[8,1,256,128]{3,1,2,0:T(1,128)S(1)} %collective-permute-done.3, f32[8,256,128]{2,0,1:T(8,128)S(1)} %copy.16, f32[8]{0:T(128)S(1)} %get-tuple-element.9, ...), kind=kLoop, calls=%fused_computation.15 | loop fusion | flops 52428800 | bytes 19923136 | tf_op jit(solution)/shard_map/add | solution.py:61
  102.0 3.2 copy-done.2
  105.2 2.8 fusion.32
  108.0 1.9 collective-permute-start.4
  109.9 6.6 %collective-permute-start.5 = (f32[8,1,256,128]{3,1,2,0:T(1,128)}, f32[8,1,256,128]{3,1,2,0:T(1,128)}, u32[]{:S(2)}, u32[]{:S(2)}) collective-permute-start(f32[8,1,256,128]{3,1,2,0:T(1,128)} %get-tuple-element.16), channel_id=1, source_target_pairs={{0,1},{1,2},{2,3},{3,4},{4,5},{5,6},{6,7},{7,8},{8,9},{9,10},{10,1... | collective-permute-start | bytes 3145736 | tf_op jit(solution)/shard_map/ppermute | solution.py:17
  116.5 1.4 scatter_custom_fusion
  118.0 17.7 %collective-permute-done.4 = f32[8,1,256,128]{3,1,2,0:T(1,128)S(1)} collective-permute-done((f32[8,1,256,128]{3,1,2,0:T(1,128)}, f32[8,1,256,128]{3,1,2,0:T(1,128)S(1)}, u32[]{:S(2)}, u32[]{:S(2)}) %collective-permute-start.4) | collective-permute-done | bytes 1048608 | tf_op jit(solution)/shard_map/ppermute | solution.py:19
  135.6 1.3 collective-permute-done.5
  136.9 24.7 %multiply_add_fusion = f32[8,8,256,128]{3,1,2,0:T(8,128)} fusion(f32[8,8,256,128]{3,1,2,0:T(8,128)} %copy-done.2, f32[8,1,256,128]{3,1,2,0:T(1,128)S(1)} %collective-permute-done.4, f32[8,1,256,128]{3,1,2,0:T(1,128)} %collective-permute-done.5, f32[8,256,128]{2,0,1:T(8,128)S(1)} %copy.16, f32[8]{0:T(128)S(1)} %get-tuple-element.9, ...), kind=kLoop, calls=%fused_computation.14 | loop fusion | flops 52428800 | bytes 19923136 | tf_op jit(solution)/shard_map/add | solution.py:61
  161.6 8.2 %gather_fusion = f32[256,8,8,128]{3,2,1,0:T(8,128)} fusion(f32[8,8,256,128]{3,1,2,0:T(8,128)} %multiply_add_fusion, s32[1024]{0:T(1024)S(1)} %pad_clamp_fusion), kind=kCustom, calls=%fused_computation | custom fusion | bytes 16778240 | tf_op jit(solution)/shard_map/jit(_take)/gather | solution.py:81
  169.8 4.0 select_bitcast_fusion
  173.9 98.9 %all_to_all.33 = f32[8,8,256,128]{3,1,0,2:T(8,128)S(1)} all-to-all(f32[8,8,256,128]{3,1,0,2:T(8,128)S(1)} %select_bitcast_fusion), channel_id=1, replica_groups=mesh['group'=4,'space'=64] {'group'}, dimensions={2} | all-to-all | bytes 16777216 | tf_op jit(solution)/shard_map/all_to_all | solution.py:83
  272.7 4.9 copy.17
  277.6 4.9 copy.18
  282.5 202.8 %all_to_all.34 = f32[32,8,64,128]{3,1,0,2:T(8,128)S(1)} all-to-all(f32[32,8,64,128]{3,1,0,2:T(8,128)S(1)} %copy.18), channel_id=1, replica_groups=mesh['group'=4,'space'=64] {'space'}, dimensions={2} | all-to-all | bytes 16777216 | tf_op jit(solution)/shard_map/all_to_all | solution.py:82
  485.3 1.0 copy.19
  486.6 1.2 multiply_reduce_fusion
  487.9 1.9 negate_multiply_fusion
  (35 shorter events, 6.8 us)
Async XLA Ops:
  0.6 16.3 %copy-start = (f32[8,6]{1,0:T(8,128)S(1)}, f32[8,6]{1,0:T(8,128)}, u32[]{:S(2)}) copy-start(f32[8,6]{1,0:T(8,128)} %param.7) | copy-start | bytes 580
  0.6 15.7 %copy-start.7 = (s32[1,2]{1,0:T(1,128)S(1)}, s32[1,2]{1,0:T(1,128)}, u32[]{:S(2)}) copy-start(s32[1,2]{1,0:T(1,128)} %param.8) | copy-start | bytes 28
  2.2 28.9 %collective-permute-start = (f32[8,1,256,128]{3,1,2,0:T(1,128)S(1)}, f32[8,1,256,128]{3,1,2,0:T(1,128)S(1)}, u32[]{:S(2)}, u32[]{:S(2)}) collective-permute-start(f32[8,1,256,128]{3,1,2,0:T(1,128)S(1)} %broadcast_in_dim.70), channel_id=1, source_target_pairs={{1,0},{2,1},{3,2},{4,3},{5,4},{6,5},{7,6},{8,7},{9,8},{10,9},{11,1... | collective-permute-start | bytes 3145736 | tf_op jit(solution)/shard_map/ppermute | solution.py:19
  5.5 27.3 %collective-permute-start.1 = (f32[8,1,256,128]{3,1,2,0:T(1,128)S(1)}, f32[8,1,256,128]{3,1,2,0:T(1,128)S(1)}, u32[]{:S(2)}, u32[]{:S(2)}) collective-permute-start(f32[8,1,256,128]{3,1,2,0:T(1,128)S(1)} %broadcast_in_dim.71), channel_id=1, source_target_pairs={{0,1},{1,2},{2,3},{3,4},{4,5},{5,6},{6,7},{7,8},{8,9},{9,10},{10,1... | collective-permute-start | bytes 3145736 | tf_op jit(solution)/shard_map/ppermute | solution.py:17
  31.1 1.7 copy-start.4
  32.8 1.0 copy-start.5
  45.8 32.0 %copy-start.3 = (f32[8,8,256,128]{3,1,2,0:T(8,128)}, f32[8,8,256,128]{3,1,2,0:T(8,128)S(1)}, u32[]{:S(2)}) copy-start(f32[8,8,256,128]{3,1,2,0:T(8,128)S(1)} %multiply_add_fusion.2) | copy-start | bytes 25165828
  49.1 28.7 %collective-permute-start.2 = (f32[8,1,256,128]{3,1,2,0:T(1,128)}, f32[8,1,256,128]{3,1,2,0:T(1,128)S(1)}, u32[]{:S(2)}, u32[]{:S(2)}) collective-permute-start(f32[8,1,256,128]{3,1,2,0:T(1,128)} %get-tuple-element.19), channel_id=1, source_target_pairs={{1,0},{2,1},{3,2},{4,3},{5,4},{6,5},{7,6},{8,7},{9,8},{10,9},{11,1... | collective-permute-start | bytes 3145736 | tf_op jit(solution)/shard_map/ppermute | solution.py:19
  51.0 65.5 %copy-start.8 = (s32[256]{0:T(256)S(1)}, s32[256]{0:T(256)}, u32[]{:S(2)}) copy-start(s32[256]{0:T(256)} %param.9) | copy-start | bytes 3076
  51.0 28.0 %collective-permute-start.3 = (f32[8,1,256,128]{3,1,2,0:T(1,128)}, f32[8,1,256,128]{3,1,2,0:T(1,128)S(1)}, u32[]{:S(2)}, u32[]{:S(2)}) collective-permute-start(f32[8,1,256,128]{3,1,2,0:T(1,128)} %get-tuple-element.18), channel_id=1, source_target_pairs={{0,1},{1,2},{2,3},{3,4},{4,5},{5,6},{6,7},{7,8},{8,9},{9,10},{10,1... | collective-permute-start | bytes 3145736 | tf_op jit(solution)/shard_map/ppermute | solution.py:17
  101.9 3.2 copy-start.2
  108.0 27.6 %collective-permute-start.4 = (f32[8,1,256,128]{3,1,2,0:T(1,128)}, f32[8,1,256,128]{3,1,2,0:T(1,128)S(1)}, u32[]{:S(2)}, u32[]{:S(2)}) collective-permute-start(f32[8,1,256,128]{3,1,2,0:T(1,128)} %get-tuple-element.17), channel_id=1, source_target_pairs={{1,0},{2,1},{3,2},{4,3},{5,4},{6,5},{7,6},{8,7},{9,8},{10,9},{11,1... | collective-permute-start | bytes 3145736 | tf_op jit(solution)/shard_map/ppermute | solution.py:19
  109.9 27.0 %collective-permute-start.5 = (f32[8,1,256,128]{3,1,2,0:T(1,128)}, f32[8,1,256,128]{3,1,2,0:T(1,128)}, u32[]{:S(2)}, u32[]{:S(2)}) collective-permute-start(f32[8,1,256,128]{3,1,2,0:T(1,128)} %get-tuple-element.16), channel_id=1, source_target_pairs={{0,1},{1,2},{2,3},{3,4},{4,5},{5,6},{6,7},{7,8},{8,9},{9,10},{10,1... | collective-permute-start | bytes 3145736 | tf_op jit(solution)/shard_map/ppermute | solution.py:17
  486.6 4.0 copy-start.1
  489.8 0.8 copy-start.6
where the time goes:
time: 491 us
  blocking collectives  302 us (62%)
  other arithmetic  68.9 us (14%)
  waiting for transfers between devices  54.5 us (11%)
  local copies, waits for them, and re-layouts  38.2 us (8%)
  starting transfers between devices  24.8 us (5%)
    all_to_all x1, blocking collectives, local(): lax.all_to_all(lax.all_to_all(ordered, 'group', split_axis=2, concat_axis...  203 us
    all_to_all x1, blocking collectives, local(): lax.all_to_all(ordered, 'group', split_axis=2, concat_axis=0, tiled=True)  98.9 us
    add x3, other arithmetic, advance(): inner + diffusion * laplace - 0.5 * transport - decay * inner  59 us
    ppermute x3, waiting for transfers between devices, extended_2(): lax.ppermute(head, axis, [((i + 1) % count, i) for i in range(ends)])  50.2 us
    ppermute x3, starting transfers between devices, extended_2(): lax.ppermute(tail, axis, [(i, (i + 1) % count) for i in range(ends)])  18.3 us
  transfers between devices with their start and end apart: 6, of which 6 were waited for; matrix products, arithmetic and copies ran while one was open for 2% of the time, Pallas kernels for 0%

commit v1 on v0

v1 whole, which is shorter than its diff:
```python
import itertools

import jax
import jax.numpy as jnp
import numpy as np
from jax import lax
from jax.experimental import pallas as pl
from jax.experimental.pallas import tpu as pltpu
from jax.sharding import PartitionSpec as P


UROWS = 7
SROWS = 5
ROWS = UROWS + SROWS
PAIRS2 = list(itertools.combinations_with_replacement(range(4), 2))
PAIRS3 = list(itertools.combinations_with_replacement(range(4), 3))
FIELDS = 50
WIDE = 48
SECTION = WIDE * 8
DEPTH = 3 * SECTION + 128
ALPHA, KAPPA, HX, HY, HZ, STRENGTH, TWICE, SQUARE, ONE = range(9)


def terms():
    out = [(1.0, ALPHA, ALPHA, ALPHA)]
    out += [(3.0, ALPHA, ALPHA, 1 + i) for i in range(4)]
    for i, j in PAIRS2:
        many = 2.0 if i != j and i > 0 else 1.0
        out.append((3.0 * many, ALPHA, 1 + i, 1 + j))
    for i, j, k in PAIRS3:
        many = 1.0
        if i > 0:
            many = {1: 1.0, 2: 3.0, 3: 6.0}[len({i, j, k})]
        out.append((many, 1 + i, 1 + j, 1 + k))
    out.append((1.0, STRENGTH, SQUARE, ONE))
    out += [(1.0, STRENGTH, TWICE, 1 + i) for i in range(4)]
    for i, j in PAIRS2:
        many = 2.0 if i != j and i > 0 else 1.0
        out.append((many, STRENGTH, 1 + i, 1 + j))
    return out


def layout():
    listed = terms()
    factor = np.zeros((1, SECTION + 128), np.float32)
    which = np.full((3, SECTION + 128), ONE, np.int32)
    for column in range(SECTION + 128):
        if column < SECTION:
            feature = column // 8
        elif column < SECTION + 48:
            feature = WIDE + ((column - SECTION) // 8) % 2
        else:
            continue
        factor[0, column] = listed[feature][0]
        which[:, column] = listed[feature][1:]
    return factor, which


def pack_kernel(owner, place, initial, source, send, row, inverse):
    count = owner.shape[0]
    servers = send.shape[0]
    group, device = place[0], place[1]

    def invert(i, carry):
        inverse[owner[i]] = i
        return carry

    lax.fori_loop(0, count, invert, 0, unroll=8)
    row[0] = inverse[device]

    def fill(s, carry):
        p = inverse[group * servers + s]
        for array, rows, first in ((initial, UROWS, 0), (source, SROWS, UROWS)):
            for k in range(rows):
                y = p + k - rows // 2
                inside = jnp.logical_and(y >= 0, y < count)
                here = jnp.clip(y, 0, count - 1)
                value = array[pl.ds(here, 8, stride=count), :]
                send[s, first + k] = jnp.where(inside, value, 0.0)
        return carry

    lax.fori_loop(0, servers, fill, 0, unroll=2)


def shifted(value, lane):
    up = jnp.where(lane == 127, 0.0, pltpu.roll(value, 127, 1))
    down = jnp.where(lane == 0, 0.0, pltpu.roll(value, 1, 1))
    return up, down


def coefficients_into(table, pairs, factor, which, matrix):
    run = lax.broadcasted_iota(jnp.int32, (64, 128), 0) // 8
    same = (
        lax.broadcasted_iota(jnp.int32, (64, 128), 0) % 8
        == lax.broadcasted_iota(jnp.int32, (64, 128), 1) % 8
    )
    lane = lax.broadcasted_iota(jnp.int32, (64, 128), 1)
    for group in range(4):
        first, second = pairs[group, 0], pairs[group, 1]
        q = []
        for k in range(6):
            swap = jnp.logical_or(run == 1, run == 2 + k)
            q.append(jnp.where(swap, table[second, k], table[first, k]))
        kappa = 0.03 + 0.12 * q[0]
        hx, hy, hz = (-0.5 * (0.3 * q[1 + i] - 0.15) for i in range(3))
        decay = 0.02 + 0.2 * q[4]
        strength = 0.5 + 1.5 * q[5]
        alpha = 1.0 - 6.0 * kappa - decay
        values = [alpha, kappa, hx, hy, hz, strength, 2.0 * alpha + 1.0, alpha * alpha + alpha + 1.0]
        rows = slice(64 * group, 64 * group + 64)
        for chunk in range(SECTION // 128 + 1):
            columns = slice(128 * chunk, 128 * chunk + 128)
            product = jnp.broadcast_to(factor[:, columns], (64, 128))
            for part in range(3):
                index = jnp.broadcast_to(which[part : part + 1, columns], (64, 128))
                chosen = jnp.ones((64, 128), jnp.float32)
                for number, value in enumerate(values):
                    chosen = jnp.where(index == number, value, chosen)
                product = product * chosen
            split = product.reshape(8, 8, 128)
            split = jnp.concatenate([split[:2], split[2:] - split[:1]], axis=0)
            product = jnp.where(same, split.reshape(64, 128), 0.0)
            high = product.astype(jnp.bfloat16)
            low = (product - high.astype(jnp.float32)).astype(jnp.bfloat16)
            if chunk < SECTION // 128:
                matrix[rows, columns] = high
                matrix[rows, SECTION + 128 * chunk : SECTION + 128 * chunk + 128] = high
                matrix[rows, 2 * SECTION + 128 * chunk : 2 * SECTION + 128 * chunk + 128] = low
            else:
                tail = jnp.where(lane < 32, high.astype(jnp.float32), low.astype(jnp.float32))
                matrix[rows, 3 * SECTION :] = tail.astype(jnp.bfloat16)


def server_kernel(
    table, pairs, row, factor, which, received,
    mean, variance, first, total,
    u, s, f1, g1, f2, matrix, phi, result,
):
    blocks = 64
    p = row[0]
    lane = lax.broadcasted_iota(jnp.int32, (8, 128), 1)
    sub = lax.broadcasted_iota(jnp.int32, (8, 128), 0)
    keep = {k: jnp.where(jnp.logical_and(p + k >= 0, p + k < 256), 1.0, 0.0) for k in range(-2, 3)}

    def halo(ref, lead):
        ref[lead + (0,)] = jnp.where(sub == 0, 0.0, pltpu.roll(ref[lead + (blocks,)], 1, 0))
        ref[lead + (blocks + 1,)] = jnp.where(sub == 7, 0.0, pltpu.roll(ref[lead + (1,)], 7, 0))

    def copy(b, carry):
        start = (b // 8) * (ROWS * 8) + b % 8
        for k in range(ROWS):
            value = received[pl.ds(start + 8 * k, 8, stride=8 * ROWS * 8), :]
            if k < UROWS:
                u[k, b + 1] = value
            else:
                s[k - UROWS, b + 1] = value
        return carry

    lax.fori_loop(0, blocks, copy, 0, unroll=2)
    for k in range(UROWS):
        halo(u, (k,))
    for k in range(SROWS):
        halo(s, (k,))

    coefficients_into(table, pairs, factor, which, matrix)
    phi[...] = jnp.zeros(phi.shape, phi.dtype)

    def parts(ref, lead, k, b):
        c = ref[lead + (k, b + 1)]
        east, west = ref[lead + (k, b + 2)], ref[lead + (k, b)]
        north, south = ref[lead + (k + 1, b + 1)], ref[lead + (k - 1, b + 1)]
        up, down = shifted(c, lane)
        every = (east + west) + (north + south) + (up + down)
        return every, east - west, north - south, up - down

    def stage1(b, carry):
        for k in range(1, 6):
            out = parts(u, (), k, b)
            for i in range(4):
                value = out[i] if k == 3 else out[i] * keep[k - 3]
                f1[i, k - 1, b + 1] = value
        for k in range(1, 4):
            out = parts(s, (), k, b)
            for i in range(4):
                value = out[i] if k == 2 else out[i] * keep[k - 2]
                g1[i, k - 1, b + 1] = value
        return carry

    lax.fori_loop(0, blocks, stage1, 0)
    for i in range(4):
        for k in range(5):
            halo(f1, (i, k))
        for k in range(3):
            halo(g1, (i, k))

    def second(ref, k, b):
        a = [parts(ref, (i,), k, b) for i in range(4)]
        return [
            a[0][0],
            a[1][0] + a[0][1],
            a[2][0] + a[0][2],
            a[3][0] + a[0][3],
            a[1][1],
            a[2][1],
            a[3][1],
            a[2][2],
            a[3][2],
            a[3][3],
        ]

    def stage2(b, carry):
        for k in range(1, 4):
            for i, value in enumerate(second(f1, k, b)):
                f2[i, k - 1, b + 1] = value if k == 2 else value * keep[k - 2]
        return carry

    lax.fori_loop(0, blocks, stage2, 0)
    for i in range(10):
        for k in range(3):
            halo(f2, (i, k))

    def third(b):
        a = {pair: parts(f2, (i,), 1, b) for i, pair in enumerate(PAIRS2)}
        out = []
        for i, j, k in PAIRS3:
            if i > 0:
                value = a[(j, k)][i]
            elif j == 0 and k == 0:
                value = a[(0, 0)][0]
            elif j == 0:
                value = a[(0, k)][0] + a[(0, 0)][k]
            elif j == k:
                value = a[(j, j)][0] + a[(0, j)][j]
            else:
                value = 2.0 * a[(j, k)][0] + a[(0, k)][j] + a[(0, j)][k]
            out.append(value)
        return out

    def features(b):
        out = [u[3, b + 1]]
        out += [f1[i, 2, b + 1] for i in range(4)]
        out += [f2[i, 1, b + 1] for i in range(10)]
        out += third(b)
        out.append(s[2, b + 1])
        out += [g1[i, 1, b + 1] for i in range(4)]
        out += second(g1, 1, b)
        return out

    def stage3(pair, carry):
        for half in range(2):
            columns = slice(128 * half, 128 * half + 128)
            listed = features(2 * pair + half)
            for i in range(0, FIELDS, 2):
                value = jnp.concatenate([listed[i], listed[i + 1]], axis=0)
                high = value.astype(jnp.bfloat16)
                low = (value - high.astype(jnp.float32)).astype(jnp.bfloat16)
                if i < WIDE:
                    at = 8 * i
                    phi[at : at + 16, columns] = high
                    phi[SECTION + at : SECTION + at + 16, columns] = low
                    phi[2 * SECTION + at : 2 * SECTION + at + 16, columns] = high
                else:
                    at = 3 * SECTION
                    phi[at : at + 16, columns] = high
                    phi[at + 16 : at + 32, columns] = low
                    phi[at + 32 : at + 48, columns] = high
        result[...] = jnp.dot(matrix[...], phi[...], preferred_element_type=jnp.float32)
        for half in range(2):
            b = 2 * pair + half
            columns = slice(128 * half, 128 * half + 128)
            both = square = None
            firsts, totals = [None] * 6, [None] * 6

            def add(old, new):
                return new if old is None else old + new

            for group in range(4):
                base = 64 * group
                run_a = result[base : base + 8, columns]
                run_b = result[base + 8 : base + 16, columns]
                both = add(both, run_a + run_b)
                square = add(square, run_a * run_a + run_b * run_b)
                for i in range(6):
                    at = base + 16 + 8 * i
                    gap = result[at : at + 8, columns]
                    firsts[i] = add(firsts[i], run_b * gap)
                    totals[i] = add(totals[i], gap * gap)
            average = both * 0.125
            mean[pl.ds(b, 8, stride=64), :] = average
            variance[pl.ds(b, 8, stride=64), :] = square * 0.125 - average * average
            for i in range(6):
                first[pl.ds(512 * i + b, 8, stride=64), :] = firsts[i] * 0.25
                total[pl.ds(512 * i + b, 8, stride=64), :] = totals[i] * 0.125
        return carry

    lax.fori_loop(0, blocks // 2, stage3, 0)


def local(initial, source, table, pairs, owner):
    tile_x, rows_y, cells_z = initial.shape
    servers = lax.axis_size("space")
    group = lax.axis_index("group")
    place = jnp.stack([group, group * servers + lax.axis_index("space")]).astype(jnp.int32)
    all_pairs = lax.all_gather(pairs, "group", axis=0, tiled=True)
    smem = pl.BlockSpec(memory_space=pltpu.SMEM)
    vmem = pl.BlockSpec(memory_space=pltpu.VMEM)
    send, row = pl.pallas_call(
        pack_kernel,
        out_shape=(
            jax.ShapeDtypeStruct((servers, ROWS, 8, cells_z), jnp.float32),
            jax.ShapeDtypeStruct((1,), jnp.int32),
        ),
        in_specs=[smem, smem, vmem, vmem],
        out_specs=(vmem, smem),
        scratch_shapes=[pltpu.SMEM((rows_y,), jnp.int32)],
        compiler_params=pltpu.CompilerParams(vmem_limit_bytes=32 * 2**20),
    )(owner, place, initial.reshape(-1, cells_z), source.reshape(-1, cells_z))
    received = lax.all_to_all(send, "space", split_axis=0, concat_axis=0, tiled=True)
    factor, which = layout()
    cells_x = 8 * servers
    flat = jax.ShapeDtypeStruct((cells_x, cells_z), jnp.float32)
    six = jax.ShapeDtypeStruct((6 * cells_x, cells_z), jnp.float32)
    mean, variance, first, total = pl.pallas_call(
        server_kernel,
        out_shape=(flat, flat, six, six),
        in_specs=[smem, smem, smem, vmem, vmem, vmem],
        out_specs=(vmem,) * 4,
        scratch_shapes=[
            pltpu.VMEM((UROWS, 66, 8, 128), jnp.float32),
            pltpu.VMEM((SROWS, 66, 8, 128), jnp.float32),
            pltpu.VMEM((4, 5, 66, 8, 128), jnp.float32),
            pltpu.VMEM((4, 3, 66, 8, 128), jnp.float32),
            pltpu.VMEM((10, 3, 66, 8, 128), jnp.float32),
            pltpu.VMEM((256, DEPTH), jnp.bfloat16),
            pltpu.VMEM((DEPTH, 256), jnp.bfloat16),
            pltpu.VMEM((256, 256), jnp.float32),
        ],
        compiler_params=pltpu.CompilerParams(vmem_limit_bytes=56 * 2**20),
    )(table, all_pairs, row, jnp.asarray(factor), jnp.asarray(which), received.reshape(-1, cells_z))
    return (
        mean.reshape(cells_x, 1, cells_z),
        variance.reshape(cells_x, 1, cells_z),
        first.reshape(6, cells_x, 1, cells_z),
        total.reshape(6, cells_x, 1, cells_z),
    )


def solution(mesh):
    placed = (P("space", None, None), P("space", None, None), P(), P("group", None), P())
    return jax.shard_map(
        local,
        mesh=mesh,
        in_specs=placed,
        out_specs=(
            P(None, ("group", "space"), None),
            P(None, ("group", "space"), None),
            P(None, None, ("group", "space"), None),
            P(None, None, ("group", "space"), None),
        ),
        check_vma=False,
    )
```

time: 491 us -> 135 us (0.27)
  blocking collectives: 302 us -> 10.3 us
  other arithmetic: 68.9 us -> 0.08 us
  Pallas kernels: 0 us -> 42.6 us
  local copies, waits for them, and re-layouts: 38.2 us -> 4.77 us
  starting transfers between devices: 24.8 us -> 13 us
  waiting for transfers between devices: 54.5 us -> 63.6 us
    all_to_all x2 -> x0, blocking collectives: 302 us -> none  [the longest x1 203 us: local(): lax.all_to_all(lax.all_to_all(ordered, 'group', split_axis=2, concat_axis...]
    all_to_all x0 -> x1, waiting for transfers between devices: none -> 63.6 us  [local(): lax.all_to_all(send, 'space', split_axis=0, concat_axis=0, tiled=True)]
    add x4 -> x0, other arithmetic: 59.2 us -> none  [the longest x3 59 us: advance(): inner + diffusion * laplace - 0.5 * transport - decay * inner]
    ppermute x6 -> x0, waiting for transfers between devices: 54.5 us -> none  [the longest x3 50.2 us: extended_2(): lax.ppermute(head, axis, [((i + 1) % count, i) for i in range(ends)])]
    pallas_call x0 -> x2, Pallas kernels: none -> 42.6 us  [the longest x1 36.4 us: local(): pl.pallas_call(server_kernel, out_shape=(flat, flat, six, six), in_specs=...]
    ppermute x6 -> x0, starting transfers between devices: 24.8 us -> none  [the longest x3 18.3 us: extended_2(): lax.ppermute(tail, axis, [(i, (i + 1) % count) for i in range(ends)])]
    all_to_all x0 -> x1, starting transfers between devices: none -> 13 us  [local(): lax.all_to_all(send, 'space', split_axis=0, concat_axis=0, tiled=True)]
    all_to_all x3 -> x0, local copies, waits for them, and re-layouts: 10.7 us -> none  [the longest x2 9.71 us: local(): lax.all_to_all(ordered, 'group', split_axis=2, concat_axis=0, tiled=True)]
  transfers between devices with their start and end apart: 6 -> 1, of which waited for: 6 -> 1; matrix products, arithmetic and copies ran while one was open for 2% -> 0% of each run, Pallas kernels for 0% -> 0%
where the time goes in v1:
time: 135 us
  waiting for transfers between devices  63.6 us (47%)
  Pallas kernels  42.6 us (32%)
  starting transfers between devices  13 us (10%)
  blocking collectives  10.3 us (8%)
  local copies, waits for them, and re-layouts  4.77 us (4%)
    all_to_all x1, waiting for transfers between devices, local(): lax.all_to_all(send, 'space', split_axis=0, concat_axis=0, tiled=True)  63.6 us
    pallas_call x1, Pallas kernels, local(): pl.pallas_call(server_kernel, out_shape=(flat, flat, six, six), in_specs=...  36.4 us
    all_to_all x1, starting transfers between devices, local(): lax.all_to_all(send, 'space', split_axis=0, concat_axis=0, tiled=True)  13 us
    all_gather x1, blocking collectives, local(): all_pairs = lax.all_gather(pairs, 'group', axis=0, tiled=True)  10.3 us
    pallas_call x1, Pallas kernels, local(): pl.pallas_call(pack_kernel, out_shape=(jax.ShapeDtypeStruct((servers, ROW...  6.25 us
    unnamed x10, local copies, waits for them, and re-layouts  4.77 us
  transfers between devices with their start and end apart: 1, of which 1 were waited for; matrix products, arithmetic and copies ran while one was open for 0% of the time, Pallas kernels for 0%

profile of v1, /device:TPU:6, one launch (start us, length us, event | category | flops | bytes accessed | tf_op | source)
XLA Modules:
  0.0 135.0 jit_solution(4891262523168067452)
XLA Ops:
  0.6 0.1 pad_add_fusion.place
  0.7 0.0 copy-start
  0.7 1.2 copy-done
  1.9 0.0 copy-start.1
  1.9 1.2 copy-done.1
  3.2 0.0 copy-start.2
  3.2 0.7 copy-done.2
  3.8 6.2 %shard_map.102 = (f32[64,12,8,128]{3,2,1,0:T(8,128)}, s32[1]{0:T(128)}) custom-call(s32[256]{0:T(256)S(1)} %copy-done.2, s32[2]{0:T(128)S(1)} %pad_add_fusion.place, f32[2048,128]{1,0:T(8,128)S(1)} %bitcast.19, f32[2048,128]{1,0:T(8,128)S(1)} %bitcast.20), custom_call_target="tpu_custom_call" | custom-call | tf_op jit(solution)/shard_map/pallas_call | solution.py:307
  10.1 0.0 copy-start.4
  10.1 13.0 %all-to-all-start = ((f32[64,12,8,128]{3,2,1,0:T(8,128)}), f32[64,12,8,128]{3,2,1,0:T(8,128)S(1)}, u32[]{:S(2)}, u32[]{:S(2)}) async-start(f32[64,12,8,128]{3,2,1,0:T(8,128)} %get-tuple-element.11), calls=%async_computation | async-start | bytes 6291456 | tf_op jit(solution)/shard_map/all_to_all | solution.py:318
  23.1 0.0 copy-done.4
  23.1 10.3 %all-gather = s32[4,1,2]{2,1,0:T(1,128)} all-gather(s32[1,1,2]{2,1,0:T(1,128)S(1)} %bitcast.23), channel_id=1, replica_groups=mesh['group'=4,'space'=64] {'group'}, dimensions={0}, use_global_device_ids=true | all-gather | bytes 40 | tf_op jit(solution)/shard_map/all_gather | solution.py:304
  33.4 63.6 %all-to-all-done = f32[64,12,8,128]{3,2,1,0:T(8,128)S(1)} async-done(((f32[64,12,8,128]{3,2,1,0:T(8,128)}), f32[64,12,8,128]{3,2,1,0:T(8,128)S(1)}, u32[]{:S(2)}, u32[]{:S(2)}) %all-to-all-start) | async-done | bytes 3145760 | tf_op jit(solution)/shard_map/all_to_all | solution.py:318
  97.0 0.0 copy-start.3
  97.0 1.6 %copy-done.3 = f32[64,12,8,128]{3,2,1,0:T(8,128)} copy-done((f32[64,12,8,128]{3,2,1,0:T(8,128)}, f32[64,12,8,128]{3,2,1,0:T(8,128)S(1)}, u32[]{:S(2)}) %copy-start.3) | copy-done | bytes 3145752
  98.6 36.4 %shard_map.103 = (f32[512,128]{1,0:T(8,128)}, f32[512,128]{1,0:T(8,128)}, f32[3072,128]{1,0:T(8,128)}, f32[3072,128]{1,0:T(8,128)}) custom-call(f32[8,6]{1,0:T(8,128)} %table.1, s32[4,2]{1,0:T(4,128)} %bitcast.22, s32[1]{0:T(128)} %get-tuple-element.10.row, f32[1,512]{1,0:T(1,128)} %constant.15.clone.factor, s32[3,512]{1,0:T(4,128)} %constant.16.clone.which, ...), custom_call_target="tpu_custom_call" | custom-call | tf_op jit(solution)/shard_map/pallas_call | solution.py:323
Async XLA Ops:
  0.7 1.2 copy-start
  1.9 1.2 copy-start.1
  3.2 0.7 copy-start.2
  10.1 13.0 %copy-start.4 = (s32[1,2]{1,0:T(1,128)S(1)}, s32[1,2]{1,0:T(1,128)}, u32[]{:S(2)}) copy-start(s32[1,2]{1,0:T(1,128)} %param.10) | copy-start | bytes 28
  10.1 86.8 %all-to-all-start = ((f32[64,12,8,128]{3,2,1,0:T(8,128)}), f32[64,12,8,128]{3,2,1,0:T(8,128)S(1)}, u32[]{:S(2)}, u32[]{:S(2)}) async-start(f32[64,12,8,128]{3,2,1,0:T(8,128)} %get-tuple-element.11), calls=%async_computation | async-start | bytes 6291456 | tf_op jit(solution)/shard_map/all_to_all | solution.py:318
  97.0 1.6 %copy-start.3 = (f32[64,12,8,128]{3,2,1,0:T(8,128)}, f32[64,12,8,128]{3,2,1,0:T(8,128)S(1)}, u32[]{:S(2)}) copy-start(f32[64,12,8,128]{3,2,1,0:T(8,128)S(1)} %all-to-all-done) | copy-start | bytes 9437188

commit v2 on v0

v2 whole, which is shorter than its diff:
```python
import itertools

import jax
import jax.numpy as jnp
import numpy as np
from jax import lax
from jax.experimental import pallas as pl
from jax.experimental.pallas import tpu as pltpu
from jax.sharding import PartitionSpec as P


NEAR_U, NEAR_S, FAR = 5, 3, 4
PAIRS2 = list(itertools.combinations_with_replacement(range(3), 2))
PAIRS3 = list(itertools.combinations_with_replacement(range(3), 3))
NEAR = 66
WIDE = 64
SECTION = WIDE * 8
DEPTH = 3 * SECTION + 128
COLUMNS = SECTION + 256
(ALPHA, KAPPA, HX, HZ, STRENGTH, UP, DOWN, UP2, DOWN2, U0, U0A, U1, UM1, S0, S0A, ONE) = range(16)
PAD = 8


def terms():
    word = (KAPPA, HX, HZ)

    def twice(i, j):
        return 2.0 if i != j and i > 0 else 1.0

    def thrice(i, j, k):
        return {1: 1.0, 2: 3.0, 3: 6.0}[len({i, j, k})] if i > 0 else 1.0

    out = [(1.0, U0, ONE, ONE)]
    out += [(1.0, U0A, w, ONE) for w in word]
    out += [(3.0 * twice(i, j), ALPHA, word[i], word[j]) for i, j in PAIRS2]
    out += [(thrice(i, j, k), word[i], word[j], word[k]) for i, j, k in PAIRS3]
    for whole, step in ((U1, UP), (UM1, DOWN)):
        out.append((1.0, whole, ONE, ONE))
        out += [(6.0, step, ALPHA, w) for w in word]
        out += [(3.0 * twice(i, j), step, word[i], word[j]) for i, j in PAIRS2]
    for square in (UP2, DOWN2):
        out.append((3.0, square, ALPHA, ONE))
        out += [(3.0, square, w, ONE) for w in word]
    out.append((1.0, S0, ONE, ONE))
    out += [(1.0, S0A, w, ONE) for w in word]
    out += [(twice(i, j), STRENGTH, word[i], word[j]) for i, j in PAIRS2]
    for step in (UP, DOWN):
        out.append((1.0, S0A, step, ONE))
        out += [(2.0, STRENGTH, step, w) for w in word]
    far = [(1.0, DOWN2, DOWN, ONE), (1.0, UP2, UP, ONE), (1.0, STRENGTH, DOWN2, ONE), (1.0, STRENGTH, UP2, ONE)]
    return out, far


def layout():
    near, far = terms()
    factor = np.zeros((1, COLUMNS), np.float32)
    which = np.full((3, COLUMNS), ONE, np.int32)
    for column in range(COLUMNS):
        if column < SECTION:
            term = near[column // 8]
        elif column < SECTION + 48:
            term = near[WIDE + (column - SECTION) // 8 % 2]
        elif SECTION + 128 <= column < SECTION + 224:
            term = far[(column - SECTION) // 8 % 4]
        else:
            continue
        factor[0, column] = term[0]
        which[:, column] = term[1:]
    return factor, which


def near_pack_kernel(owner, place, initial, source, send, row, padded_u, padded_s, inverse, sems):
    count = owner.shape[0]
    servers = send.shape[0]
    inner = pl.ds(PAD, count)
    copies = [
        pltpu.make_async_copy(initial, padded_u.at[:, inner, :], sems.at[0]),
        pltpu.make_async_copy(source, padded_s.at[:, inner, :], sems.at[1]),
    ]
    for copy in copies:
        copy.start()
    for ref in (padded_u, padded_s):
        for x in range(8):
            ref[x, :PAD] = jnp.zeros((PAD, 128), jnp.float32)
            ref[x, PAD + count :] = jnp.zeros((PAD, 128), jnp.float32)
    group, device = place[0], place[1]

    def invert(i, carry):
        inverse[owner[i]] = i
        return carry

    lax.fori_loop(0, count, invert, 0, unroll=8)
    row[0] = inverse[device]
    for copy in copies:
        copy.wait()
    first = lax.broadcasted_iota(jnp.int32, (8, 128), 0) < NEAR_U

    def fill(s, carry):
        p = inverse[group * servers + s] + PAD
        for x in range(8):
            rows_u = padded_u[x, pl.ds(p - NEAR_U // 2, 8), :]
            rows_s = padded_s[x, pl.ds(p - NEAR_S // 2 - NEAR_U, 8), :]
            send[s, x] = jnp.where(first, rows_u, rows_s)
        return carry

    lax.fori_loop(0, servers, fill, 0, unroll=2)


def far_pack_kernel(owner, place, initial, source, send, inverse):
    count = owner.shape[0]
    servers = send.shape[0]
    group = place[0]

    def invert(i, carry):
        inverse[owner[i]] = i
        return carry

    lax.fori_loop(0, count, invert, 0, unroll=8)

    def fill(s, carry):
        p = inverse[group * servers + s]
        for k, (array, step) in enumerate(((initial, -3), (initial, 3), (source, -2), (source, 2))):
            y = p + step
            inside = jnp.logical_and(y >= 0, y < count)
            value = array[pl.ds(jnp.clip(y, 0, count - 1), 8, stride=count), :]
            send[s, k] = jnp.where(inside, value, 0.0)
        return carry

    lax.fori_loop(0, servers, fill, 0, unroll=2)


def coefficient_kernel(rows_y, table, pairs, row, factor, which, near, far):
    p = row[0]
    run = lax.broadcasted_iota(jnp.int32, (64, 128), 0) // 8
    lane = lax.broadcasted_iota(jnp.int32, (64, 128), 1)
    same = lax.broadcasted_iota(jnp.int32, (64, 128), 0) % 8 == lane % 8

    def inside(k):
        return jnp.where(jnp.logical_and(p + k >= 0, p + k < rows_y), 1.0, 0.0)

    ways = inside(1) + inside(-1)
    ways_up = inside(2) + 1.0 + inside(-1)
    ways_down = inside(-2) + 1.0 + inside(1)
    for group in range(4):
        first, second = pairs[group, 0], pairs[group, 1]
        q = []
        for k in range(6):
            swap = jnp.logical_or(run == 1, run == 2 + k)
            q.append(jnp.where(swap, table[second, k], table[first, k]))
        kappa = 0.03 + 0.12 * q[0]
        hx, hy, hz = (-0.5 * (0.3 * q[1 + i] - 0.15) for i in range(3))
        decay = 0.02 + 0.2 * q[4]
        strength = 0.5 + 1.5 * q[5]
        alpha = 1.0 - 6.0 * kappa - decay
        up, down = kappa + hy, kappa - hy
        both = up * down
        values = [None] * ONE
        values[ALPHA], values[KAPPA], values[HX], values[HZ] = alpha, kappa, hx, hz
        values[STRENGTH], values[UP], values[DOWN] = strength, up, down
        values[UP2], values[DOWN2] = up * up, down * down
        values[U0] = alpha * (alpha * alpha + 3.0 * ways * both)
        values[U0A] = 3.0 * (alpha * alpha + ways * both)
        values[U1] = up * (3.0 * alpha * alpha + ways_up * both)
        values[UM1] = down * (3.0 * alpha * alpha + ways_down * both)
        values[S0] = strength * (alpha * alpha + alpha + 1.0 + ways * both)
        values[S0A] = strength * (2.0 * alpha + 1.0)
        rows = slice(64 * group, 64 * group + 64)
        for chunk in range(COLUMNS // 128):
            columns = slice(128 * chunk, 128 * chunk + 128)
            product = jnp.broadcast_to(factor[:, columns], (64, 128))
            for part in range(3):
                index = jnp.broadcast_to(which[part : part + 1, columns], (64, 128))
                chosen = jnp.ones((64, 128), jnp.float32)
                for number, value in enumerate(values):
                    chosen = jnp.where(index == number, value, chosen)
                product = product * chosen
            split = product.reshape(8, 8, 128)
            split = jnp.concatenate([split[:2], split[2:] - split[:1]], axis=0)
            product = jnp.where(same, split.reshape(64, 128), 0.0)
            high = product.astype(jnp.bfloat16)
            rest = product - high.astype(jnp.float32)
            if chunk < SECTION // 128:
                low = rest.astype(jnp.bfloat16)
                near[rows, columns] = high
                near[rows, SECTION + 128 * chunk : SECTION + 128 * chunk + 128] = high
                near[rows, 2 * SECTION + 128 * chunk : 2 * SECTION + 128 * chunk + 128] = low
            elif chunk == SECTION // 128:
                tail = jnp.where(lane < 32, high.astype(jnp.float32), rest)
                near[rows, 3 * SECTION :] = tail.astype(jnp.bfloat16)
            else:
                tail = jnp.where(lane < 64, high.astype(jnp.float32), rest)
                far[rows, :] = tail.astype(jnp.bfloat16)


def near_kernel(received, matrix, partial, rows, one, two, phi):
    blocks = partial.shape[0]
    size = 8 * blocks
    lane = lax.broadcasted_iota(jnp.int32, (8, 128), 1)
    zero = jnp.zeros((PAD, 128), jnp.float32)
    for ref, lead in ((rows, (8,)), (one, (3, 8)), (two, (6, 4))):
        for index in itertools.product(*(range(n) for n in lead)):
            ref[index + (slice(0, PAD),)] = zero
            ref[index + (slice(PAD + size, 2 * PAD + size),)] = zero
    phi[3 * SECTION :, :] = jnp.zeros((128, phi.shape[1]), phi.dtype)

    def at(b, step=0):
        return pl.ds(pl.multiple_of(8 * b, 8) + PAD + step, 8)

    def copy(b, carry):
        for k in range(8):
            rows[k, at(b), :] = received[pl.ds(64 * b + k, 8, stride=8), :]
        return carry

    lax.fori_loop(0, blocks, copy, 0, unroll=2)

    def parts(ref, lead, b):
        c = ref[lead + (at(b), slice(None))]
        east, west = ref[lead + (at(b, 1), slice(None))], ref[lead + (at(b, -1), slice(None))]
        up = jnp.where(lane == 127, 0.0, pltpu.roll(c, 127, 1))
        down = jnp.where(lane == 0, 0.0, pltpu.roll(c, 1, 1))
        return (east + west) + (up + down), east - west, up - down

    def stage1(b, carry):
        for k in range(8):
            for i, value in enumerate(parts(rows, (k,), b)):
                one[i, k, at(b), :] = value
        return carry

    lax.fori_loop(0, blocks, stage1, 0)
    inner = (1, 2, 3, 6)

    def stage2(b, carry):
        for n, k in enumerate(inner):
            m, x, z = (parts(one, (i, k), b) for i in range(3))
            words = (m[0], x[0] + m[1], z[0] + m[2], x[1], z[1], z[2])
            for i, value in enumerate(words):
                two[i, n, at(b), :] = value
        return carry

    lax.fori_loop(0, blocks, stage2, 0)

    def third(b):
        a = {pair: parts(two, (i, 1), b) for i, pair in enumerate(PAIRS2)}
        out = []
        for i, j, k in PAIRS3:
            if i > 0:
                value = a[(j, k)][i]
            elif j == 0 and k == 0:
                value = a[(0, 0)][0]
            elif j == 0:
                value = a[(0, k)][0] + a[(0, 0)][k]
            elif j == k:
                value = a[(j, j)][0] + a[(0, j)][j]
            else:
                value = 2.0 * a[(j, k)][0] + a[(0, k)][j] + a[(0, j)][k]
            out.append(value)
        return out

    def features(b):
        def words(k, n):
            out = [rows[k, at(b), :]] + [one[i, k, at(b), :] for i in range(3)]
            return out + [two[i, n, at(b), :] for i in range(6)] if n is not None else out

        out = words(2, 1) + third(b)
        out += words(3, 2) + words(1, 0)
        out += words(4, None) + words(0, None)
        out += words(6, 3) + words(7, None) + words(5, None)
        return out

    def stage3(pair, carry):
        for half in range(2):
            columns = slice(128 * half, 128 * half + 128)
            listed = features(2 * pair + half)
            for i in range(0, NEAR, 2):
                value = jnp.concatenate([listed[i], listed[i + 1]], axis=0)
                high = value.astype(jnp.bfloat16)
                low = (value - high.astype(jnp.float32)).astype(jnp.bfloat16)
                places = (8 * i, SECTION + 8 * i, 2 * SECTION + 8 * i)
                if i >= WIDE:
                    places = (3 * SECTION, 3 * SECTION + 16, 3 * SECTION + 32)
                for place, part in zip(places, (high, low, high)):
                    phi[place : place + 16, columns] = part
        result = jnp.dot(matrix[...], phi[...], preferred_element_type=jnp.float32)
        partial[2 * pair] = result[:, :128]
        partial[2 * pair + 1] = result[:, 128:]
        return carry

    lax.fori_loop(0, blocks // 2, stage3, 0)


def far_kernel(received, matrix, partial, mean, variance, first, total, phi, result):
    blocks = partial.shape[0]

    @pl.when(pl.program_id(0) == 0)
    def _():
        phi[96:, :] = jnp.zeros((32, phi.shape[1]), phi.dtype)

    for b in range(blocks):
        columns = slice(128 * b, 128 * b + 128)
        for i in range(0, FAR, 2):
            value = received[b, i : i + 2].reshape(16, 128)
            high = value.astype(jnp.bfloat16)
            low = (value - high.astype(jnp.float32)).astype(jnp.bfloat16)
            for place, part in zip((8 * i, 32 + 8 * i, 64 + 8 * i), (high, low, high)):
                phi[place : place + 16, columns] = part
    result[...] = jnp.dot(matrix[...], phi[...], preferred_element_type=jnp.float32)
    for b in range(blocks):
        columns = slice(128 * b, 128 * b + 128)
        out = slice(8 * b, 8 * b + 8)

        def run(number):
            rows = slice(8 * number, 8 * number + 8)
            return result[rows, columns] + partial[b, rows, :]

        def add(old, new):
            return new if old is None else old + new

        both = square = None
        firsts, totals = [None] * 6, [None] * 6
        for group in range(4):
            run_a, run_b = run(8 * group), run(8 * group + 1)
            both = add(both, run_a + run_b)
            square = add(square, run_a * run_a + run_b * run_b)
            for i in range(6):
                gap = run(8 * group + 2 + i)
                firsts[i] = add(firsts[i], run_b * gap)
                totals[i] = add(totals[i], gap * gap)
        average = both * 0.125
        mean[out, :] = average
        variance[out, :] = square * 0.125 - average * average
        for i in range(6):
            first[i, out, :] = firsts[i] * 0.25
            total[i, out, :] = totals[i] * 0.125


def shape(*dims):
    return jax.ShapeDtypeStruct(dims, jnp.float32)


def local(initial, source, table, pairs, owner):
    tile_x, rows_y, cells_z = initial.shape
    servers = lax.axis_size("space")
    group = lax.axis_index("group")
    place = jnp.stack([group, group * servers + lax.axis_index("space")]).astype(jnp.int32)
    all_pairs = lax.all_gather(pairs, "group", axis=0, tiled=True)
    smem = pl.BlockSpec(memory_space=pltpu.SMEM)
    vmem = pl.BlockSpec(memory_space=pltpu.VMEM)
    anywhere = pl.BlockSpec(memory_space=pl.ANY)
    limit = pltpu.CompilerParams(vmem_limit_bytes=32 * 2**20)
    near_send, row = pl.pallas_call(
        near_pack_kernel,
        out_shape=(shape(servers, 8, 8, cells_z), jax.ShapeDtypeStruct((1,), jnp.int32)),
        in_specs=[smem, smem, anywhere, anywhere],
        out_specs=(vmem, smem),
        scratch_shapes=[
            pltpu.VMEM((8, rows_y + 2 * PAD, cells_z), jnp.float32),
            pltpu.VMEM((8, rows_y + 2 * PAD, cells_z), jnp.float32),
            pltpu.SMEM((rows_y,), jnp.int32),
            pltpu.SemaphoreType.DMA((2,)),
        ],
        compiler_params=limit,
        name="near_pack",
    )(owner, place, initial, source)
    near_received = lax.all_to_all(near_send, "space", split_axis=0, concat_axis=0, tiled=True)
    far_send = pl.pallas_call(
        far_pack_kernel,
        out_shape=shape(servers, FAR, 8, cells_z),
        in_specs=[smem, smem, vmem, vmem],
        out_specs=vmem,
        scratch_shapes=[pltpu.SMEM((rows_y,), jnp.int32)],
        compiler_params=limit,
        name="far_pack",
    )(owner, place, initial.reshape(-1, cells_z), source.reshape(-1, cells_z))
    far_received = lax.all_to_all(far_send, "space", split_axis=0, concat_axis=0, tiled=True)
    factor, which = layout()

    def coefficients(*refs):
        coefficient_kernel(rows_y, *refs)

    near_matrix, far_matrix = pl.pallas_call(
        coefficients,
        out_shape=(
            jax.ShapeDtypeStruct((256, DEPTH), jnp.bfloat16),
            jax.ShapeDtypeStruct((256, 128), jnp.bfloat16),
        ),
        in_specs=[smem, smem, smem, vmem, vmem],
        out_specs=(vmem, vmem),
        compiler_params=limit,
        name="coefficients",
    )(table, all_pairs, row, jnp.asarray(factor), jnp.asarray(which))
    cells_x = 8 * servers
    long = cells_x + 2 * PAD
    partial = pl.pallas_call(
        near_kernel,
        out_shape=shape(servers, 256, cells_z),
        in_specs=[vmem, vmem],
        out_specs=vmem,
        scratch_shapes=[
            pltpu.VMEM((8, long, cells_z), jnp.float32),
            pltpu.VMEM((3, 8, long, cells_z), jnp.float32),
            pltpu.VMEM((6, 4, long, cells_z), jnp.float32),
            pltpu.VMEM((DEPTH, 256), jnp.bfloat16),
        ],
        compiler_params=pltpu.CompilerParams(vmem_limit_bytes=48 * 2**20),
        name="near",
    )(near_received.reshape(-1, cells_z), near_matrix)
    step = 4
    flat = pl.BlockSpec((8 * step, cells_z), lambda j: (j, 0))
    six = pl.BlockSpec((6, 8 * step, cells_z), lambda j: (0, j, 0))
    mean, variance, first, total = pl.pallas_call(
        far_kernel,
        grid=(servers // step,),
        out_shape=(shape(cells_x, cells_z), shape(cells_x, cells_z), shape(6, cells_x, cells_z), shape(6, cells_x, cells_z)),
        in_specs=[
            pl.BlockSpec((step, FAR, 8, cells_z), lambda j: (j, 0, 0, 0)),
            pl.BlockSpec((256, 128), lambda j: (0, 0)),
            pl.BlockSpec((step, 256, cells_z), lambda j: (j, 0, 0)),
        ],
        out_specs=(flat, flat, six, six),
        scratch_shapes=[
            pltpu.VMEM((128, 128 * step), jnp.bfloat16),
            pltpu.VMEM((256, 128 * step), jnp.float32),
        ],
        compiler_params=limit,
        name="far",
    )(far_received, far_matrix, partial)
    return (
        mean.reshape(cells_x, 1, cells_z),
        variance.reshape(cells_x, 1, cells_z),
        first.reshape(6, cells_x, 1, cells_z),
        total.reshape(6, cells_x, 1, cells_z),
    )


def solution(mesh):
    placed = (P("space", None, None), P("space", None, None), P(), P("group", None), P())
    return jax.shard_map(
        local,
        mesh=mesh,
        in_specs=placed,
        out_specs=(
            P(None, ("group", "space"), None),
            P(None, ("group", "space"), None),
            P(None, None, ("group", "space"), None),
            P(None, None, ("group", "space"), None),
        ),
        check_vma=False,
    )
```

time: 491 us -> 133 us (0.27)
  blocking collectives: 302 us -> 6.55 us
  other arithmetic: 68.9 us -> 0.08 us
  Pallas kernels: 0 us -> 48.2 us
  local copies, waits for them, and re-layouts: 38.2 us -> 10.1 us
  waiting for transfers between devices: 54.5 us -> 46.7 us
  starting transfers between devices: 24.8 us -> 18.8 us
    all_to_all x2 -> x0, blocking collectives: 302 us -> none  [the longest x1 203 us: local(): lax.all_to_all(lax.all_to_all(ordered, 'group', split_axis=2, concat_axis...]
    add x4 -> x0, other arithmetic: 59.2 us -> none  [the longest x3 59 us: advance(): inner + diffusion * laplace - 0.5 * transport - decay * inner]
    ppermute x6 -> x0, waiting for transfers between devices: 54.5 us -> none  [the longest x3 50.2 us: extended_2(): lax.ppermute(head, axis, [((i + 1) % count, i) for i in range(ends)])]
    pallas_call x0 -> x5, Pallas kernels: none -> 48.2 us  [the longest x1 32.1 us: local(): pl.pallas_call(near_kernel, out_shape=shape(servers, 256, cells_z), in_sp...]
    all_to_all x0 -> x2, waiting for transfers between devices: none -> 46.7 us  [the longest x1 46.7 us: local(): lax.all_to_all(near_send, 'space', split_axis=0, concat_axis=0, tiled=True)]
    ppermute x6 -> x0, starting transfers between devices: 24.8 us -> none  [the longest x3 18.3 us: extended_2(): lax.ppermute(tail, axis, [(i, (i + 1) % count) for i in range(ends)])]
    all_to_all x0 -> x2, starting transfers between devices: none -> 18.8 us  [the longest x1 13.1 us: local(): lax.all_to_all(near_send, 'space', split_axis=0, concat_axis=0, tiled=True)]
    all_to_all x3 -> x0, local copies, waits for them, and re-layouts: 10.7 us -> none  [the longest x2 9.71 us: local(): lax.all_to_all(ordered, 'group', split_axis=2, concat_axis=0, tiled=True)]
  transfers between devices with their start and end apart: 6 -> 2, of which waited for: 6 -> 1; matrix products, arithmetic and copies ran while one was open for 2% -> 0% of each run, Pallas kernels for 0% -> 29%
where the time goes in v2:
time: 133 us; the launch traced here: 131 us
  Pallas kernels  48.2 us (36%)
  waiting for transfers between devices  46.7 us (35%)
  starting transfers between devices  18.8 us (14%)
  local copies, waits for them, and re-layouts  10.1 us (8%)
  blocking collectives  6.55 us (5%)
    all_to_all x1, waiting for transfers between devices, local(): lax.all_to_all(near_send, 'space', split_axis=0, concat_axis=0, tiled=True)  46.7 us
    pallas_call x1, Pallas kernels, local(): pl.pallas_call(near_kernel, out_shape=shape(servers, 256, cells_z), in_sp...  32.1 us
    all_to_all x1, starting transfers between devices, local(): lax.all_to_all(near_send, 'space', split_axis=0, concat_axis=0, tiled=True)  13.1 us
    unnamed x26, local copies, waits for them, and re-layouts  10.1 us
    pallas_call x1, Pallas kernels, local(): pl.pallas_call(far_kernel, grid=(servers // step,), out_shape=(shape(cell...  7.81 us
    all_gather x1, blocking collectives, local(): all_pairs = lax.all_gather(pairs, 'group', axis=0, tiled=True)  6.55 us
    all_to_all x1, starting transfers between devices, local(): lax.all_to_all(far_send, 'space', split_axis=0, concat_axis=0, tiled=True)  5.67 us
    pallas_call x1, Pallas kernels, local(): pl.pallas_call(coefficients, out_shape=(jax.ShapeDtypeStruct((256, DEPTH)...  3.77 us
  transfers between devices with their start and end apart: 2, of which 1 were waited for; matrix products, arithmetic and copies ran while one was open for 0% of the time, Pallas kernels for 29%

profile of v2, /device:TPU:6, one launch (start us, length us, event | category | flops | bytes accessed | tf_op | source)
XLA Modules:
  0.0 131.1 jit_solution(3425469617374357249)
XLA Ops:
  0.6 0.1 pad_add_fusion.place
  0.7 0.0 copy-start.1
  0.7 1.2 copy-done.1
  1.9 0.0 copy-start.3
  1.9 1.2 copy-done.3
  3.2 0.0 copy-start.8
  3.2 0.7 copy-done.8
  3.8 2.1 %near_pack.1 = (f32[64,8,8,128]{3,2,1,0:T(8,128)S(1)}, s32[1]{0:T(128)}) custom-call(s32[256]{0:T(256)S(1)} %copy-done.8, s32[2]{0:T(128)S(1)} %pad_add_fusion.place, f32[8,256,128]{2,1,0:T(8,128)S(1)} %copy-done.1, f32[8,256,128]{2,1,0:T(8,128)S(1)} %copy-done.3), custom_call_target="tpu_custom_call" | custom-call | tf_op jit(solution)/shard_map/near_pack/pallas_call | solution.py:350
  6.0 0.0 copy-start.6
  6.0 1.3 %copy-done.6 = f32[64,8,8,128]{3,2,1,0:T(8,128)} copy-done((f32[64,8,8,128]{3,2,1,0:T(8,128)}, f32[64,8,8,128]{3,2,1,0:T(8,128)S(1)}, u32[]{:S(2)}) %copy-start.6) | copy-done | bytes 2097176
  7.3 0.0 copy-start.2
  7.3 0.0 copy-start.9
  7.3 13.1 %all-to-all-start.1 = ((f32[64,8,8,128]{3,2,1,0:T(8,128)}), f32[64,8,8,128]{3,2,1,0:T(8,128)S(1)}, u32[]{:S(2)}, u32[]{:S(2)}) async-start(f32[64,8,8,128]{3,2,1,0:T(8,128)} %copy-done.6), calls=%async_computation.1 | async-start | bytes 4194304 | tf_op jit(solution)/shard_map/all_to_all | solution.py:364
  20.4 0.0 copy-done.2
  20.4 0.0 copy-done.9
  20.4 0.0 copy-start.4
  20.4 1.2 copy-done.4
  21.7 2.5 %far_pack.1 = f32[64,4,8,128]{3,2,1,0:T(8,128)S(1)} custom-call(s32[256]{0:T(256)S(1)} %copy-done.9, s32[2]{0:T(128)S(1)} %pad_add_fusion.place, f32[2048,128]{1,0:T(8,128)S(1)} %bitcast.20, f32[2048,128]{1,0:T(8,128)S(1)} %bitcast.21), custom_call_target="tpu_custom_call" | custom-call | tf_op jit(solution)/shard_map/far_pack/pallas_call | solution.py:365
  24.1 0.0 copy-start.5
  24.1 1.0 copy-done.5
  25.1 46.7 %all-to-all-done.1 = f32[64,8,8,128]{3,2,1,0:T(8,128)S(1)} async-done(((f32[64,8,8,128]{3,2,1,0:T(8,128)}), f32[64,8,8,128]{3,2,1,0:T(8,128)S(1)}, u32[]{:S(2)}, u32[]{:S(2)}) %all-to-all-start.1) | async-done | bytes 2097184 | tf_op jit(solution)/shard_map/all_to_all | solution.py:364
  71.8 5.7 %all-to-all-start = ((f32[64,4,8,128]{3,2,1,0:T(8,128)}), f32[64,4,8,128]{3,2,1,0:T(8,128)S(1)}, u32[]{:S(2)}, u32[]{:S(2)}) async-start(f32[64,4,8,128]{3,2,1,0:T(8,128)} %copy-done.5), calls=%async_computation | async-start | bytes 2097152 | tf_op jit(solution)/shard_map/all_to_all | solution.py:374
  77.5 0.0 copy-done.12
  77.5 6.5 %all-gather = s32[4,1,2]{2,1,0:T(1,128)S(1)} all-gather(s32[1,1,2]{2,1,0:T(1,128)S(1)} %bitcast.23), channel_id=1, replica_groups=mesh['group'=4,'space'=64] {'group'}, dimensions={0}, use_global_device_ids=true | all-gather | bytes 40 | tf_op jit(solution)/shard_map/all_gather | solution.py:345
  84.0 0.0 copy-done.7
  84.0 0.0 copy-done.10
  84.0 0.0 copy-done.11
  84.0 3.8 %coefficients.1 = (bf16[256,1664]{1,0:T(8,128)(2,1)S(1)}, bf16[256,128]{1,0:T(8,128)(2,1)S(1)}) custom-call(f32[8,6]{1,0:T(8,128)S(1)} %copy-done.10, s32[4,2]{1,0:T(4,128)S(1)} %bitcast.22, s32[1]{0:T(128)} %get-tuple-element.12.refs_2_, f32[1,768]{1,0:T(1,128)S(1)} %copy-done.11, s32[3,768]{1,0:T(4,128)S(1)} %copy-done.7), custom_call_target="tpu_custom_call" | custom-call | tf_op jit(solution)/shard_map/coefficients/pallas_call | solution.py:380
  87.8 32.1 %near.1.partial = f32[64,256,128]{2,1,0:T(8,128)} custom-call(f32[4096,128]{1,0:T(8,128)S(1)} %bitcast.19, bf16[256,1664]{1,0:T(8,128)(2,1)S(1)} %get-tuple-element.15.matrix), custom_call_target="tpu_custom_call" | custom-call | tf_op jit(solution)/shard_map/near/pallas_call | solution.py:393
  119.9 0.0 all-to-all-done.received
  119.9 3.4 %copy-done = f32[64,256,128]{2,1,0:T(8,128)S(1)} copy-done((f32[64,256,128]{2,1,0:T(8,128)S(1)}, f32[64,256,128]{2,1,0:T(8,128)}, u32[]{:S(2)}) %copy-start) | copy-done | bytes 8388632
  123.3 7.8 %far.1 = (f32[512,128]{1,0:T(8,128)}, f32[512,128]{1,0:T(8,128)}, f32[6,512,128]{2,1,0:T(8,128)}, f32[6,512,128]{2,1,0:T(8,128)}) custom-call(f32[64,4,8,128]{3,2,1,0:T(8,128)S(1)} %all-to-all-done.received, bf16[256,128]{1,0:T(8,128)(2,1)S(1)} %get-tuple-element.13.matrix, f32[64,256,128]{2,1,0:T(8,128)S(1)} %copy-done), custom_call_target="tpu_custom_call" | custom-call | tf_op jit(solution)/shard_map/far/pallas_call | solution.py:410
  (5 shorter events, 0.0 us)
Async XLA Ops:
  0.7 1.2 copy-start.1
  1.9 1.2 copy-start.3
  3.2 0.7 copy-start.8
  6.0 1.3 %copy-start.6 = (f32[64,8,8,128]{3,2,1,0:T(8,128)}, f32[64,8,8,128]{3,2,1,0:T(8,128)S(1)}, u32[]{:S(2)}) copy-start(f32[64,8,8,128]{3,2,1,0:T(8,128)S(1)} %get-tuple-element.14) | copy-start | bytes 6291460
  7.3 13.1 %copy-start.2 = (f32[8,256,128]{2,1,0:T(8,128)S(1)}, f32[8,256,128]{2,1,0:T(8,128)}, u32[]{:S(2)}) copy-start(f32[8,256,128]{2,1,0:T(8,128)} %initial.1) | copy-start | bytes 3145732
  7.3 13.1 %copy-start.9 = (s32[256]{0:T(256)S(1)}, s32[256]{0:T(256)}, u32[]{:S(2)}) copy-start(s32[256]{0:T(256)} %owner.3) | copy-start | bytes 3076
  7.3 64.5 %all-to-all-start.1 = ((f32[64,8,8,128]{3,2,1,0:T(8,128)}), f32[64,8,8,128]{3,2,1,0:T(8,128)S(1)}, u32[]{:S(2)}, u32[]{:S(2)}) async-start(f32[64,8,8,128]{3,2,1,0:T(8,128)} %copy-done.6), calls=%async_computation.1 | async-start | bytes 4194304 | tf_op jit(solution)/shard_map/all_to_all | solution.py:364
  20.4 1.2 copy-start.4
  21.7 55.8 %copy-start.12 = (s32[1,2]{1,0:T(1,128)S(1)}, s32[1,2]{1,0:T(1,128)}, u32[]{:S(2)}) copy-start(s32[1,2]{1,0:T(1,128)} %param.10) | copy-start | bytes 28
  21.7 62.4 %copy-start.7 = (s32[3,768]{1,0:T(4,128)S(1)}, s32[3,768]{1,0:T(4,128)}, u32[]{:S(2)}) copy-start(s32[3,768]{1,0:T(4,128)} %constant.16.clone.refs_4_) | copy-start | bytes 27652
  21.7 62.4 %copy-start.10 = (f32[8,6]{1,0:T(8,128)S(1)}, f32[8,6]{1,0:T(8,128)}, u32[]{:S(2)}) copy-start(f32[8,6]{1,0:T(8,128)} %refs_0_.1) | copy-start | bytes 580
  21.7 62.4 %copy-start.11 = (f32[1,768]{1,0:T(1,128)S(1)}, f32[1,768]{1,0:T(1,128)}, u32[]{:S(2)}) copy-start(f32[1,768]{1,0:T(1,128)} %constant.15.clone.refs_3_) | copy-start | bytes 9220
  24.1 1.0 copy-start.5
  71.8 48.1 %all-to-all-start = ((f32[64,4,8,128]{3,2,1,0:T(8,128)}), f32[64,4,8,128]{3,2,1,0:T(8,128)S(1)}, u32[]{:S(2)}, u32[]{:S(2)}) async-start(f32[64,4,8,128]{3,2,1,0:T(8,128)} %copy-done.5), calls=%async_computation | async-start | bytes 2097152 | tf_op jit(solution)/shard_map/all_to_all | solution.py:374
  119.9 3.4 %copy-start = (f32[64,256,128]{2,1,0:T(8,128)S(1)}, f32[64,256,128]{2,1,0:T(8,128)}, u32[]{:S(2)}) copy-start(f32[64,256,128]{2,1,0:T(8,128)} %near.1.partial) | copy-start | bytes 25165828

commit v3 on v0

v3 whole, which is shorter than its diff:
```python
import itertools

import jax
import jax.numpy as jnp
import numpy as np
from jax import lax
from jax.experimental import pallas as pl
from jax.experimental.pallas import tpu as pltpu
from jax.sharding import Mesh, PartitionSpec as P


PAIRS2 = list(itertools.combinations_with_replacement(range(3), 2))
PAIRS3 = list(itertools.combinations_with_replacement(range(3), 3))
(ALPHA, KAPPA, HX, HZ, STRENGTH, UP, DOWN, UP2, DOWN2, U0, U0A, U1, UM1, S0, S0A, ONE) = range(16)
PAD = 8
GROUP = 4
U_WIDE, U_REST = 48, 2
S_WIDE, S_REST = 16, 4
U_DEPTH = 3 * 8 * U_WIDE + 128
S_DEPTH = 3 * 8 * S_WIDE + 128
AXES = {"yh": 2, "core": 2, "yl": 2, "z": 8, "x": 4}
SPACE = ("yl", "z", "x")
PLANE = ("yh", "core", "yl", "x")


def terms():
    word = (KAPPA, HX, HZ)

    def twice(i, j):
        return 2.0 if i != j and i > 0 else 1.0

    def thrice(i, j, k):
        return {1: 1.0, 2: 3.0, 3: 6.0}[len({i, j, k})] if i > 0 else 1.0

    u = [(1.0, U0, ONE, ONE)]
    u += [(1.0, U0A, w, ONE) for w in word]
    u += [(3.0 * twice(i, j), ALPHA, word[i], word[j]) for i, j in PAIRS2]
    u += [(thrice(i, j, k), word[i], word[j], word[k]) for i, j, k in PAIRS3]
    for whole, step in ((U1, UP), (UM1, DOWN)):
        u.append((1.0, whole, ONE, ONE))
        u += [(6.0, step, ALPHA, w) for w in word]
        u += [(3.0 * twice(i, j), step, word[i], word[j]) for i, j in PAIRS2]
    for square in (UP2, DOWN2):
        u.append((3.0, square, ALPHA, ONE))
        u += [(3.0, square, w, ONE) for w in word]
    u += [(1.0, UP2, UP, ONE), (1.0, DOWN2, DOWN, ONE)]
    s = [(1.0, S0, ONE, ONE)]
    s += [(1.0, S0A, w, ONE) for w in word]
    s += [(twice(i, j), STRENGTH, word[i], word[j]) for i, j in PAIRS2]
    for step in (UP, DOWN):
        s.append((1.0, S0A, step, ONE))
        s += [(2.0, STRENGTH, step, w) for w in word]
    s += [(1.0, STRENGTH, UP2, ONE), (1.0, STRENGTH, DOWN2, ONE)]
    return u, s


def layout():
    chosen = []
    for listed, wide, rest in zip(terms(), (U_WIDE, S_WIDE), (U_REST, S_REST)):
        chosen += [listed[c // 8] for c in range(8 * wide)]
        chosen += [listed[wide + c // 8 % rest] for c in range(24 * rest)]
        chosen += [(0.0, ONE, ONE, ONE)] * (128 - 24 * rest)
    factor = np.array([[term[0] for term in chosen]], np.float32)
    which = np.array([term[1:] for term in chosen], np.int32).T
    return factor, np.ascontiguousarray(which)


def pack_kernel(halo, owner, place, *refs):
    tiles, (send, row, padded, inverse, sems) = refs[:-5], refs[-5:]
    rows = 2 * halo + 1
    count = owner.shape[0]
    z, device = place[0], place[1]
    inner = pl.ds(PAD, count)
    slots = [(0, 2), (2, 2), (4, 2), (6, 2), (14, 2), (12, 2), (10, 2), (8, 1), (9, 1)]
    copies = []
    for n, (tile, (slot, many)) in enumerate(zip(tiles, slots)):
        copies.append(pltpu.make_async_copy(tile, padded.at[pl.ds(slot, many), inner, :], sems.at[n]))
    for copy in copies:
        copy.start()
    for i in range(16):
        padded[i, :PAD] = jnp.zeros((PAD, 128), jnp.float32)
        padded[i, PAD + count :] = jnp.zeros((PAD, 128), jnp.float32)

    def invert(i, carry):
        inverse[owner[i]] = i
        return carry

    lax.fori_loop(0, count, invert, 0, unroll=8)
    row[0] = inverse[device]
    for copy in copies:
        copy.wait()

    def fill(j, carry):
        target = (j // 8) * 64 + (j // 4 % 2) * 32 + z * 4 + j % 4
        start = inverse[target] + PAD - halo
        for i in range(16):
            send[j, rows * i : rows * i + rows, :] = padded[i, pl.ds(start, rows), :]
        return carry

    lax.fori_loop(0, send.shape[0], fill, 0, unroll=2)


def coefficient_kernel(rows_y, table, pairs, row, factor, which, u_matrix, s_matrix):
    p = row[0]
    run = lax.broadcasted_iota(jnp.int32, (64, 128), 0) // 8
    lane = lax.broadcasted_iota(jnp.int32, (64, 128), 1)
    same = lax.broadcasted_iota(jnp.int32, (64, 128), 0) % 8 == lane % 8

    def inside(k):
        return jnp.where(jnp.logical_and(p + k >= 0, p + k < rows_y), 1.0, 0.0)

    ways = inside(1) + inside(-1)
    ways_up = inside(2) + 1.0 + inside(-1)
    ways_down = inside(-2) + 1.0 + inside(1)
    for group in range(4):
        first, second = pairs[group, 0], pairs[group, 1]
        q = []
        for k in range(6):
            swap = jnp.logical_or(run == 1, run == 2 + k)
            q.append(jnp.where(swap, table[second, k], table[first, k]))
        kappa = 0.03 + 0.12 * q[0]
        hx, hy, hz = (-0.5 * (0.3 * q[1 + i] - 0.15) for i in range(3))
        decay = 0.02 + 0.2 * q[4]
        strength = 0.5 + 1.5 * q[5]
        alpha = 1.0 - 6.0 * kappa - decay
        up, down = kappa + hy, kappa - hy
        both = up * down
        values = [None] * ONE
        values[ALPHA], values[KAPPA], values[HX], values[HZ] = alpha, kappa, hx, hz
        values[STRENGTH], values[UP], values[DOWN] = strength, up, down
        values[UP2], values[DOWN2] = up * up, down * down
        values[U0] = alpha * (alpha * alpha + 3.0 * ways * both)
        values[U0A] = 3.0 * (alpha * alpha + ways * both)
        values[U1] = up * (3.0 * alpha * alpha + ways_up * both)
        values[UM1] = down * (3.0 * alpha * alpha + ways_down * both)
        values[S0] = strength * (alpha * alpha + alpha + 1.0 + ways * both)
        values[S0A] = strength * (2.0 * alpha + 1.0)
        rows = slice(64 * group, 64 * group + 64)
        chunk = 0
        for matrix, wide, rest in ((u_matrix, U_WIDE, U_REST), (s_matrix, S_WIDE, S_REST)):
            for at in range(0, 8 * wide + 128, 128):
                columns = slice(128 * chunk, 128 * chunk + 128)
                chunk += 1
                product = jnp.broadcast_to(factor[:, columns], (64, 128))
                for part in range(3):
                    index = jnp.broadcast_to(which[part : part + 1, columns], (64, 128))
                    chosen = jnp.ones((64, 128), jnp.float32)
                    for number, value in enumerate(values):
                        chosen = jnp.where(index == number, value, chosen)
                    product = product * chosen
                split = product.reshape(8, 8, 128)
                split = jnp.concatenate([split[:2], split[2:] - split[:1]], axis=0)
                product = jnp.where(same, split.reshape(64, 128), 0.0)
                high = product.astype(jnp.bfloat16)
                low = product - high.astype(jnp.float32)
                if at < 8 * wide:
                    matrix[rows, at : at + 128] = high
                    matrix[rows, 8 * wide + at : 8 * wide + at + 128] = high
                    matrix[rows, 16 * wide + at : 16 * wide + at + 128] = low.astype(jnp.bfloat16)
                else:
                    tail = jnp.where(lane < 16 * rest, high.astype(jnp.float32), low)
                    matrix[rows, 24 * wide :] = tail.astype(jnp.bfloat16)


def at(b, step=0):
    return pl.ds(pl.multiple_of(8 * b, 8) + PAD + step, 8)


def unpack(received, rows, z, blocks):
    many = rows.shape[0]
    device = 16 * many

    def copy(t, carry):
        r = (t // 4 % 8 - z + 8) % 8
        start = (t // 32 * 4 + t % 4) * device + 2 * many * r
        for x in range(2):
            for k in range(many):
                value = received[pl.ds(start + many * x + k, 4, stride=8 * device), :]
                rows.at[k][pl.ds(8 * t + PAD + x, 4, stride=2), :] = value
        return carry

    lax.fori_loop(0, blocks, copy, 0, unroll=2)


def clear_ends(size, *refs):
    zero = jnp.zeros((PAD, 128), jnp.float32)
    for ref in refs:
        for index in itertools.product(*(range(n) for n in ref.shape[:-2])):
            ref[index + (slice(0, PAD),)] = zero
            ref[index + (slice(PAD + size, 2 * PAD + size),)] = zero


def parts(ref, lead, b):
    lane = lax.broadcasted_iota(jnp.int32, (8, 128), 1)
    c = ref[lead + (at(b), slice(None))]
    east, west = ref[lead + (at(b, 1), slice(None))], ref[lead + (at(b, -1), slice(None))]
    up = jnp.where(lane == 127, 0.0, pltpu.roll(c, 127, 1))
    down = jnp.where(lane == 0, 0.0, pltpu.roll(c, 1, 1))
    return (east + west) + (up + down), east - west, up - down


def first_words(rows, one, skip, blocks):
    def body(b, carry):
        for n in range(one.shape[1]):
            for i, value in enumerate(parts(rows, (n + skip,), b)):
                one[i, n, at(b), :] = value
        return carry

    lax.fori_loop(0, blocks, body, 0)


def second_words(one, lead, b):
    m, x, z = (parts(one, (i, lead), b) for i in range(3))
    return [m[0], x[0] + m[1], z[0] + m[2], x[1], z[1], z[2]]


def third_words(two, lead, b):
    a = {pair: parts(two, (i, lead), b) for i, pair in enumerate(PAIRS2)}
    out = []
    for i, j, k in PAIRS3:
        if i > 0:
            value = a[(j, k)][i]
        elif j == 0 and k == 0:
            value = a[(0, 0)][0]
        elif j == 0:
            value = a[(0, k)][0] + a[(0, 0)][k]
        elif j == k:
            value = a[(j, j)][0] + a[(0, j)][j]
        else:
            value = 2.0 * a[(j, k)][0] + a[(0, k)][j] + a[(0, j)][k]
        out.append(value)
    return out


def store_features(phi, listed, wide, columns):
    rest = len(listed) - wide
    for i in range(0, len(listed), 2):
        value = jnp.concatenate([listed[i], listed[i + 1]], axis=0)
        high = value.astype(jnp.bfloat16)
        low = (value - high.astype(jnp.float32)).astype(jnp.bfloat16)
        base, size, here = (0, 8 * wide, i) if i < wide else (24 * wide, 8 * rest, i - wide)
        for n, part in enumerate((high, low, high)):
            place = base + size * n + 8 * here
            phi[place : place + 16, columns] = part


def u_kernel(place, received, matrix, partial, rows, one, two, phi):
    blocks = partial.shape[0]
    clear_ends(8 * blocks, rows, one, two)
    phi[24 * U_WIDE :, :] = jnp.zeros((128, phi.shape[1]), phi.dtype)
    unpack(received, rows, place[0], blocks)
    first_words(rows, one, 1, blocks)

    def second(b, carry):
        for n in range(3):
            for i, value in enumerate(second_words(one, n + 1, b)):
                two[i, n, at(b), :] = value
        return carry

    lax.fori_loop(0, blocks, second, 0)

    def words(k, b):
        out = [rows[k, at(b), :]]
        if 1 <= k <= 5:
            out += [one[i, k - 1, at(b), :] for i in range(3)]
        if 2 <= k <= 4:
            out += [two[i, k - 2, at(b), :] for i in range(6)]
        return out

    def last(group, carry):
        for n in range(GROUP):
            b = GROUP * group + n
            listed = words(3, b) + third_words(two, 1, b)
            for k in (4, 2, 5, 1, 6, 0):
                listed += words(k, b)
            store_features(phi, listed, U_WIDE, slice(128 * n, 128 * n + 128))
        result = jnp.dot(matrix[...], phi[...], preferred_element_type=jnp.float32)
        for n in range(GROUP):
            partial[GROUP * group + n] = result[:, 128 * n : 128 * n + 128]
        return carry

    lax.fori_loop(0, blocks // GROUP, last, 0)


def s_kernel(place, received, matrix, partial, mean, variance, first, total,
             rows, one, phi, result, mean_out, variance_out, first_out, total_out, sems):
    blocks = partial.shape[0]
    clear_ends(8 * blocks, rows, one)
    phi[24 * S_WIDE :, :] = jnp.zeros((128, phi.shape[1]), phi.dtype)
    unpack(received, rows, place[0], blocks)
    first_words(rows, one, 1, blocks)

    def add(old, new):
        return new if old is None else old + new

    def last(group, carry):
        for n in range(GROUP):
            b = GROUP * group + n

            def words(k):
                return [rows[k, at(b), :]] + [one[i, k - 1, at(b), :] for i in range(3)]

            listed = words(2) + second_words(one, 1, b) + words(3) + words(1)
            listed += [rows[4, at(b), :], rows[0, at(b), :]]
            store_features(phi, listed, S_WIDE, slice(128 * n, 128 * n + 128))
        result[...] = jnp.dot(matrix[...], phi[...], preferred_element_type=jnp.float32)
        for n in range(GROUP):
            b = GROUP * group + n
            columns = slice(128 * n, 128 * n + 128)
            out = pl.ds(pl.multiple_of(8 * b, 8), 8)

            def run(number):
                here = slice(8 * number, 8 * number + 8)
                return result[here, columns] + partial[b, here, :]

            both = square = None
            firsts, totals = [None] * 6, [None] * 6
            for g in range(4):
                run_a, run_b = run(8 * g), run(8 * g + 1)
                both = add(both, run_a + run_b)
                square = add(square, run_a * run_a + run_b * run_b)
                for i in range(6):
                    gap = run(8 * g + 2 + i)
                    firsts[i] = add(firsts[i], run_b * gap)
                    totals[i] = add(totals[i], gap * gap)
            average = both * 0.125
            mean_out[out, :] = average
            variance_out[out, :] = square * 0.125 - average * average
            for i in range(6):
                first_out[i, out, :] = firsts[i] * 0.25
                total_out[i, out, :] = totals[i] * 0.125
        return carry

    copies = []
    quarter = blocks // GROUP // 4
    for n in range(4):
        lax.fori_loop(n * quarter, n * quarter + quarter, last, 0)
        x = pl.ds(n * 2 * blocks, 2 * blocks)
        for k, (here, there) in enumerate(((mean_out, mean), (variance_out, variance))):
            copies.append(pltpu.make_async_copy(here.at[x, :], there.at[x, :], sems.at[4 * n + k]))
            copies[-1].start()
        for k, (here, there) in enumerate(((first_out, first), (total_out, total))):
            copies.append(pltpu.make_async_copy(here.at[:, x, :], there.at[:, x, :], sems.at[4 * n + 2 + k]))
            copies[-1].start()
    for copy in copies:
        copy.wait()


def shape(*dims):
    return jax.ShapeDtypeStruct(dims, jnp.float32)


def limit(mib):
    return pltpu.CompilerParams(vmem_limit_bytes=mib * 2**20)


def ring(tile):
    count = lax.axis_size("z")
    to_next = [(i, (i + 1) % count) for i in range(count)]
    to_last = [(i, (i - 1) % count) for i in range(count)]
    below, above = [tile], [tile]
    for _ in range(3):
        below.append(lax.ppermute(below[-1], "z", to_next))
        above.append(lax.ppermute(above[-1], "z", to_last))
    ends = [lax.ppermute(below[-1][:1], "z", to_next), lax.ppermute(above[-1][1:], "z", to_last)]
    return [tile] + above[1:] + below[1:] + ends


def local(initial, source, table, pairs, owner):
    tile_x, rows_y, cells_z = initial.shape
    servers = 64
    quarter = lax.axis_index(("yh", "core"))
    place = jnp.stack([lax.axis_index("z"), quarter * servers + lax.axis_index(SPACE)]).astype(jnp.int32)
    all_pairs = lax.all_gather(pairs, ("yh", "core"), axis=0, tiled=True)
    smem = pl.BlockSpec(memory_space=pltpu.SMEM)
    vmem = pl.BlockSpec(memory_space=pltpu.VMEM)
    anywhere = pl.BlockSpec(memory_space=pl.ANY)

    def deliver(array, halo, name):
        rows = 2 * halo + 1
        tiles = ring(lax.dynamic_slice_in_dim(array, 2 * quarter, 2, axis=0))
        send, row = pl.pallas_call(
            lambda *refs: pack_kernel(halo, *refs),
            out_shape=(shape(32, 16 * rows, cells_z), jax.ShapeDtypeStruct((1,), jnp.int32)),
            in_specs=[smem, smem] + [anywhere] * 9,
            out_specs=(vmem, smem),
            scratch_shapes=[
                pltpu.VMEM((16, rows_y + 2 * PAD, cells_z), jnp.float32),
                pltpu.SMEM((rows_y,), jnp.int32),
                pltpu.SemaphoreType.DMA((9,)),
            ],
            compiler_params=limit(8),
            name=name,
        )(owner, place, *tiles)
        received = lax.all_to_all(send, PLANE, split_axis=0, concat_axis=0, tiled=True)
        return received.reshape(-1, cells_z), row

    u_received, row = deliver(initial, 3, "u_pack")
    s_received, _ = deliver(source, 2, "s_pack")
    factor, which = layout()
    u_matrix, s_matrix = pl.pallas_call(
        lambda *refs: coefficient_kernel(rows_y, *refs),
        out_shape=(
            jax.ShapeDtypeStruct((256, U_DEPTH), jnp.bfloat16),
            jax.ShapeDtypeStruct((256, S_DEPTH), jnp.bfloat16),
        ),
        in_specs=[smem, smem, smem, vmem, vmem],
        out_specs=(vmem, vmem),
        compiler_params=limit(8),
        name="coefficients",
    )(table, all_pairs, row, jnp.asarray(factor), jnp.asarray(which))
    cells_x = tile_x * servers
    long = cells_x + 2 * PAD
    partial = pl.pallas_call(
        u_kernel,
        out_shape=shape(servers, 256, cells_z),
        in_specs=[smem, vmem, vmem],
        out_specs=vmem,
        scratch_shapes=[
            pltpu.VMEM((7, long, cells_z), jnp.float32),
            pltpu.VMEM((3, 5, long, cells_z), jnp.float32),
            pltpu.VMEM((6, 3, long, cells_z), jnp.float32),
            pltpu.VMEM((U_DEPTH, 128 * GROUP), jnp.bfloat16),
        ],
        compiler_params=limit(20),
        name="u_words",
    )(place, u_received, u_matrix)
    flat, six = shape(cells_x, cells_z), shape(6, cells_x, cells_z)
    mean, variance, first, total = pl.pallas_call(
        s_kernel,
        out_shape=(flat, flat, six, six),
        in_specs=[smem, vmem, vmem, vmem],
        out_specs=(anywhere,) * 4,
        scratch_shapes=[
            pltpu.VMEM((5, long, cells_z), jnp.float32),
            pltpu.VMEM((3, 3, long, cells_z), jnp.float32),
            pltpu.VMEM((S_DEPTH, 128 * GROUP), jnp.bfloat16),
            pltpu.VMEM((256, 128 * GROUP), jnp.float32),
            pltpu.VMEM(flat.shape, jnp.float32),
            pltpu.VMEM(flat.shape, jnp.float32),
            pltpu.VMEM(six.shape, jnp.float32),
            pltpu.VMEM(six.shape, jnp.float32),
            pltpu.SemaphoreType.DMA((16,)),
        ],
        compiler_params=limit(16),
        name="s_words",
    )(place, s_received, s_matrix, partial)
    return (
        mean.reshape(cells_x, 1, cells_z),
        variance.reshape(cells_x, 1, cells_z),
        first.reshape(6, cells_x, 1, cells_z),
        total.reshape(6, cells_x, 1, cells_z),
    )


def solution(mesh):
    axes = Mesh(mesh.devices.reshape(tuple(AXES.values())), tuple(AXES))
    group = ("yh", "core")
    placed = (P(SPACE, None, None), P(SPACE, None, None), P(), P(group, None), P())
    return jax.shard_map(
        local,
        mesh=axes,
        in_specs=placed,
        out_specs=(
            P(None, group + SPACE, None),
            P(None, group + SPACE, None),
            P(None, None, group + SPACE, None),
            P(None, None, group + SPACE, None),
        ),
        check_vma=False,
    )
```

time: 491 us -> 166 us (0.34)
  blocking collectives: 302 us -> 18.7 us
  other arithmetic: 68.9 us -> 0.07 us
  Pallas kernels: 0 us -> 49.4 us
  local copies, waits for them, and re-layouts: 38.2 us -> 11.9 us
  starting transfers between devices: 24.8 us -> 44.6 us
  waiting for transfers between devices: 54.5 us -> 39.1 us
    all_to_all x2 -> x0, blocking collectives: 302 us -> none  [the longest x1 203 us: local(): lax.all_to_all(lax.all_to_all(ordered, 'group', split_axis=2, concat_axis...]
    add x4 -> x0, other arithmetic: 59.2 us -> none  [the longest x3 59 us: advance(): inner + diffusion * laplace - 0.5 * transport - decay * inner]
    pallas_call x0 -> x5, Pallas kernels: none -> 49.4 us  [the longest x1 24 us: local(): pl.pallas_call(u_kernel, out_shape=shape(servers, 256, cells_z), in_specs...]
    all_gather x0 -> x1, blocking collectives: none -> 18.7 us  [local(): all_pairs = lax.all_gather(pairs, ('yh', 'core'), axis=0, tiled=True)]
    ppermute x6 -> x16, waiting for transfers between devices: 54.5 us -> 39.1 us  [the longest x6 33.5 us: ring(): below.append(lax.ppermute(below[-1], 'z', to_next))]
    all_to_all x0 -> x2, starting transfers between devices: none -> 15.2 us  [deliver(): lax.all_to_all(send, PLANE, split_axis=0, concat_axis=0, tiled=True)]
    all_to_all x3 -> x0, local copies, waits for them, and re-layouts: 10.7 us -> none  [the longest x2 9.71 us: local(): lax.all_to_all(ordered, 'group', split_axis=2, concat_axis=0, tiled=True)]
    gather x1 -> x0, local copies, waits for them, and re-layouts: 8.22 us -> none  [local(): jnp.take(blocks, inverse, axis=2).reshape(count, tile_x, rows_y, cells_z)]
  transfers between devices with their start and end apart: 6 -> 18, of which waited for: 6 -> 8; matrix products, arithmetic and copies ran while one was open for 2% -> 1% of each run, Pallas kernels for 0% -> 19%
where the time goes in v3:
time: 166 us; the launch traced here: 165 us
  Pallas kernels  49.4 us (30%)
  starting transfers between devices  44.6 us (27%)
  waiting for transfers between devices  39.1 us (24%)
  blocking collectives  18.7 us (11%)
  local copies, waits for them, and re-layouts  11.9 us (7%)
    ppermute x6, waiting for transfers between devices, ring(): below.append(lax.ppermute(below[-1], 'z', to_next))  33.5 us
    pallas_call x1, Pallas kernels, local(): pl.pallas_call(u_kernel, out_shape=shape(servers, 256, cells_z), in_specs...  24 us
    ppermute x6, starting transfers between devices, ring(): above.append(lax.ppermute(above[-1], 'z', to_last))  20.4 us
    all_gather x1, blocking collectives, local(): all_pairs = lax.all_gather(pairs, ('yh', 'core'), axis=0, tiled=True)  18.7 us
    pallas_call x1, Pallas kernels, local(): pl.pallas_call(s_kernel, out_shape=(flat, flat, six, six), in_specs=[smem...  16.1 us
    all_to_all x2, starting transfers between devices, deliver(): lax.all_to_all(send, PLANE, split_axis=0, concat_axis=0, tiled=True)  15.2 us
    unnamed x20, local copies, waits for them, and re-layouts  10.9 us
    ppermute x2, starting transfers between devices, ring(): lax.ppermute(above[-1][1:], 'z', to_last)  6.57 us
  transfers between devices with their start and end apart: 18, of which 8 were waited for; matrix products, arithmetic and copies ran while one was open for 1% of the time, Pallas kernels for 19%

profile of v3, /device:TPU:6, one launch (start us, length us, event | category | flops | bytes accessed | tf_op | source)
XLA Modules:
  0.0 164.7 jit_solution(4331252692673794750)
XLA Ops:
  0.7 1.2 copy-done
  1.9 2.0 %collective-permute-start.11 = (f32[2,256,128]{2,1,0:T(8,128)S(1)}, f32[2,256,128]{2,1,0:T(8,128)S(1)}, u32[]{:S(2)}, u32[]{:S(2)}) collective-permute-start(f32[2,256,128]{2,1,0:T(8,128)S(1)} %constant_dynamic-slice_fusion.refs_2_), channel_id=1, source_target_pairs={{0,4},{4,8},{8,12},{12,16},{16,20},{20,24},{24,28},{28,0},{1,5},{5... | collective-permute-start | bytes 786440 | tf_op jit(solution)/shard_map/ppermute | solution.py:363
  3.9 4.0 %collective-permute-start.8 = (f32[2,256,128]{2,1,0:T(8,128)S(1)}, f32[2,256,128]{2,1,0:T(8,128)S(1)}, u32[]{:S(2)}, u32[]{:S(2)}) collective-permute-start(f32[2,256,128]{2,1,0:T(8,128)S(1)} %constant_dynamic-slice_fusion.refs_2_), channel_id=1, source_target_pairs={{0,28},{4,0},{8,4},{12,8},{16,12},{20,16},{24,20},{28,24},{1,29},{... | collective-permute-start | bytes 786440 | tf_op jit(solution)/shard_map/ppermute | solution.py:364
  7.9 6.2 %collective-permute-done.11.refs_6_ = f32[2,256,128]{2,1,0:T(8,128)S(1)} collective-permute-done((f32[2,256,128]{2,1,0:T(8,128)S(1)}, f32[2,256,128]{2,1,0:T(8,128)S(1)}, u32[]{:S(2)}, u32[]{:S(2)}) %collective-permute-start.11) | collective-permute-done | bytes 262176 | tf_op jit(solution)/shard_map/ppermute | solution.py:363
  14.1 3.2 %collective-permute-start.9 = (f32[2,256,128]{2,1,0:T(8,128)S(1)}, f32[2,256,128]{2,1,0:T(8,128)S(1)}, u32[]{:S(2)}, u32[]{:S(2)}) collective-permute-start(f32[2,256,128]{2,1,0:T(8,128)S(1)} %collective-permute-done.8.refs_3_), channel_id=1, source_target_pairs={{0,28},{4,0},{8,4},{12,8},{16,12},{20,16},{24,20},{28,24},{1,29},{... | collective-permute-start | bytes 786440 | tf_op jit(solution)/shard_map/ppermute | solution.py:364
  17.4 5.5 %collective-permute-done.12.refs_7_ = f32[2,256,128]{2,1,0:T(8,128)S(1)} collective-permute-done((f32[2,256,128]{2,1,0:T(8,128)S(1)}, f32[2,256,128]{2,1,0:T(8,128)S(1)}, u32[]{:S(2)}, u32[]{:S(2)}) %collective-permute-start.12) | collective-permute-done | bytes 262176 | tf_op jit(solution)/shard_map/ppermute | solution.py:363
  22.8 3.2 %collective-permute-start.10 = (f32[2,256,128]{2,1,0:T(8,128)S(1)}, f32[2,256,128]{2,1,0:T(8,128)S(1)}, u32[]{:S(2)}, u32[]{:S(2)}) collective-permute-start(f32[2,256,128]{2,1,0:T(8,128)S(1)} %collective-permute-done.9.refs_4_), channel_id=1, source_target_pairs={{0,28},{4,0},{8,4},{12,8},{16,12},{20,16},{24,20},{28,24},{1,29},{... | collective-permute-start | bytes 786440 | tf_op jit(solution)/shard_map/ppermute | solution.py:364
  26.1 4.5 %collective-permute-done.13.refs_8_ = f32[2,256,128]{2,1,0:T(8,128)S(1)} collective-permute-done((f32[2,256,128]{2,1,0:T(8,128)S(1)}, f32[2,256,128]{2,1,0:T(8,128)S(1)}, u32[]{:S(2)}, u32[]{:S(2)}) %collective-permute-start.13) | collective-permute-done | bytes 262176 | tf_op jit(solution)/shard_map/ppermute | solution.py:363
  30.7 3.3 %collective-permute-start.15 = (f32[1,256,128]{2,1,0:T(8,128)S(1)}, f32[1,256,128]{2,1,0:T(8,128)S(1)}, u32[]{:S(2)}, u32[]{:S(2)}) collective-permute-start(f32[1,256,128]{2,1,0:T(8,128)S(1)} %slice.19), channel_id=1, source_target_pairs={{0,28},{4,0},{8,4},{12,8},{16,12},{20,16},{24,20},{28,24},{1,29},{... | collective-permute-start | bytes 393224 | tf_op jit(solution)/shard_map/ppermute | solution.py:365
  34.1 2.8 %collective-permute-done.14.refs_9_ = f32[1,256,128]{2,1,0:T(8,128)S(1)} collective-permute-done((f32[1,256,128]{2,1,0:T(8,128)S(1)}, f32[1,256,128]{2,1,0:T(8,128)S(1)}, u32[]{:S(2)}, u32[]{:S(2)}) %collective-permute-start.14) | collective-permute-done | bytes 131104 | tf_op jit(solution)/shard_map/ppermute | solution.py:365
  36.9 0.7 copy-done.6
  37.6 2.7 %u_pack.1 = (f32[32,112,128]{2,1,0:T(8,128)S(1)}, s32[1]{0:T(128)}) custom-call(s32[256]{0:T(256)S(1)} %copy-done.6, s32[2]{0:T(128)S(1)} %pad_add_fusion.refs_1_.place, f32[2,256,128]{2,1,0:T(8,128)S(1)} %constant_dynamic-slice_fusion.refs_2_, f32[2,256,128]{2,1,0:T(8,128)S(1)} %collective-permute-done.8.refs_3_, ...), custom_call_target="tpu_custom_call" | custom-call | tf_op jit(solution)/shard_map/u_pack/pallas_call | solution.py:382
  40.3 1.3 copy-done.3
  41.6 7.6 %all-to-all-start.1 = ((f32[32,112,128]{2,1,0:T(8,128)}), f32[32,112,128]{2,1,0:T(8,128)S(1)}, u32[]{:S(2)}, u32[]{:S(2)}) async-start(f32[32,112,128]{2,1,0:T(8,128)} %copy-done.3), calls=%async_computation.1 | async-start | bytes 3670016 | tf_op jit(solution)/shard_map/all_to_all | solution.py:395
  49.1 1.0 constant_dynamic-slice_fusion.1.refs_2_
  50.2 3.4 %collective-permute-start = (f32[2,256,128]{2,1,0:T(8,128)S(1)}, f32[2,256,128]{2,1,0:T(8,128)S(1)}, u32[]{:S(2)}, u32[]{:S(2)}) collective-permute-start(f32[2,256,128]{2,1,0:T(8,128)S(1)} %constant_dynamic-slice_fusion.1.refs_2_), channel_id=1, source_target_pairs={{0,28},{4,0},{8,4},{12,8},{16,12},{20,16},{24,20},{28,24},{1,29},{... | collective-permute-start | bytes 786440 | tf_op jit(solution)/shard_map/ppermute | solution.py:364
  53.6 6.5 %collective-permute-done.3.refs_6_ = f32[2,256,128]{2,1,0:T(8,128)S(1)} collective-permute-done((f32[2,256,128]{2,1,0:T(8,128)S(1)}, f32[2,256,128]{2,1,0:T(8,128)S(1)}, u32[]{:S(2)}, u32[]{:S(2)}) %collective-permute-start.3) | collective-permute-done | bytes 262176 | tf_op jit(solution)/shard_map/ppermute | solution.py:363
  60.1 3.2 %collective-permute-start.1 = (f32[2,256,128]{2,1,0:T(8,128)S(1)}, f32[2,256,128]{2,1,0:T(8,128)S(1)}, u32[]{:S(2)}, u32[]{:S(2)}) collective-permute-start(f32[2,256,128]{2,1,0:T(8,128)S(1)} %collective-permute-done.refs_3_), channel_id=1, source_target_pairs={{0,28},{4,0},{8,4},{12,8},{16,12},{20,16},{24,20},{28,24},{1,29},{... | collective-permute-start | bytes 786440 | tf_op jit(solution)/shard_map/ppermute | solution.py:364
  63.4 5.8 %collective-permute-done.4.refs_7_ = f32[2,256,128]{2,1,0:T(8,128)S(1)} collective-permute-done((f32[2,256,128]{2,1,0:T(8,128)S(1)}, f32[2,256,128]{2,1,0:T(8,128)S(1)}, u32[]{:S(2)}, u32[]{:S(2)}) %collective-permute-start.4) | collective-permute-done | bytes 262176 | tf_op jit(solution)/shard_map/ppermute | solution.py:363
  69.2 3.2 %collective-permute-start.2 = (f32[2,256,128]{2,1,0:T(8,128)S(1)}, f32[2,256,128]{2,1,0:T(8,128)S(1)}, u32[]{:S(2)}, u32[]{:S(2)}) collective-permute-start(f32[2,256,128]{2,1,0:T(8,128)S(1)} %collective-permute-done.1.refs_4_), channel_id=1, source_target_pairs={{0,28},{4,0},{8,4},{12,8},{16,12},{20,16},{24,20},{28,24},{1,29},{... | collective-permute-start | bytes 786440 | tf_op jit(solution)/shard_map/ppermute | solution.py:364
  72.4 4.9 %collective-permute-done.5.refs_8_ = f32[2,256,128]{2,1,0:T(8,128)S(1)} collective-permute-done((f32[2,256,128]{2,1,0:T(8,128)S(1)}, f32[2,256,128]{2,1,0:T(8,128)S(1)}, u32[]{:S(2)}, u32[]{:S(2)}) %collective-permute-start.5) | collective-permute-done | bytes 262176 | tf_op jit(solution)/shard_map/ppermute | solution.py:363
  77.7 3.3 %collective-permute-start.7 = (f32[1,256,128]{2,1,0:T(8,128)S(1)}, f32[1,256,128]{2,1,0:T(8,128)S(1)}, u32[]{:S(2)}, u32[]{:S(2)}) collective-permute-start(f32[1,256,128]{2,1,0:T(8,128)S(1)} %slice.17), channel_id=1, source_target_pairs={{0,28},{4,0},{8,4},{12,8},{16,12},{20,16},{24,20},{28,24},{1,29},{... | collective-permute-start | bytes 393224 | tf_op jit(solution)/shard_map/ppermute | solution.py:365
  81.0 2.8 %collective-permute-done.6.refs_9_ = f32[1,256,128]{2,1,0:T(8,128)S(1)} collective-permute-done((f32[1,256,128]{2,1,0:T(8,128)S(1)}, f32[1,256,128]{2,1,0:T(8,128)S(1)}, u32[]{:S(2)}, u32[]{:S(2)}) %collective-permute-start.6) | collective-permute-done | bytes 131104 | tf_op jit(solution)/shard_map/ppermute | solution.py:365
  83.8 2.7 %s_pack.1 = (f32[32,80,128]{2,1,0:T(8,128)S(1)}, s32[1]{0:T(128)}) custom-call(s32[256]{0:T(256)S(1)} %copy-done.6, s32[2]{0:T(128)S(1)} %pad_add_fusion.refs_1_.place, f32[2,256,128]{2,1,0:T(8,128)S(1)} %constant_dynamic-slice_fusion.1.refs_2_, f32[2,256,128]{2,1,0:T(8,128)S(1)} %collective-permute-done.refs_3_, ...), custom_call_target="tpu_custom_call" | custom-call | tf_op jit(solution)/shard_map/s_pack/pallas_call | solution.py:382
  86.6 1.0 copy-done.4
  87.6 7.6 %all-to-all-start = ((f32[32,80,128]{2,1,0:T(8,128)}), f32[32,80,128]{2,1,0:T(8,128)}, u32[]{:S(2)}, u32[]{:S(2)}) async-start(f32[32,80,128]{2,1,0:T(8,128)} %copy-done.4), calls=%async_computation | async-start | bytes 2621440 | tf_op jit(solution)/shard_map/all_to_all | solution.py:395
  95.3 18.7 %all-gather = s32[4,1,2]{2,1,0:T(1,128)S(1)} all-gather(s32[1,1,2]{2,1,0:T(1,128)S(1)} %bitcast.20), channel_id=1, replica_groups=mesh['yh'=2,'core'=2,'yl'=2,'z'=8,'x'=4] {'yh','core'}, dimensions={0}, use_global_device_ids=true | all-gather | bytes 40 | tf_op jit(solution)/shard_map/all_gather | solution.py:374
  114.0 3.8 %coefficients.1 = (bf16[256,1280]{1,0:T(8,128)(2,1)S(1)}, bf16[256,512]{1,0:T(8,128)(2,1)S(1)}) custom-call(f32[8,6]{1,0:T(8,128)S(1)} %copy-done.7, s32[4,2]{1,0:T(4,128)S(1)} %bitcast.19, s32[1]{0:T(128)} %get-tuple-element.14.refs_2_, f32[1,768]{1,0:T(1,128)S(1)} %copy-done.8, s32[3,768]{1,0:T(4,128)S(1)} %copy-done.5), custom_call_target="tpu_custom_call" | custom-call | tf_op jit(solution)/shard_map/coefficients/pallas_call | solution.py:401
  117.8 24.0 %u_words.1.partial = f32[64,256,128]{2,1,0:T(8,128)S(1)} custom-call(s32[2]{0:T(128)S(1)} %pad_add_fusion.refs_1_.place, f32[3584,128]{1,0:T(8,128)S(1)} %bitcast.18, bf16[256,1280]{1,0:T(8,128)(2,1)S(1)} %get-tuple-element.17.matrix), custom_call_target="tpu_custom_call" | custom-call | tf_op jit(solution)/shard_map/u_words/pallas_call | solution.py:414
  141.8 3.3 %copy-done.1 = f32[64,256,128]{2,1,0:T(8,128)} copy-done((f32[64,256,128]{2,1,0:T(8,128)}, f32[64,256,128]{2,1,0:T(8,128)S(1)}, u32[]{:S(2)}) %copy-start.1) | copy-done | bytes 8388632
  145.0 3.4 %copy-done.2 = f32[64,256,128]{2,1,0:T(8,128)S(1)} copy-done((f32[64,256,128]{2,1,0:T(8,128)S(1)}, f32[64,256,128]{2,1,0:T(8,128)}, u32[]{:S(2)}) %copy-start.2) | copy-done | bytes 8388632
  148.4 16.1 %s_words.1 = (f32[512,128]{1,0:T(8,128)}, f32[512,128]{1,0:T(8,128)}, f32[6,512,128]{2,1,0:T(8,128)}, f32[6,512,128]{2,1,0:T(8,128)}) custom-call(s32[2]{0:T(128)S(1)} %pad_add_fusion.refs_1_.place, f32[2560,128]{1,0:T(8,128)} %bitcast.2.received, bf16[256,512]{1,0:T(8,128)(2,1)S(1)} %get-tuple-element.15.matrix, f32[64,256,128]{2,1,0:T(8,128)S(1)} %copy-done.2), custom_call_target="tpu_custom_call" | custom-call | tf_op jit(solution)/shard_map/s_words/pallas_call | solution.py:429
  (37 shorter events, 0.6 us)
Async XLA Ops:
  0.6 1.2 copy-start
  1.9 12.2 %collective-permute-start.11 = (f32[2,256,128]{2,1,0:T(8,128)S(1)}, f32[2,256,128]{2,1,0:T(8,128)S(1)}, u32[]{:S(2)}, u32[]{:S(2)}) collective-permute-start(f32[2,256,128]{2,1,0:T(8,128)S(1)} %constant_dynamic-slice_fusion.refs_2_), channel_id=1, source_target_pairs={{0,4},{4,8},{8,12},{12,16},{16,20},{20,24},{24,28},{28,0},{1,5},{5... | collective-permute-start | bytes 786440 | tf_op jit(solution)/shard_map/ppermute | solution.py:363
  3.9 10.2 %collective-permute-start.8 = (f32[2,256,128]{2,1,0:T(8,128)S(1)}, f32[2,256,128]{2,1,0:T(8,128)S(1)}, u32[]{:S(2)}, u32[]{:S(2)}) collective-permute-start(f32[2,256,128]{2,1,0:T(8,128)S(1)} %constant_dynamic-slice_fusion.refs_2_), channel_id=1, source_target_pairs={{0,28},{4,0},{8,4},{12,8},{16,12},{20,16},{24,20},{28,24},{1,29},{... | collective-permute-start | bytes 786440 | tf_op jit(solution)/shard_map/ppermute | solution.py:364
  14.1 8.7 %collective-permute-start.12 = (f32[2,256,128]{2,1,0:T(8,128)S(1)}, f32[2,256,128]{2,1,0:T(8,128)S(1)}, u32[]{:S(2)}, u32[]{:S(2)}) collective-permute-start(f32[2,256,128]{2,1,0:T(8,128)S(1)} %collective-permute-done.11.refs_6_), channel_id=1, source_target_pairs={{0,4},{4,8},{8,12},{12,16},{16,20},{20,24},{24,28},{28,0},{1,5},{5... | collective-permute-start | bytes 786440 | tf_op jit(solution)/shard_map/ppermute | solution.py:363
  14.1 8.7 %collective-permute-start.9 = (f32[2,256,128]{2,1,0:T(8,128)S(1)}, f32[2,256,128]{2,1,0:T(8,128)S(1)}, u32[]{:S(2)}, u32[]{:S(2)}) collective-permute-start(f32[2,256,128]{2,1,0:T(8,128)S(1)} %collective-permute-done.8.refs_3_), channel_id=1, source_target_pairs={{0,28},{4,0},{8,4},{12,8},{16,12},{20,16},{24,20},{28,24},{1,29},{... | collective-permute-start | bytes 786440 | tf_op jit(solution)/shard_map/ppermute | solution.py:364
  22.8 7.8 %collective-permute-start.13 = (f32[2,256,128]{2,1,0:T(8,128)S(1)}, f32[2,256,128]{2,1,0:T(8,128)S(1)}, u32[]{:S(2)}, u32[]{:S(2)}) collective-permute-start(f32[2,256,128]{2,1,0:T(8,128)S(1)} %collective-permute-done.12.refs_7_), channel_id=1, source_target_pairs={{0,4},{4,8},{8,12},{12,16},{16,20},{20,24},{24,28},{28,0},{1,5},{5... | collective-permute-start | bytes 786440 | tf_op jit(solution)/shard_map/ppermute | solution.py:363
  22.8 7.9 %collective-permute-start.10 = (f32[2,256,128]{2,1,0:T(8,128)S(1)}, f32[2,256,128]{2,1,0:T(8,128)S(1)}, u32[]{:S(2)}, u32[]{:S(2)}) collective-permute-start(f32[2,256,128]{2,1,0:T(8,128)S(1)} %collective-permute-done.9.refs_4_), channel_id=1, source_target_pairs={{0,28},{4,0},{8,4},{12,8},{16,12},{20,16},{24,20},{28,24},{1,29},{... | collective-permute-start | bytes 786440 | tf_op jit(solution)/shard_map/ppermute | solution.py:364
  30.6 6.3 %collective-permute-start.14 = (f32[1,256,128]{2,1,0:T(8,128)S(1)}, f32[1,256,128]{2,1,0:T(8,128)S(1)}, u32[]{:S(2)}, u32[]{:S(2)}) collective-permute-start(f32[1,256,128]{2,1,0:T(8,128)S(1)} %slice.18), channel_id=1, source_target_pairs={{0,4},{4,8},{8,12},{12,16},{16,20},{20,24},{24,28},{28,0},{1,5},{5... | collective-permute-start | bytes 393224 | tf_op jit(solution)/shard_map/ppermute | solution.py:365
  30.7 6.1 %collective-permute-start.15 = (f32[1,256,128]{2,1,0:T(8,128)S(1)}, f32[1,256,128]{2,1,0:T(8,128)S(1)}, u32[]{:S(2)}, u32[]{:S(2)}) collective-permute-start(f32[1,256,128]{2,1,0:T(8,128)S(1)} %slice.19), channel_id=1, source_target_pairs={{0,28},{4,0},{8,4},{12,8},{16,12},{20,16},{24,20},{28,24},{1,29},{... | collective-permute-start | bytes 393224 | tf_op jit(solution)/shard_map/ppermute | solution.py:365
  36.9 0.7 copy-start.6
  40.3 1.3 copy-start.3
  41.6 46.1 %all-to-all-start.1 = ((f32[32,112,128]{2,1,0:T(8,128)}), f32[32,112,128]{2,1,0:T(8,128)S(1)}, u32[]{:S(2)}, u32[]{:S(2)}) async-start(f32[32,112,128]{2,1,0:T(8,128)} %copy-done.3), calls=%async_computation.1 | async-start | bytes 3670016 | tf_op jit(solution)/shard_map/all_to_all | solution.py:395
  50.1 10.0 %collective-permute-start.3 = (f32[2,256,128]{2,1,0:T(8,128)S(1)}, f32[2,256,128]{2,1,0:T(8,128)S(1)}, u32[]{:S(2)}, u32[]{:S(2)}) collective-permute-start(f32[2,256,128]{2,1,0:T(8,128)S(1)} %constant_dynamic-slice_fusion.1.refs_2_), channel_id=1, source_target_pairs={{0,4},{4,8},{8,12},{12,16},{16,20},{20,24},{24,28},{28,0},{1,5},{5... | collective-permute-start | bytes 786440 | tf_op jit(solution)/shard_map/ppermute | solution.py:363
  50.2 9.9 %collective-permute-start = (f32[2,256,128]{2,1,0:T(8,128)S(1)}, f32[2,256,128]{2,1,0:T(8,128)S(1)}, u32[]{:S(2)}, u32[]{:S(2)}) collective-permute-start(f32[2,256,128]{2,1,0:T(8,128)S(1)} %constant_dynamic-slice_fusion.1.refs_2_), channel_id=1, source_target_pairs={{0,28},{4,0},{8,4},{12,8},{16,12},{20,16},{24,20},{28,24},{1,29},{... | collective-permute-start | bytes 786440 | tf_op jit(solution)/shard_map/ppermute | solution.py:364
  60.1 9.1 %collective-permute-start.4 = (f32[2,256,128]{2,1,0:T(8,128)S(1)}, f32[2,256,128]{2,1,0:T(8,128)S(1)}, u32[]{:S(2)}, u32[]{:S(2)}) collective-permute-start(f32[2,256,128]{2,1,0:T(8,128)S(1)} %collective-permute-done.3.refs_6_), channel_id=1, source_target_pairs={{0,4},{4,8},{8,12},{12,16},{16,20},{20,24},{24,28},{28,0},{1,5},{5... | collective-permute-start | bytes 786440 | tf_op jit(solution)/shard_map/ppermute | solution.py:363
  60.1 9.1 %collective-permute-start.1 = (f32[2,256,128]{2,1,0:T(8,128)S(1)}, f32[2,256,128]{2,1,0:T(8,128)S(1)}, u32[]{:S(2)}, u32[]{:S(2)}) collective-permute-start(f32[2,256,128]{2,1,0:T(8,128)S(1)} %collective-permute-done.refs_3_), channel_id=1, source_target_pairs={{0,28},{4,0},{8,4},{12,8},{16,12},{20,16},{24,20},{28,24},{1,29},{... | collective-permute-start | bytes 786440 | tf_op jit(solution)/shard_map/ppermute | solution.py:364
  69.2 8.2 %collective-permute-start.5 = (f32[2,256,128]{2,1,0:T(8,128)S(1)}, f32[2,256,128]{2,1,0:T(8,128)S(1)}, u32[]{:S(2)}, u32[]{:S(2)}) collective-permute-start(f32[2,256,128]{2,1,0:T(8,128)S(1)} %collective-permute-done.4.refs_7_), channel_id=1, source_target_pairs={{0,4},{4,8},{8,12},{12,16},{16,20},{20,24},{24,28},{28,0},{1,5},{5... | collective-permute-start | bytes 786440 | tf_op jit(solution)/shard_map/ppermute | solution.py:363
  69.2 8.4 %collective-permute-start.2 = (f32[2,256,128]{2,1,0:T(8,128)S(1)}, f32[2,256,128]{2,1,0:T(8,128)S(1)}, u32[]{:S(2)}, u32[]{:S(2)}) collective-permute-start(f32[2,256,128]{2,1,0:T(8,128)S(1)} %collective-permute-done.1.refs_4_), channel_id=1, source_target_pairs={{0,28},{4,0},{8,4},{12,8},{16,12},{20,16},{24,20},{28,24},{1,29},{... | collective-permute-start | bytes 786440 | tf_op jit(solution)/shard_map/ppermute | solution.py:364
  77.4 6.4 %collective-permute-start.6 = (f32[1,256,128]{2,1,0:T(8,128)S(1)}, f32[1,256,128]{2,1,0:T(8,128)S(1)}, u32[]{:S(2)}, u32[]{:S(2)}) collective-permute-start(f32[1,256,128]{2,1,0:T(8,128)S(1)} %slice.16), channel_id=1, source_target_pairs={{0,4},{4,8},{8,12},{12,16},{16,20},{20,24},{24,28},{28,0},{1,5},{5... | collective-permute-start | bytes 393224 | tf_op jit(solution)/shard_map/ppermute | solution.py:365
  77.7 6.1 %collective-permute-start.7 = (f32[1,256,128]{2,1,0:T(8,128)S(1)}, f32[1,256,128]{2,1,0:T(8,128)S(1)}, u32[]{:S(2)}, u32[]{:S(2)}) collective-permute-start(f32[1,256,128]{2,1,0:T(8,128)S(1)} %slice.17), channel_id=1, source_target_pairs={{0,28},{4,0},{8,4},{12,8},{16,12},{20,16},{24,20},{28,24},{1,29},{... | collective-permute-start | bytes 393224 | tf_op jit(solution)/shard_map/ppermute | solution.py:365
  86.5 1.1 copy-start.4
  87.6 7.7 %copy-start.9 = (s32[1,2]{1,0:T(1,128)S(1)}, s32[1,2]{1,0:T(1,128)}, u32[]{:S(2)}) copy-start(s32[1,2]{1,0:T(1,128)} %param.10) | copy-start | bytes 28
  87.6 26.4 %copy-start.5 = (s32[3,768]{1,0:T(4,128)S(1)}, s32[3,768]{1,0:T(4,128)}, u32[]{:S(2)}) copy-start(s32[3,768]{1,0:T(4,128)} %constant.39.clone.refs_4_) | copy-start | bytes 27652
  87.6 26.4 %copy-start.7 = (f32[8,6]{1,0:T(8,128)S(1)}, f32[8,6]{1,0:T(8,128)}, u32[]{:S(2)}) copy-start(f32[8,6]{1,0:T(8,128)} %refs_0_.5) | copy-start | bytes 580
  87.6 26.4 %copy-start.8 = (f32[1,768]{1,0:T(1,128)S(1)}, f32[1,768]{1,0:T(1,128)}, u32[]{:S(2)}) copy-start(f32[1,768]{1,0:T(1,128)} %constant.38.clone.refs_3_) | copy-start | bytes 9220
  87.6 57.4 %all-to-all-start = ((f32[32,80,128]{2,1,0:T(8,128)}), f32[32,80,128]{2,1,0:T(8,128)}, u32[]{:S(2)}, u32[]{:S(2)}) async-start(f32[32,80,128]{2,1,0:T(8,128)} %copy-done.4), calls=%async_computation | async-start | bytes 2621440 | tf_op jit(solution)/shard_map/all_to_all | solution.py:395
  141.7 3.3 %copy-start.1 = (f32[64,256,128]{2,1,0:T(8,128)}, f32[64,256,128]{2,1,0:T(8,128)S(1)}, u32[]{:S(2)}) copy-start(f32[64,256,128]{2,1,0:T(8,128)S(1)} %u_words.1.partial) | copy-start | bytes 25165828
  145.0 3.4 %copy-start.2 = (f32[64,256,128]{2,1,0:T(8,128)S(1)}, f32[64,256,128]{2,1,0:T(8,128)}, u32[]{:S(2)}) copy-start(f32[64,256,128]{2,1,0:T(8,128)} %copy-done.1) | copy-start | bytes 25165828

commit v4 on v2

--- a/solution.py
+++ b/solution.py
@@ -19,6 +19,8 @@
 COLUMNS = SECTION + 256
 (ALPHA, KAPPA, HX, HZ, STRENGTH, UP, DOWN, UP2, DOWN2, U0, U0A, U1, UM1, S0, S0A, ONE) = range(16)
 PAD = 8
+GROUP = 4
+DEEP = 4
 
 
 def terms():
@@ -69,8 +71,10 @@
     return factor, which
 
 
-def near_pack_kernel(owner, place, initial, source, send, row, padded_u, padded_s, inverse, sems):
+def near_pack_kernel(place, owner_there, initial, source, send, padded_u, padded_s, ready, owner, inverse, sems):
     count = owner.shape[0]
+    listed = pltpu.make_async_copy(owner_there, owner, sems.at[6])
+    listed.start()
     servers = send.shape[0]
     inner = pl.ds(PAD, count)
     copies = [
@@ -83,14 +87,14 @@
         for x in range(8):
             ref[x, :PAD] = jnp.zeros((PAD, 128), jnp.float32)
             ref[x, PAD + count :] = jnp.zeros((PAD, 128), jnp.float32)
-    group, device = place[0], place[1]
+    group = place[0]
+    listed.wait()
 
     def invert(i, carry):
         inverse[owner[i]] = i
         return carry
 
     lax.fori_loop(0, count, invert, 0, unroll=8)
-    row[0] = inverse[device]
     for copy in copies:
         copy.wait()
     first = lax.broadcasted_iota(jnp.int32, (8, 128), 0) < NEAR_U
@@ -100,10 +104,18 @@
         for x in range(8):
             rows_u = padded_u[x, pl.ds(p - NEAR_U // 2, 8), :]
             rows_s = padded_s[x, pl.ds(p - NEAR_S // 2 - NEAR_U, 8), :]
-            send[s, x] = jnp.where(first, rows_u, rows_s)
-        return carry
-
-    lax.fori_loop(0, servers, fill, 0, unroll=2)
+            ready[s, x] = jnp.where(first, rows_u, rows_s)
+        return carry
+
+    copies = []
+    many = servers // 4
+    for part in range(4):
+        lax.fori_loop(part * many, part * many + many, fill, 0, unroll=2)
+        here = pl.ds(part * many, many)
+        copies.append(pltpu.make_async_copy(ready.at[here], send.at[here], sems.at[2 + part]))
+        copies[-1].start()
+    for copy in copies:
+        copy.wait()
 
 
 def far_pack_kernel(owner, place, initial, source, send, inverse):
@@ -129,8 +141,13 @@
     lax.fori_loop(0, servers, fill, 0, unroll=2)
 
 
-def coefficient_kernel(rows_y, table, pairs, row, factor, which, near, far):
-    p = row[0]
+def coefficient_kernel(table, pairs, owner, place, factor, which, near, far):
+    rows_y = owner.shape[0]
+
+    def find(i, found):
+        return jnp.where(owner[i] == place[1], i, found)
+
+    p = lax.fori_loop(0, rows_y, find, 0, unroll=8)
     run = lax.broadcasted_iota(jnp.int32, (64, 128), 0) // 8
     lane = lax.broadcasted_iota(jnp.int32, (64, 128), 1)
     same = lax.broadcasted_iota(jnp.int32, (64, 128), 0) % 8 == lane % 8
@@ -192,7 +209,7 @@
                 far[rows, :] = tail.astype(jnp.bfloat16)
 
 
-def near_kernel(received, matrix, partial, rows, one, two, phi):
+def near_kernel(received, matrix, partial, rows, one, two, phi, ready, sems):
     blocks = partial.shape[0]
     size = 8 * blocks
     lane = lax.broadcasted_iota(jnp.int32, (8, 128), 1)
@@ -267,10 +284,20 @@
         out += words(6, 3) + words(7, None) + words(5, None)
         return out
 
-    def stage3(pair, carry):
-        for half in range(2):
-            columns = slice(128 * half, 128 * half + 128)
-            listed = features(2 * pair + half)
+    def sent(group, slot):
+        here = partial.at[pl.ds(GROUP * group, GROUP)]
+        return pltpu.make_async_copy(ready.at[slot], here, sems.at[slot])
+
+    def stage3(group, carry):
+        slot = group % 2
+
+        @pl.when(group >= 2)
+        def _():
+            sent(group - 2, slot).wait()
+
+        for n in range(GROUP):
+            columns = slice(128 * n, 128 * n + 128)
+            listed = features(GROUP * group + n)
             for i in range(0, NEAR, 2):
                 value = jnp.concatenate([listed[i], listed[i + 1]], axis=0)
                 high = value.astype(jnp.bfloat16)
@@ -281,60 +308,101 @@
                 for place, part in zip(places, (high, low, high)):
                     phi[place : place + 16, columns] = part
         result = jnp.dot(matrix[...], phi[...], preferred_element_type=jnp.float32)
-        partial[2 * pair] = result[:, :128]
-        partial[2 * pair + 1] = result[:, 128:]
-        return carry
-
-    lax.fori_loop(0, blocks // 2, stage3, 0)
-
-
-def far_kernel(received, matrix, partial, mean, variance, first, total, phi, result):
+        for n in range(GROUP):
+            ready[slot, n] = result[:, 128 * n : 128 * n + 128]
+        sent(group, slot).start()
+        return carry
+
+    groups = blocks // GROUP
+    lax.fori_loop(0, groups, stage3, 0)
+    for group in (groups - 2, groups - 1):
+        sent(group, group % 2).wait()
+
+
+def far_kernel(received, matrix, partial, mean, variance, first, total,
+               phi, result, near, mean_out, variance_out, first_out, total_out, near_sems, sems):
     blocks = partial.shape[0]
-
-    @pl.when(pl.program_id(0) == 0)
-    def _():
-        phi[96:, :] = jnp.zeros((32, phi.shape[1]), phi.dtype)
-
-    for b in range(blocks):
-        columns = slice(128 * b, 128 * b + 128)
-        for i in range(0, FAR, 2):
-            value = received[b, i : i + 2].reshape(16, 128)
-            high = value.astype(jnp.bfloat16)
-            low = (value - high.astype(jnp.float32)).astype(jnp.bfloat16)
-            for place, part in zip((8 * i, 32 + 8 * i, 64 + 8 * i), (high, low, high)):
-                phi[place : place + 16, columns] = part
-    result[...] = jnp.dot(matrix[...], phi[...], preferred_element_type=jnp.float32)
-    for b in range(blocks):
-        columns = slice(128 * b, 128 * b + 128)
-        out = slice(8 * b, 8 * b + 8)
-
-        def run(number):
-            rows = slice(8 * number, 8 * number + 8)
-            return result[rows, columns] + partial[b, rows, :]
-
-        def add(old, new):
-            return new if old is None else old + new
-
-        both = square = None
-        firsts, totals = [None] * 6, [None] * 6
-        for group in range(4):
-            run_a, run_b = run(8 * group), run(8 * group + 1)
-            both = add(both, run_a + run_b)
-            square = add(square, run_a * run_a + run_b * run_b)
+    groups = blocks // GROUP
+    phi[96:, :] = jnp.zeros((32, phi.shape[1]), phi.dtype)
+
+    def fetched(group, slot):
+        return pltpu.make_async_copy(partial.at[pl.ds(GROUP * group, GROUP)], near.at[slot], near_sems.at[slot])
+
+    for group in range(DEEP - 1):
+        fetched(group, group).start()
+
+    def add(old, new):
+        return new if old is None else old + new
+
+    def body(group, carry):
+        slot = group % DEEP
+
+        @pl.when(group + DEEP - 1 < groups)
+        def _():
+            fetched(group + DEEP - 1, (group + DEEP - 1) % DEEP).start()
+
+        for n in range(GROUP):
+            columns = slice(128 * n, 128 * n + 128)
+            for i in range(0, FAR, 2):
+                value = received[GROUP * group + n, i : i + 2].reshape(16, 128)
+                high = value.astype(jnp.bfloat16)
+                low = (value - high.astype(jnp.float32)).astype(jnp.bfloat16)
+                for place, part in zip((8 * i, 32 + 8 * i, 64 + 8 * i), (high, low, high)):
+                    phi[place : place + 16, columns] = part
+        result[...] = jnp.dot(matrix[...], phi[...], preferred_element_type=jnp.float32)
+        fetched(group, slot).wait()
+        for n in range(GROUP):
+            columns = slice(128 * n, 128 * n + 128)
+            out = pl.ds(pl.multiple_of(8 * (GROUP * group + n), 8), 8)
+
+            def run(number):
+                rows = slice(8 * number, 8 * number + 8)
+                return result[rows, columns] + near[slot, n, rows, :]
+
+            both = square = None
+            firsts, totals = [None] * 6, [None] * 6
+            for g in range(4):
+                run_a, run_b = run(8 * g), run(8 * g + 1)
+                both = add(both, run_a + run_b)
+                square = add(square, run_a * run_a + run_b * run_b)
+                for i in range(6):
+                    gap = run(8 * g + 2 + i)
+                    firsts[i] = add(firsts[i], run_b * gap)
+                    totals[i] = add(totals[i], gap * gap)
+            average = both * 0.125
+            mean_out[out, :] = average
+            variance_out[out, :] = square * 0.125 - average * average
             for i in range(6):
-                gap = run(8 * group + 2 + i)
-                firsts[i] = add(firsts[i], run_b * gap)
-                totals[i] = add(totals[i], gap * gap)
-        average = both * 0.125
-        mean[out, :] = average
-        variance[out, :] = square * 0.125 - average * average
-        for i in range(6):
-            first[i, out, :] = firsts[i] * 0.25
-            total[i, out, :] = totals[i] * 0.125
+                first_out[i, out, :] = firsts[i] * 0.25
+                total_out[i, out, :] = totals[i] * 0.125
+        return carry
+
+    copies = []
+    quarter = groups // 4
+    size = 2 * blocks
+    for n in range(4):
+        lax.fori_loop(n * quarter, n * quarter + quarter, body, 0)
+        x = pl.ds(n * size, size)
+        for k, (here, there) in enumerate(((mean_out, mean), (variance_out, variance))):
+            copies.append(pltpu.make_async_copy(here.at[x, :], there.at[x, :], sems.at[4 * n + k]))
+            copies[-1].start()
+        for k, (here, there) in enumerate(((first_out, first), (total_out, total))):
+            copies.append(pltpu.make_async_copy(here.at[:, x, :], there.at[:, x, :], sems.at[4 * n + 2 + k]))
+            copies[-1].start()
+    for copy in copies:
+        copy.wait()
 
 
 def shape(*dims):
     return jax.ShapeDtypeStruct(dims, jnp.float32)
+
+
+def held(array):
+    return pltpu.with_memory_space_constraint(array, pltpu.HBM)
+
+
+def limit(mib):
+    return pltpu.CompilerParams(vmem_limit_bytes=mib * 2**20)
 
 
 def local(initial, source, table, pairs, owner):
@@ -345,22 +413,23 @@
     all_pairs = lax.all_gather(pairs, "group", axis=0, tiled=True)
     smem = pl.BlockSpec(memory_space=pltpu.SMEM)
     vmem = pl.BlockSpec(memory_space=pltpu.VMEM)
-    anywhere = pl.BlockSpec(memory_space=pl.ANY)
-    limit = pltpu.CompilerParams(vmem_limit_bytes=32 * 2**20)
-    near_send, row = pl.pallas_call(
+    hbm = pl.BlockSpec(memory_space=pltpu.HBM)
+    near_send = pl.pallas_call(
         near_pack_kernel,
-        out_shape=(shape(servers, 8, 8, cells_z), jax.ShapeDtypeStruct((1,), jnp.int32)),
-        in_specs=[smem, smem, anywhere, anywhere],
-        out_specs=(vmem, smem),
+        out_shape=pltpu.HBM((servers, 8, 8, cells_z), jnp.float32),
+        in_specs=[smem, hbm, hbm, hbm],
+        out_specs=hbm,
         scratch_shapes=[
             pltpu.VMEM((8, rows_y + 2 * PAD, cells_z), jnp.float32),
             pltpu.VMEM((8, rows_y + 2 * PAD, cells_z), jnp.float32),
+            pltpu.VMEM((servers, 8, 8, cells_z), jnp.float32),
             pltpu.SMEM((rows_y,), jnp.int32),
-            pltpu.SemaphoreType.DMA((2,)),
+            pltpu.SMEM((rows_y,), jnp.int32),
+            pltpu.SemaphoreType.DMA((7,)),
         ],
-        compiler_params=limit,
+        compiler_params=limit(8),
         name="near_pack",
-    )(owner, place, initial, source)
+    )(place, held(owner), held(initial), held(source))
     near_received = lax.all_to_all(near_send, "space", split_axis=0, concat_axis=0, tiled=True)
     far_send = pl.pallas_call(
         far_pack_kernel,
@@ -368,62 +437,61 @@
         in_specs=[smem, smem, vmem, vmem],
         out_specs=vmem,
         scratch_shapes=[pltpu.SMEM((rows_y,), jnp.int32)],
-        compiler_params=limit,
+        compiler_params=limit(8),
         name="far_pack",
     )(owner, place, initial.reshape(-1, cells_z), source.reshape(-1, cells_z))
-    far_received = lax.all_to_all(far_send, "space", split_axis=0, concat_axis=0, tiled=True)
     factor, which = layout()
-
-    def coefficients(*refs):
-        coefficient_kernel(rows_y, *refs)
-
     near_matrix, far_matrix = pl.pallas_call(
-        coefficients,
+        coefficient_kernel,
         out_shape=(
             jax.ShapeDtypeStruct((256, DEPTH), jnp.bfloat16),
             jax.ShapeDtypeStruct((256, 128), jnp.bfloat16),
         ),
-        in_specs=[smem, smem, smem, vmem, vmem],
+        in_specs=[smem, smem, smem, smem, vmem, vmem],
         out_specs=(vmem, vmem),
-        compiler_params=limit,
+        compiler_params=limit(8),
         name="coefficients",
-    )(table, all_pairs, row, jnp.asarray(factor), jnp.asarray(which))
+    )(table, all_pairs, owner, place, jnp.asarray(factor), jnp.asarray(which))
+    far_send, near_matrix, far_matrix = lax.optimization_barrier((far_send, near_matrix, far_matrix))
+    far_received = lax.all_to_all(far_send, "space", split_axis=0, concat_axis=0, tiled=True)
     cells_x = 8 * servers
     long = cells_x + 2 * PAD
     partial = pl.pallas_call(
         near_kernel,
-        out_shape=shape(servers, 256, cells_z),
+        out_shape=pltpu.HBM((servers, 256, cells_z), jnp.float32),
         in_specs=[vmem, vmem],
-        out_specs=vmem,
+        out_specs=hbm,
         scratch_shapes=[
             pltpu.VMEM((8, long, cells_z), jnp.float32),
             pltpu.VMEM((3, 8, long, cells_z), jnp.float32),
             pltpu.VMEM((6, 4, long, cells_z), jnp.float32),
-            pltpu.VMEM((DEPTH, 256), jnp.bfloat16),
+            pltpu.VMEM((DEPTH, 128 * GROUP), jnp.bfloat16),
+            pltpu.VMEM((2, GROUP, 256, cells_z), jnp.float32),
+            pltpu.SemaphoreType.DMA((2,)),
         ],
-        compiler_params=pltpu.CompilerParams(vmem_limit_bytes=48 * 2**20),
+        compiler_params=limit(24),
         name="near",
     )(near_received.reshape(-1, cells_z), near_matrix)
-    step = 4
-    flat = pl.BlockSpec((8 * step, cells_z), lambda j: (j, 0))
-    six = pl.BlockSpec((6, 8 * step, cells_z), lambda j: (0, j, 0))
+    flat, six = shape(cells_x, cells_z), shape(6, cells_x, cells_z)
     mean, variance, first, total = pl.pallas_call(
         far_kernel,
-        grid=(servers // step,),
-        out_shape=(shape(cells_x, cells_z), shape(cells_x, cells_z), shape(6, cells_x, cells_z), shape(6, cells_x, cells_z)),
-        in_specs=[
-            pl.BlockSpec((step, FAR, 8, cells_z), lambda j: (j, 0, 0, 0)),
-            pl.BlockSpec((256, 128), lambda j: (0, 0)),
-            pl.BlockSpec((step, 256, cells_z), lambda j: (j, 0, 0)),
+        out_shape=(flat, flat, six, six),
+        in_specs=[vmem, vmem, hbm],
+        out_specs=(hbm,) * 4,
+        scratch_shapes=[
+            pltpu.VMEM((128, 128 * GROUP), jnp.bfloat16),
+            pltpu.VMEM((256, 128 * GROUP), jnp.float32),
+            pltpu.VMEM((DEEP, GROUP, 256, cells_z), jnp.float32),
+            pltpu.VMEM(flat.shape, jnp.float32),
+            pltpu.VMEM(flat.shape, jnp.float32),
+            pltpu.VMEM(six.shape, jnp.float32),
+            pltpu.VMEM(six.shape, jnp.float32),
+            pltpu.SemaphoreType.DMA((DEEP,)),
+            pltpu.SemaphoreType.DMA((16,)),
         ],
-        out_specs=(flat, flat, six, six),
-        scratch_shapes=[
-            pltpu.VMEM((128, 128 * step), jnp.bfloat16),
-            pltpu.VMEM((256, 128 * step), jnp.float32),
-        ],
-        compiler_params=limit,
+        compiler_params=limit(16),
         name="far",
-    )(far_received, far_matrix, partial)
+    )(far_received, far_matrix, held(partial))
     return (
         mean.reshape(cells_x, 1, cells_z),
         variance.reshape(cells_x, 1, cells_z),

time: 133 us -> 111 us (0.83); the launches traced: 131 us -> 111 us
  waiting for transfers between devices: 46.7 us -> 36.5 us
  local copies, waits for them, and re-layouts: 10.1 us -> 4.28 us
  Pallas kernels: 48.2 us -> 43.2 us
    all_to_all x1, waiting for transfers between devices: 46.7 us -> 34.9 us  [local(): lax.all_to_all(near_send, 'space', split_axis=0, concat_axis=0, tiled=True)]
    unnamed x26 -> x20, local copies, waits for them, and re-layouts: 10.1 us -> 4.28 us
    pallas_call x4, Pallas kernels: 45.8 us -> 40.7 us  [the longest x1 25.7 us: local(): pl.pallas_call(near_kernel, out_shape=pltpu.HBM((servers, 256, cells_z),...]
    all_to_all x1, waiting for transfers between devices: 0.01 us -> 1.63 us  [local(): lax.all_to_all(far_send, 'space', split_axis=0, concat_axis=0, tiled=True)]
  transfers between devices with their start and end apart: 2 -> 2, of which waited for: 1 -> 2; matrix products, arithmetic and copies ran while one was open for 0% -> 0% of each run, Pallas kernels for 29% -> 29%
where the time goes in v4:
time: 111 us
  Pallas kernels  43.2 us (39%)
  waiting for transfers between devices  36.5 us (33%)
  starting transfers between devices  18.8 us (17%)
  blocking collectives  7.3 us (7%)
  local copies, waits for them, and re-layouts  4.28 us (4%)
    all_to_all x1, waiting for transfers between devices, local(): lax.all_to_all(near_send, 'space', split_axis=0, concat_axis=0, tiled=True)  34.9 us
    pallas_call x1, Pallas kernels, local(): pl.pallas_call(near_kernel, out_shape=pltpu.HBM((servers, 256, cells_z),...  25.7 us
    all_to_all x1, starting transfers between devices, local(): lax.all_to_all(near_send, 'space', split_axis=0, concat_axis=0, tiled=True)  13.1 us
    pallas_call x1, Pallas kernels, local(): pl.pallas_call(far_kernel, out_shape=(flat, flat, six, six), in_specs=[vm...  7.83 us
    all_gather x1, blocking collectives, local(): all_pairs = lax.all_gather(pairs, 'group', axis=0, tiled=True)  7.3 us
    all_to_all x1, starting transfers between devices, local(): lax.all_to_all(far_send, 'space', split_axis=0, concat_axis=0, tiled=True)  5.67 us
    unnamed x20, local copies, waits for them, and re-layouts  4.28 us
    pallas_call x1, Pallas kernels, local(): pl.pallas_call(coefficient_kernel, out_shape=(jax.ShapeDtypeStruct((256,...  3.59 us
  transfers between devices with their start and end apart: 2, of which 2 were waited for; matrix products, arithmetic and copies ran while one was open for 0% of the time, Pallas kernels for 29%

profile of v4, /device:TPU:6, one launch (start us, length us, event | category | flops | bytes accessed | tf_op | source)
XLA Modules:
  0.0 110.9 jit_solution(15850914085658313800)
XLA Ops:
  0.6 0.1 pad_add_fusion.place
  0.7 3.6 %near_pack.1 = f32[64,8,8,128]{3,2,1,0:T(8,128)} custom-call(s32[2]{0:T(128)S(1)} %pad_add_fusion.place, s32[256]{0:T(256)} %owner_there.1, f32[8,256,128]{2,1,0:T(8,128)} %initial.1, f32[8,256,128]{2,1,0:T(8,128)} %source.1), custom_call_target="tpu_custom_call" | custom-call | tf_op jit(solution)/shard_map/near_pack/pallas_call | solution.py:417
  4.3 0.0 copy-start.9
  4.3 0.0 copy-start
  4.3 0.0 copy-start.6
  4.3 0.0 copy-start.5
  4.4 13.1 %all-to-all-start.1 = ((f32[64,8,8,128]{3,2,1,0:T(8,128)}), f32[64,8,8,128]{3,2,1,0:T(8,128)S(1)}, u32[]{:S(2)}, u32[]{:S(2)}) async-start(f32[64,8,8,128]{3,2,1,0:T(8,128)} %near_pack.1), calls=%async_computation.1 | async-start | bytes 4194304 | tf_op jit(solution)/shard_map/all_to_all | solution.py:433
  17.5 0.0 copy-start.7
  17.5 0.0 copy-start.8
  17.5 0.0 copy-done.9
  17.5 7.3 %all-gather = s32[4,1,2]{2,1,0:T(1,128)S(1)} all-gather(s32[1,1,2]{2,1,0:T(1,128)S(1)} %bitcast.23), channel_id=1, replica_groups=mesh['group'=4,'space'=64] {'group'}, dimensions={0}, use_global_device_ids=true | all-gather | bytes 40 | tf_op jit(solution)/shard_map/all_gather | solution.py:413
  24.8 0.0 copy-done
  24.8 0.0 copy-done.6
  24.8 0.0 copy-start.1
  24.8 1.2 %copy-done.1 = f32[8,256,128]{2,1,0:T(8,128)S(1)} copy-done((f32[8,256,128]{2,1,0:T(8,128)S(1)}, f32[8,256,128]{2,1,0:T(8,128)}, u32[]{:S(2)}) %copy-start.1) | copy-done | bytes 1048600
  26.0 2.5 %far_pack.1 = f32[64,4,8,128]{3,2,1,0:T(8,128)S(1)} custom-call(s32[256]{0:T(256)S(1)} %copy-done.6, s32[2]{0:T(128)S(1)} %pad_add_fusion.place, f32[2048,128]{1,0:T(8,128)S(1)} %bitcast.20, f32[2048,128]{1,0:T(8,128)S(1)} %bitcast.21), custom_call_target="tpu_custom_call" | custom-call | tf_op jit(solution)/shard_map/far_pack/pallas_call | solution.py:434
  28.5 0.0 copy-start.2
  28.5 1.0 copy-done.2
  29.5 0.0 copy-done.5
  29.5 0.0 copy-done.7
  29.5 0.0 copy-done.8
  29.5 3.6 %coefficients.1 = (bf16[256,1664]{1,0:T(8,128)(2,1)S(1)}, bf16[256,128]{1,0:T(8,128)(2,1)S(1)}) custom-call(f32[8,6]{1,0:T(8,128)S(1)} %copy-done.7, s32[4,2]{1,0:T(4,128)S(1)} %bitcast.22, s32[256]{0:T(256)S(1)} %copy-done.6, s32[2]{0:T(128)S(1)} %pad_add_fusion.place, f32[1,768]{1,0:T(1,128)S(1)} %copy-done.8, s32[3,768]{1,0:T(4,128)S(1)} %copy-done.5), custom_call_target="tpu_custom_call" | custom-call | tf_op jit(solution)/shard_map/coefficients/pallas_call | solution.py:444
  33.1 0.0 copy-start.3
  33.1 0.9 copy-done.3
  34.0 34.9 %all-to-all-done.1 = f32[64,8,8,128]{3,2,1,0:T(8,128)S(1)} async-done(((f32[64,8,8,128]{3,2,1,0:T(8,128)}), f32[64,8,8,128]{3,2,1,0:T(8,128)S(1)}, u32[]{:S(2)}, u32[]{:S(2)}) %all-to-all-start.1) | async-done | bytes 2097184 | tf_op jit(solution)/shard_map/all_to_all | solution.py:433
  68.9 5.7 %all-to-all-start = ((f32[64,4,8,128]{3,2,1,0:T(8,128)}), f32[64,4,8,128]{3,2,1,0:T(8,128)S(1)}, u32[]{:S(2)}, u32[]{:S(2)}) async-start(f32[64,4,8,128]{3,2,1,0:T(8,128)} %copy-done.2), calls=%async_computation | async-start | bytes 2097152 | tf_op jit(solution)/shard_map/all_to_all | solution.py:456
  74.5 0.0 copy-start.4
  74.5 1.1 %copy-done.4 = bf16[256,1664]{1,0:T(8,128)(2,1)S(1)} copy-done((bf16[256,1664]{1,0:T(8,128)(2,1)S(1)}, bf16[256,1664]{1,0:T(8,128)(2,1)}, u32[]{:S(2)}) %copy-start.4) | copy-done | bytes 851992
  75.7 25.7 %near.1.partial = f32[64,256,128]{2,1,0:T(8,128)} custom-call(f32[4096,128]{1,0:T(8,128)S(1)} %bitcast.19, bf16[256,1664]{1,0:T(8,128)(2,1)S(1)} %copy-done.4), custom_call_target="tpu_custom_call" | custom-call | tf_op jit(solution)/shard_map/near/pallas_call | solution.py:459
  101.4 1.6 %all-to-all-done.received = f32[64,4,8,128]{3,2,1,0:T(8,128)S(1)} async-done(((f32[64,4,8,128]{3,2,1,0:T(8,128)}), f32[64,4,8,128]{3,2,1,0:T(8,128)S(1)}, u32[]{:S(2)}, u32[]{:S(2)}) %all-to-all-start) | async-done | bytes 1048608 | tf_op jit(solution)/shard_map/all_to_all | solution.py:456
  103.0 7.8 %far.1 = (f32[512,128]{1,0:T(8,128)}, f32[512,128]{1,0:T(8,128)}, f32[6,512,128]{2,1,0:T(8,128)}, f32[6,512,128]{2,1,0:T(8,128)}) custom-call(f32[64,4,8,128]{3,2,1,0:T(8,128)S(1)} %all-to-all-done.received, bf16[256,128]{1,0:T(8,128)(2,1)S(1)} %get-tuple-element.16.matrix, f32[64,256,128]{2,1,0:T(8,128)} %near.1.partial), custom_call_target="tpu_custom_call" | custom-call | tf_op jit(solution)/shard_map/far/pallas_call | solution.py:476
Async XLA Ops:
  4.3 13.2 %copy-start.9 = (s32[1,2]{1,0:T(1,128)S(1)}, s32[1,2]{1,0:T(1,128)}, u32[]{:S(2)}) copy-start(s32[1,2]{1,0:T(1,128)} %param.10) | copy-start | bytes 28
  4.3 20.5 %copy-start = (f32[8,256,128]{2,1,0:T(8,128)S(1)}, f32[8,256,128]{2,1,0:T(8,128)}, u32[]{:S(2)}) copy-start(f32[8,256,128]{2,1,0:T(8,128)} %initial.1) | copy-start | bytes 3145732
  4.3 20.5 %copy-start.6 = (s32[256]{0:T(256)S(1)}, s32[256]{0:T(256)}, u32[]{:S(2)}) copy-start(s32[256]{0:T(256)} %owner_there.1) | copy-start | bytes 3076
  4.3 25.1 %copy-start.5 = (s32[3,768]{1,0:T(4,128)S(1)}, s32[3,768]{1,0:T(4,128)}, u32[]{:S(2)}) copy-start(s32[3,768]{1,0:T(4,128)} %constant.16.clone.which) | copy-start | bytes 27652
  4.4 64.5 %all-to-all-start.1 = ((f32[64,8,8,128]{3,2,1,0:T(8,128)}), f32[64,8,8,128]{3,2,1,0:T(8,128)S(1)}, u32[]{:S(2)}, u32[]{:S(2)}) async-start(f32[64,8,8,128]{3,2,1,0:T(8,128)} %near_pack.1), calls=%async_computation.1 | async-start | bytes 4194304 | tf_op jit(solution)/shard_map/all_to_all | solution.py:433
  17.5 12.0 %copy-start.7 = (f32[8,6]{1,0:T(8,128)S(1)}, f32[8,6]{1,0:T(8,128)}, u32[]{:S(2)}) copy-start(f32[8,6]{1,0:T(8,128)} %table.1) | copy-start | bytes 580
  17.5 12.0 %copy-start.8 = (f32[1,768]{1,0:T(1,128)S(1)}, f32[1,768]{1,0:T(1,128)}, u32[]{:S(2)}) copy-start(f32[1,768]{1,0:T(1,128)} %constant.15.clone.factor) | copy-start | bytes 9220
  24.8 1.2 %copy-start.1 = (f32[8,256,128]{2,1,0:T(8,128)S(1)}, f32[8,256,128]{2,1,0:T(8,128)}, u32[]{:S(2)}) copy-start(f32[8,256,128]{2,1,0:T(8,128)} %source.1) | copy-start | bytes 3145732
  28.5 1.0 copy-start.2
  33.1 0.9 copy-start.3
  68.9 34.2 %all-to-all-start = ((f32[64,4,8,128]{3,2,1,0:T(8,128)}), f32[64,4,8,128]{3,2,1,0:T(8,128)S(1)}, u32[]{:S(2)}, u32[]{:S(2)}) async-start(f32[64,4,8,128]{3,2,1,0:T(8,128)} %copy-done.2), calls=%async_computation | async-start | bytes 2097152 | tf_op jit(solution)/shard_map/all_to_all | solution.py:456
  74.5 1.2 %copy-start.4 = (bf16[256,1664]{1,0:T(8,128)(2,1)S(1)}, bf16[256,1664]{1,0:T(8,128)(2,1)}, u32[]{:S(2)}) copy-start(bf16[256,1664]{1,0:T(8,128)(2,1)} %copy-done.3) | copy-start | bytes 2555908

commit v5 on v4

v5 whole, which is shorter than its diff:
```python
import itertools

import jax
import jax.numpy as jnp
import numpy as np
from jax import lax
from jax.experimental import pallas as pl
from jax.experimental.pallas import tpu as pltpu
from jax.sharding import PartitionSpec as P


NEAR_U, NEAR_S, FAR = 5, 3, 4
PAIRS2 = list(itertools.combinations_with_replacement(range(3), 2))
PAIRS3 = list(itertools.combinations_with_replacement(range(3), 3))
FEATURES = 70
WIDE = 64
REST = FEATURES - WIDE
SECTION = WIDE * 8
HIGH = SECTION + 128
TALL = HIGH + SECTION
DEPTH = TALL + HIGH
COLUMNS = SECTION + 128
(ALPHA, KAPPA, HX, HZ, STRENGTH, UP, DOWN, UP2, DOWN2, U0, U0A, U1, UM1, S0, S0A, ONE) = range(16)
PAD = 8
STAGES = 4
GROUP = 4
HELD = 96


def terms():
    word = (KAPPA, HX, HZ)

    def twice(i, j):
        return 2.0 if i != j and i > 0 else 1.0

    def thrice(i, j, k):
        return {1: 1.0, 2: 3.0, 3: 6.0}[len({i, j, k})] if i > 0 else 1.0

    out = [(1.0, U0, ONE, ONE)]
    out += [(1.0, U0A, w, ONE) for w in word]
    out += [(3.0 * twice(i, j), ALPHA, word[i], word[j]) for i, j in PAIRS2]
    out += [(thrice(i, j, k), word[i], word[j], word[k]) for i, j, k in PAIRS3]
    for whole, step in ((U1, UP), (UM1, DOWN)):
        out.append((1.0, whole, ONE, ONE))
        out += [(6.0, step, ALPHA, w) for w in word]
        out += [(3.0 * twice(i, j), step, word[i], word[j]) for i, j in PAIRS2]
    for square in (UP2, DOWN2):
        out.append((3.0, square, ALPHA, ONE))
        out += [(3.0, square, w, ONE) for w in word]
    out.append((1.0, S0, ONE, ONE))
    out += [(1.0, S0A, w, ONE) for w in word]
    out += [(twice(i, j), STRENGTH, word[i], word[j]) for i, j in PAIRS2]
    for step in (UP, DOWN):
        out.append((1.0, S0A, step, ONE))
        out += [(2.0, STRENGTH, step, w) for w in word]
    far = [(1.0, DOWN2, DOWN, ONE), (1.0, UP2, UP, ONE), (1.0, STRENGTH, DOWN2, ONE), (1.0, STRENGTH, UP2, ONE)]
    return out + far


def layout():
    listed = terms()
    factor = np.zeros((1, COLUMNS), np.float32)
    which = np.full((3, COLUMNS), ONE, np.int32)
    for column in range(SECTION + 16 * REST):
        rest = WIDE + (column - SECTION) // 8 % REST
        term = listed[column // 8 if column < SECTION else rest]
        factor[0, column] = term[0]
        which[:, column] = term[1:]
    return factor, which


def pack_kernel(place, owner_there, initial, source, send, padded_u, padded_s, ready, owner, inverse, in_sems, out_sems):
    count = owner.shape[0]
    servers = send.shape[0]
    listed = pltpu.make_async_copy(owner_there, owner, in_sems.at[2 * STAGES])
    listed.start()
    many = 8 // STAGES
    copies = []
    for n in range(STAGES):
        x = pl.ds(many * n, many)
        for k, (there, here) in enumerate(((initial, padded_u), (source, padded_s))):
            inner = here.at[x, pl.ds(PAD, count), :]
            copies.append(pltpu.make_async_copy(there.at[x], inner, in_sems.at[2 * n + k]))
            copies[-1].start()
    for ref in (padded_u, padded_s):
        for x in range(8):
            ref[x, :PAD] = jnp.zeros((PAD, 128), jnp.float32)
            ref[x, PAD + count :] = jnp.zeros((PAD, 128), jnp.float32)
    group = place[0]
    listed.wait()

    def invert(i, carry):
        inverse[owner[i]] = i
        return carry

    lax.fori_loop(0, count, invert, 0, unroll=16)
    first = lax.broadcasted_iota(jnp.int32, (8, 128), 0) < NEAR_U
    sent = []
    for n in range(STAGES):
        copies[2 * n].wait()
        copies[2 * n + 1].wait()

        def fill(s, carry):
            p = inverse[group * servers + s] + PAD
            for x in range(many * n, many * n + many):
                rows_u = padded_u[x, pl.ds(p - NEAR_U // 2, 8), :]
                rows_s = padded_s[x, pl.ds(p - NEAR_S // 2 - NEAR_U, 8), :]
                ready[s, 8 * x : 8 * x + 8, :] = jnp.where(first, rows_u, rows_s)
            return carry

        lax.fori_loop(0, servers, fill, 0, unroll=8)
        here = pl.ds(8 * many * n, 8 * many)
        sent.append(pltpu.make_async_copy(ready.at[:, here], send.at[:, here], out_sems.at[n]))
        sent[-1].start()

    def fill_far(s, carry):
        p = inverse[group * servers + s] + PAD
        for k, (ref, step) in enumerate(((flat_u, -3), (flat_u, 3), (flat_s, -2), (flat_s, 2))):
            ready[s, 64 + 8 * k : 72 + 8 * k, :] = ref[pl.ds(p + step, 8, stride=count + 2 * PAD), :]
        return carry

    flat_u = padded_u.reshape(8 * (count + 2 * PAD), 128)
    flat_s = padded_s.reshape(8 * (count + 2 * PAD), 128)
    lax.fori_loop(0, servers, fill_far, 0, unroll=4)
    here = pl.ds(64, 32)
    sent.append(pltpu.make_async_copy(ready.at[:, here], send.at[:, here], out_sems.at[STAGES]))
    sent[-1].start()
    for copy in sent:
        copy.wait()


def coefficient_kernel(table, pairs, owner, place, factor, which, matrix):
    rows_y = owner.shape[0]

    def find(i, found):
        return jnp.where(owner[i] == place[1], i, found)

    p = lax.fori_loop(0, rows_y, find, 0, unroll=8)
    run = lax.broadcasted_iota(jnp.int32, (64, 128), 0) // 8
    lane = lax.broadcasted_iota(jnp.int32, (64, 128), 1)
    same = lax.broadcasted_iota(jnp.int32, (64, 128), 0) % 8 == lane % 8

    def inside(k):
        return jnp.where(jnp.logical_and(p + k >= 0, p + k < rows_y), 1.0, 0.0)

    ways = inside(1) + inside(-1)
    ways_up = inside(2) + 1.0 + inside(-1)
    ways_down = inside(-2) + 1.0 + inside(1)
    for group in range(4):
        first, second = pairs[group, 0], pairs[group, 1]
        q = []
        for k in range(6):
            swap = jnp.logical_or(run == 1, run == 2 + k)
            q.append(jnp.where(swap, table[second, k], table[first, k]))
        kappa = 0.03 + 0.12 * q[0]
        hx, hy, hz = (-0.5 * (0.3 * q[1 + i] - 0.15) for i in range(3))
        decay = 0.02 + 0.2 * q[4]
        strength = 0.5 + 1.5 * q[5]
        alpha = 1.0 - 6.0 * kappa - decay
        up, down = kappa + hy, kappa - hy
        both = up * down
        values = [None] * ONE
        values[ALPHA], values[KAPPA], values[HX], values[HZ] = alpha, kappa, hx, hz
        values[STRENGTH], values[UP], values[DOWN] = strength, up, down
        values[UP2], values[DOWN2] = up * up, down * down
        values[U0] = alpha * (alpha * alpha + 3.0 * ways * both)
        values[U0A] = 3.0 * (alpha * alpha + ways * both)
        values[U1] = up * (3.0 * alpha * alpha + ways_up * both)
        values[UM1] = down * (3.0 * alpha * alpha + ways_down * both)
        values[S0] = strength * (alpha * alpha + alpha + 1.0 + ways * both)
        values[S0A] = strength * (2.0 * alpha + 1.0)
        rows = slice(64 * group, 64 * group + 64)
        for chunk in range(COLUMNS // 128):
            columns = slice(128 * chunk, 128 * chunk + 128)
            product = jnp.broadcast_to(factor[:, columns], (64, 128))
            for part in range(3):
                index = jnp.broadcast_to(which[part : part + 1, columns], (64, 128))
                chosen = jnp.ones((64, 128), jnp.float32)
                for number, value in enumerate(values):
                    chosen = jnp.where(index == number, value, chosen)
                product = product * chosen
            split = product.reshape(8, 8, 128)
            split = jnp.concatenate([split[:2], split[2:] - split[:1]], axis=0)
            product = jnp.where(same, split.reshape(64, 128), 0.0)
            high = product.astype(jnp.bfloat16)
            low = product - high.astype(jnp.float32)
            if chunk == SECTION // 128:
                low = jnp.where(lane < 8 * REST, 0.0, low)
            else:
                matrix[rows, HIGH + 128 * chunk : HIGH + 128 * chunk + 128] = high
            matrix[rows, columns] = high
            last = TALL + 128 * ((chunk + 1) % (SECTION // 128 + 1))
            matrix[rows, last : last + 128] = low.astype(jnp.bfloat16)


def server_kernel(received, matrix_there, mean, variance, first, total, rows, one, two, phi_a, phi_b, result_a, result_b,
                  mean_out, variance_out, first_out, total_out, matrix, matrix_sem, sems):
    size = mean.shape[0]
    blocks = size // 8
    groups = blocks // GROUP
    lane = lax.broadcasted_iota(jnp.int32, (8, 128), 1)
    brought = pltpu.make_async_copy(matrix_there, matrix, matrix_sem.at[0])
    brought.start()
    zero = jnp.zeros((PAD, 128), jnp.float32)
    for ref, lead in ((rows, (8,)), (one, (3, 8)), (two, (6, 4))):
        for index in itertools.product(*(range(n) for n in lead)):
            ref[index + (slice(0, PAD),)] = zero
            ref[index + (slice(PAD + size, 2 * PAD + size),)] = zero
    for phi in (phi_a, phi_b):
        phi[SECTION + 16 * REST : HIGH, :] = jnp.zeros((128 - 16 * REST, phi.shape[1]), phi.dtype)

    def at(b, step=0):
        return pl.ds(pl.multiple_of(8 * b, 8) + PAD + step, 8)

    def copy(b, carry):
        for k in range(8):
            rows[k, at(b), :] = received[pl.ds(HELD * b + k, 8, stride=8), :]
        return carry

    lax.fori_loop(0, blocks, copy, 0, unroll=4)

    def parts(ref, lead, b):
        c = ref[lead + (at(b), slice(None))]
        east, west = ref[lead + (at(b, 1), slice(None))], ref[lead + (at(b, -1), slice(None))]
        up = jnp.where(lane == 127, 0.0, pltpu.roll(c, 127, 1))
        down = jnp.where(lane == 0, 0.0, pltpu.roll(c, 1, 1))
        return (east + west) + (up + down), east - west, up - down

    def stage1(b, carry):
        for k in range(8):
            for i, value in enumerate(parts(rows, (k,), b)):
                one[i, k, at(b), :] = value
        return carry

    lax.fori_loop(0, 5 * GROUP, stage1, 0, unroll=4)
    inner = (1, 2, 3, 6)

    def stage2(b, carry):
        for n, k in enumerate(inner):
            m, x, z = (parts(one, (i, k), b) for i in range(3))
            words = (m[0], x[0] + m[1], z[0] + m[2], x[1], z[1], z[2])
            for i, value in enumerate(words):
                two[i, n, at(b), :] = value
        return carry

    lax.fori_loop(0, 3 * GROUP, stage2, 0, unroll=4)

    def third(b):
        a = {pair: parts(two, (i, 1), b) for i, pair in enumerate(PAIRS2)}
        out = []
        for i, j, k in PAIRS3:
            if i > 0:
                value = a[(j, k)][i]
            elif j == 0 and k == 0:
                value = a[(0, 0)][0]
            elif j == 0:
                value = a[(0, k)][0] + a[(0, 0)][k]
            elif j == k:
                value = a[(j, j)][0] + a[(0, j)][j]
            else:
                value = 2.0 * a[(j, k)][0] + a[(0, k)][j] + a[(0, j)][k]
            out.append(value)
        return out

    def features(b):
        def words(k, n):
            out = [rows[k, at(b), :]] + [one[i, k, at(b), :] for i in range(3)]
            return out + [two[i, n, at(b), :] for i in range(6)] if n is not None else out

        out = words(2, 1) + third(b)
        out += words(3, 2) + words(1, 0)
        out += words(4, None) + words(0, None)
        out += words(6, 3) + words(7, None) + words(5, None)
        far = HELD * b + 64
        return out + [received[pl.ds(pl.multiple_of(far + 8 * k, 8), 8), :] for k in range(FAR)]

    def fill(group, phi, blocks_of):
        for n in blocks_of:
            columns = slice(128 * n, 128 * n + 128)
            listed = features(GROUP * group + n)
            for i in range(0, FEATURES, 2):
                value = jnp.concatenate([listed[i], listed[i + 1]], axis=0)
                high = value.astype(jnp.bfloat16)
                low = (value - high.astype(jnp.float32)).astype(jnp.bfloat16)
                places = (8 * i, HIGH + 8 * i) if i < WIDE else (8 * i, 8 * (i + REST))
                for place, part in zip(places, (low, high)):
                    phi[place : place + 16, columns] = part

    def multiply(phi, result, blocks_of):
        columns = slice(128 * blocks_of[0], 128 * blocks_of[-1] + 128)
        whole = jnp.dot(matrix[:, :TALL], phi[:, columns], preferred_element_type=jnp.float32)
        rest = jnp.dot(matrix[:, TALL:], phi[SECTION:, columns], preferred_element_type=jnp.float32)
        result[:, columns] = whole + rest

    def add(old, new):
        return new if old is None else old + new

    def reduce(group, result, blocks_of):
        for n in blocks_of:
            columns = slice(128 * n, 128 * n + 128)
            out = pl.ds(pl.multiple_of(8 * (GROUP * group + n), 8), 8)

            def run(number):
                return result[8 * number : 8 * number + 8, columns]

            both = square = None
            firsts, totals = [None] * 6, [None] * 6
            for g in range(4):
                run_a, run_b = run(8 * g), run(8 * g + 1)
                both = add(both, run_a + run_b)
                square = add(square, run_a * run_a + run_b * run_b)
                for i in range(6):
                    gap = run(8 * g + 2 + i)
                    firsts[i] = add(firsts[i], run_b * gap)
                    totals[i] = add(totals[i], gap * gap)
            average = both * 0.125
            mean_out[out, :] = average
            variance_out[out, :] = square * 0.125 - average * average
            for i in range(6):
                first_out[i, out, :] = firsts[i] * 0.25
                total_out[i, out, :] = totals[i] * 0.125

    copies = []

    def finish(part):
        x = pl.ds(part * (size // 4), size // 4)
        for k, (here, there) in enumerate(((mean_out, mean), (variance_out, variance))):
            copies.append(pltpu.make_async_copy(here.at[x, :], there.at[x, :], sems.at[4 * part + k]))
            copies[-1].start()
        for k, (here, there) in enumerate(((first_out, first), (total_out, total))):
            copies.append(pltpu.make_async_copy(here.at[:, x, :], there.at[:, x, :], sems.at[4 * part + 2 + k]))
            copies[-1].start()

    def ahead(group, blocks_of):
        for stage, lead in ((stage2, 3), (stage1, 5)):
            start = GROUP * jnp.minimum(group + lead, groups - 1)
            for n in blocks_of:
                stage(start + n, 0)

    def step(group, now, later):
        for at in range(0, GROUP, 2):
            blocks_of = range(at, at + 2)
            multiply(now[0], now[1], blocks_of)
            fill(jnp.minimum(group + 1, groups - 1), later[0], blocks_of)
            ahead(group, blocks_of)
            reduce(jnp.maximum(group - 1, 0), later[1], blocks_of)

    def body(pair, carry):
        step(2 * pair, (phi_a, result_a), (phi_b, result_b))
        step(2 * pair + 1, (phi_b, result_b), (phi_a, result_a))
        return carry

    fill(0, phi_a, range(GROUP))
    brought.wait()
    many = groups // 8
    for part in range(4):
        lax.fori_loop(part * many, part * many + many, body, 0)
        if part > 0:
            finish(part - 1)
    reduce(groups - 1, result_b, range(GROUP))
    finish(3)
    for copy in copies:
        copy.wait()


def shape(*dims):
    return jax.ShapeDtypeStruct(dims, jnp.float32)


def held(array):
    return pltpu.with_memory_space_constraint(array, pltpu.HBM)


def limit(mib):
    return pltpu.CompilerParams(vmem_limit_bytes=mib * 2**20)


def local(initial, source, table, pairs, owner):
    tile_x, rows_y, cells_z = initial.shape
    servers = lax.axis_size("space")
    group = lax.axis_index("group")
    place = jnp.stack([group, group * servers + lax.axis_index("space")]).astype(jnp.int32)
    all_pairs = lax.all_gather(pairs, "group", axis=0, tiled=True)
    smem = pl.BlockSpec(memory_space=pltpu.SMEM)
    vmem = pl.BlockSpec(memory_space=pltpu.VMEM)
    hbm = pl.BlockSpec(memory_space=pltpu.HBM)
    send = pl.pallas_call(
        pack_kernel,
        out_shape=pltpu.HBM((servers, HELD, cells_z), jnp.float32),
        in_specs=[smem, hbm, hbm, hbm],
        out_specs=hbm,
        scratch_shapes=[
            pltpu.VMEM((8, rows_y + 2 * PAD, cells_z), jnp.float32),
            pltpu.VMEM((8, rows_y + 2 * PAD, cells_z), jnp.float32),
            pltpu.VMEM((servers, HELD, cells_z), jnp.float32),
            pltpu.SMEM((rows_y,), jnp.int32),
            pltpu.SMEM((rows_y,), jnp.int32),
            pltpu.SemaphoreType.DMA((2 * STAGES + 1,)),
            pltpu.SemaphoreType.DMA((STAGES + 1,)),
        ],
        compiler_params=limit(12),
        name="pack",
    )(place, held(owner), held(initial), held(source))
    received = lax.all_to_all(send, "space", split_axis=0, concat_axis=0, tiled=True)
    factor, which = layout()
    matrix = pl.pallas_call(
        coefficient_kernel,
        out_shape=pltpu.HBM((256, DEPTH), jnp.bfloat16),
        in_specs=[smem, smem, smem, smem, vmem, vmem],
        out_specs=vmem,
        compiler_params=limit(8),
        name="coefficients",
    )(table, all_pairs, owner, place, jnp.asarray(factor), jnp.asarray(which))
    cells_x = 8 * servers
    long = cells_x + 2 * PAD
    flat, six = shape(cells_x, cells_z), shape(6, cells_x, cells_z)
    mean, variance, first, total = pl.pallas_call(
        server_kernel,
        out_shape=(flat, flat, six, six),
        in_specs=[vmem, hbm],
        out_specs=(hbm,) * 4,
        scratch_shapes=[
            pltpu.VMEM((8, long, cells_z), jnp.float32),
            pltpu.VMEM((3, 8, long, cells_z), jnp.float32),
            pltpu.VMEM((6, 4, long, cells_z), jnp.float32),
            pltpu.VMEM((TALL, 128 * GROUP), jnp.bfloat16),
            pltpu.VMEM((TALL, 128 * GROUP), jnp.bfloat16),
            pltpu.VMEM((256, 128 * GROUP), jnp.float32),
            pltpu.VMEM((256, 128 * GROUP), jnp.float32),
            pltpu.VMEM(flat.shape, jnp.float32),
            pltpu.VMEM(flat.shape, jnp.float32),
            pltpu.VMEM(six.shape, jnp.float32),
            pltpu.VMEM(six.shape, jnp.float32),
            pltpu.VMEM((256, DEPTH), jnp.bfloat16),
            pltpu.SemaphoreType.DMA((1,)),
            pltpu.SemaphoreType.DMA((16,)),
        ],
        compiler_params=limit(40),
        name="server",
    )(received.reshape(-1, cells_z), held(matrix))
    return (
        mean.reshape(cells_x, 1, cells_z),
        variance.reshape(cells_x, 1, cells_z),
        first.reshape(6, cells_x, 1, cells_z),
        total.reshape(6, cells_x, 1, cells_z),
    )


def solution(mesh):
    placed = (P("space", None, None), P("space", None, None), P(), P("group", None), P())
    return jax.shard_map(
        local,
        mesh=mesh,
        in_specs=placed,
        out_specs=(
            P(None, ("group", "space"), None),
            P(None, ("group", "space"), None),
            P(None, None, ("group", "space"), None),
            P(None, None, ("group", "space"), None),
        ),
        check_vma=False,
    )
```

time: 111 us -> 107 us (0.964)
  waiting for transfers between devices: 36.5 us -> 59.8 us
  Pallas kernels: 43.2 us -> 23.4 us
  starting transfers between devices: 18.8 us -> 13.1 us
  local copies, waits for them, and re-layouts: 4.28 us -> 0.03 us
  blocking collectives: 7.3 us -> 9.84 us
    all_to_all x2 -> x1, waiting for transfers between devices: 36.5 us -> 59.8 us  [local(): lax.all_to_all(send, 'space', split_axis=0, concat_axis=0, tiled=True)]
    pallas_call x5 -> x3, Pallas kernels: 43.2 us -> 23.4 us  [the longest x1 15.4 us: local(): pl.pallas_call(server_kernel, out_shape=(flat, flat, six, six), in_specs=...]
    all_to_all x2 -> x1, starting transfers between devices: 18.8 us -> 13.1 us  [local(): lax.all_to_all(send, 'space', split_axis=0, concat_axis=0, tiled=True)]
    unnamed x20 -> x10, local copies, waits for them, and re-layouts: 4.28 us -> 0.03 us
    all_gather x1, blocking collectives: 7.3 us -> 9.84 us  [local(): all_pairs = lax.all_gather(pairs, 'group', axis=0, tiled=True)]
  transfers between devices with their start and end apart: 2 -> 1, of which waited for: 2 -> 1; matrix products, arithmetic and copies ran while one was open for 0% -> 0% of each run, Pallas kernels for 29% -> 4%
where the time goes in v5:
time: 107 us
  waiting for transfers between devices  59.8 us (56%)
  Pallas kernels  23.4 us (22%)
  starting transfers between devices  13.1 us (12%)
  blocking collectives  9.84 us (9%)
    all_to_all x1, waiting for transfers between devices, local(): lax.all_to_all(send, 'space', split_axis=0, concat_axis=0, tiled=True)  59.8 us
    pallas_call x1, Pallas kernels, local(): pl.pallas_call(server_kernel, out_shape=(flat, flat, six, six), in_specs=...  15.4 us
    all_to_all x1, starting transfers between devices, local(): lax.all_to_all(send, 'space', split_axis=0, concat_axis=0, tiled=True)  13.1 us
    all_gather x1, blocking collectives, local(): all_pairs = lax.all_gather(pairs, 'group', axis=0, tiled=True)  9.84 us
    pallas_call x1, Pallas kernels, local(): pl.pallas_call(coefficient_kernel, out_shape=pltpu.HBM((256, DEPTH), jnp....  4.24 us
    pallas_call x1, Pallas kernels, local(): pl.pallas_call(pack_kernel, out_shape=pltpu.HBM((servers, HELD, cells_z),...  3.71 us
  transfers between devices with their start and end apart: 1, of which 1 were waited for; matrix products, arithmetic and copies ran while one was open for 0% of the time, Pallas kernels for 4%

profile of v5, /device:TPU:6, one launch (start us, length us, event | category | flops | bytes accessed | tf_op | source)
XLA Modules:
  0.0 106.9 jit_solution(12937109204824830064)
XLA Ops:
  0.6 0.1 pad_add_fusion.place
  0.7 3.7 %pack.1 = f32[64,96,128]{2,1,0:T(8,128)} custom-call(s32[2]{0:T(128)S(1)} %pad_add_fusion.place, s32[256]{0:T(256)} %owner.1, f32[8,256,128]{2,1,0:T(8,128)} %initial.1, f32[8,256,128]{2,1,0:T(8,128)} %source.1), custom_call_target="tpu_custom_call" | custom-call | tf_op jit(solution)/shard_map/pack/pallas_call | solution.py:387
  4.4 0.0 copy-start.4
  4.4 0.0 copy-start
  4.5 0.0 copy-start.1
  4.5 0.0 copy-start.2
  4.5 0.0 copy-start.3
  4.5 13.1 %all-to-all-start = ((f32[64,96,128]{2,1,0:T(8,128)}), f32[64,96,128]{2,1,0:T(8,128)S(1)}, u32[]{:S(2)}, u32[]{:S(2)}) async-start(f32[64,96,128]{2,1,0:T(8,128)} %pack.1), calls=%async_computation | async-start | bytes 6291456 | tf_op jit(solution)/shard_map/all_to_all | solution.py:404
  17.6 0.0 copy-done.4
  17.6 9.8 %all-gather = s32[4,1,2]{2,1,0:T(1,128)S(1)} all-gather(s32[1,1,2]{2,1,0:T(1,128)S(1)} %bitcast.19), channel_id=1, replica_groups=mesh['group'=4,'space'=64] {'group'}, dimensions={0}, use_global_device_ids=true | all-gather | bytes 40 | tf_op jit(solution)/shard_map/all_gather | solution.py:383
  27.5 0.0 copy-done
  27.5 0.0 copy-done.1
  27.5 0.0 copy-done.2
  27.5 0.0 copy-done.3
  27.5 4.2 %coefficients.1.matrix_there = bf16[256,1792]{1,0:T(8,128)(2,1)} custom-call(f32[8,6]{1,0:T(8,128)S(1)} %copy-done.1, s32[4,2]{1,0:T(4,128)S(1)} %bitcast.18, s32[256]{0:T(256)S(1)} %copy-done.2, s32[2]{0:T(128)S(1)} %pad_add_fusion.place, f32[1,640]{1,0:T(1,128)S(1)} %copy-done.3, s32[3,640]{1,0:T(4,128)S(1)} %copy-done), custom_call_target="tpu_custom_call" | custom-call | tf_op jit(solution)/shard_map/coefficients/pallas_call | solution.py:406
  31.7 59.8 %all-to-all-done = f32[64,96,128]{2,1,0:T(8,128)S(1)} async-done(((f32[64,96,128]{2,1,0:T(8,128)}), f32[64,96,128]{2,1,0:T(8,128)S(1)}, u32[]{:S(2)}, u32[]{:S(2)}) %all-to-all-start) | async-done | bytes 3145760 | tf_op jit(solution)/shard_map/all_to_all | solution.py:404
  91.5 15.4 %server.1 = (f32[512,128]{1,0:T(8,128)}, f32[512,128]{1,0:T(8,128)}, f32[6,512,128]{2,1,0:T(8,128)}, f32[6,512,128]{2,1,0:T(8,128)}) custom-call(f32[6144,128]{1,0:T(8,128)S(1)} %bitcast.17, bf16[256,1792]{1,0:T(8,128)(2,1)} %coefficients.1.matrix_there), custom_call_target="tpu_custom_call" | custom-call | tf_op jit(solution)/shard_map/server/pallas_call | solution.py:417
Async XLA Ops:
  4.4 13.2 %copy-start.4 = (s32[1,2]{1,0:T(1,128)S(1)}, s32[1,2]{1,0:T(1,128)}, u32[]{:S(2)}) copy-start(s32[1,2]{1,0:T(1,128)} %param.10) | copy-start | bytes 28
  4.4 23.0 %copy-start = (s32[3,640]{1,0:T(4,128)S(1)}, s32[3,640]{1,0:T(4,128)}, u32[]{:S(2)}) copy-start(s32[3,640]{1,0:T(4,128)} %constant.16.clone.which) | copy-start | bytes 23044
  4.5 23.0 %copy-start.1 = (f32[8,6]{1,0:T(8,128)S(1)}, f32[8,6]{1,0:T(8,128)}, u32[]{:S(2)}) copy-start(f32[8,6]{1,0:T(8,128)} %table.1) | copy-start | bytes 580
  4.5 23.0 %copy-start.2 = (s32[256]{0:T(256)S(1)}, s32[256]{0:T(256)}, u32[]{:S(2)}) copy-start(s32[256]{0:T(256)} %owner.1) | copy-start | bytes 3076
  4.5 23.0 %copy-start.3 = (f32[1,640]{1,0:T(1,128)S(1)}, f32[1,640]{1,0:T(1,128)}, u32[]{:S(2)}) copy-start(f32[1,640]{1,0:T(1,128)} %constant.15.clone.factor) | copy-start | bytes 7684
  4.5 87.0 %all-to-all-start = ((f32[64,96,128]{2,1,0:T(8,128)}), f32[64,96,128]{2,1,0:T(8,128)S(1)}, u32[]{:S(2)}, u32[]{:S(2)}) async-start(f32[64,96,128]{2,1,0:T(8,128)} %pack.1), calls=%async_computation | async-start | bytes 6291456 | tf_op jit(solution)/shard_map/all_to_all | solution.py:404

commit v6 on v5

--- a/solution.py
+++ b/solution.py
@@ -146,6 +146,7 @@
     ways = inside(1) + inside(-1)
     ways_up = inside(2) + 1.0 + inside(-1)
     ways_down = inside(-2) + 1.0 + inside(1)
+    bases = []
     for group in range(4):
         first, second = pairs[group, 0], pairs[group, 1]
         q = []
@@ -180,7 +181,12 @@
                     chosen = jnp.where(index == number, value, chosen)
                 product = product * chosen
             split = product.reshape(8, 8, 128)
-            split = jnp.concatenate([split[:2], split[2:] - split[:1]], axis=0)
+            if group == 0:
+                bases.append(split[:1])
+                near = [split[:1], split[1:2] - split[:1]]
+            else:
+                near = [split[:2] - bases[chunk]]
+            split = jnp.concatenate(near + [split[2:] - split[:1]], axis=0)
             product = jnp.where(same, split.reshape(64, 128), 0.0)
             high = product.astype(jnp.bfloat16)
             low = product - high.astype(jnp.float32)
@@ -305,16 +311,22 @@
 
             both = square = None
             firsts, totals = [None] * 6, [None] * 6
+            base = run(0)
             for g in range(4):
-                run_a, run_b = run(8 * g), run(8 * g + 1)
-                both = add(both, run_a + run_b)
-                square = add(square, run_a * run_a + run_b * run_b)
+                run_b = run(8 * g + 1)
+                if g > 0:
+                    run_a = run(8 * g)
+                    both = add(both, run_a)
+                    square = add(square, run_a * run_a)
+                both = add(both, run_b)
+                square = add(square, run_b * run_b)
+                run_b = base + run_b
                 for i in range(6):
                     gap = run(8 * g + 2 + i)
                     firsts[i] = add(firsts[i], run_b * gap)
                     totals[i] = add(totals[i], gap * gap)
             average = both * 0.125
-            mean_out[out, :] = average
+            mean_out[out, :] = base + average
             variance_out[out, :] = square * 0.125 - average * average
             for i in range(6):
                 first_out[i, out, :] = firsts[i] * 0.25
@@ -341,9 +353,9 @@
         for at in range(0, GROUP, 2):
             blocks_of = range(at, at + 2)
             multiply(now[0], now[1], blocks_of)
+            reduce(jnp.maximum(group - 1, 0), later[1], blocks_of)
             fill(jnp.minimum(group + 1, groups - 1), later[0], blocks_of)
             ahead(group, blocks_of)
-            reduce(jnp.maximum(group - 1, 0), later[1], blocks_of)
 
     def body(pair, carry):
         step(2 * pair, (phi_a, result_a), (phi_b, result_b))

time: 107 us -> 107 us (level)
  no operation moved by 1% of the time
where the time goes in v6:
time: 107 us
  waiting for transfers between devices  59.7 us (56%)
  Pallas kernels  23.2 us (22%)
  starting transfers between devices  13.1 us (12%)
  blocking collectives  9.84 us (9%)
    all_to_all x1, waiting for transfers between devices, local(): lax.all_to_all(send, 'space', split_axis=0, concat_axis=0, tiled=True)  59.7 us
    pallas_call x1, Pallas kernels, local(): pl.pallas_call(server_kernel, out_shape=(flat, flat, six, six), in_specs=...  15.2 us
    all_to_all x1, starting transfers between devices, local(): lax.all_to_all(send, 'space', split_axis=0, concat_axis=0, tiled=True)  13.1 us
    all_gather x1, blocking collectives, local(): all_pairs = lax.all_gather(pairs, 'group', axis=0, tiled=True)  9.84 us
    pallas_call x1, Pallas kernels, local(): pl.pallas_call(coefficient_kernel, out_shape=pltpu.HBM((256, DEPTH), jnp....  4.25 us
    pallas_call x1, Pallas kernels, local(): pl.pallas_call(pack_kernel, out_shape=pltpu.HBM((servers, HELD, cells_z),...  3.71 us
  transfers between devices with their start and end apart: 1, of which 1 were waited for; matrix products, arithmetic and copies ran while one was open for 0% of the time, Pallas kernels for 4%

profile of v6, /device:TPU:6, one launch (start us, length us, event | category | flops | bytes accessed | tf_op | source)
XLA Modules:
  0.0 106.7 jit_solution(2255038476530522835)
XLA Ops:
  0.6 0.1 pad_add_fusion.place
  0.7 3.7 %pack.1 = f32[64,96,128]{2,1,0:T(8,128)} custom-call(s32[2]{0:T(128)S(1)} %pad_add_fusion.place, s32[256]{0:T(256)} %owner.1, f32[8,256,128]{2,1,0:T(8,128)} %initial.1, f32[8,256,128]{2,1,0:T(8,128)} %source.1), custom_call_target="tpu_custom_call" | custom-call | tf_op jit(solution)/shard_map/pack/pallas_call | solution.py:399
  4.4 0.0 copy-start.4
  4.4 0.0 copy-start
  4.5 0.0 copy-start.1
  4.5 0.0 copy-start.2
  4.5 0.0 copy-start.3
  4.5 13.1 %all-to-all-start = ((f32[64,96,128]{2,1,0:T(8,128)}), f32[64,96,128]{2,1,0:T(8,128)S(1)}, u32[]{:S(2)}, u32[]{:S(2)}) async-start(f32[64,96,128]{2,1,0:T(8,128)} %pack.1), calls=%async_computation | async-start | bytes 6291456 | tf_op jit(solution)/shard_map/all_to_all | solution.py:416
  17.6 0.0 copy-done.4
  17.6 9.8 %all-gather = s32[4,1,2]{2,1,0:T(1,128)S(1)} all-gather(s32[1,1,2]{2,1,0:T(1,128)S(1)} %bitcast.19), channel_id=1, replica_groups=mesh['group'=4,'space'=64] {'group'}, dimensions={0}, use_global_device_ids=true | all-gather | bytes 40 | tf_op jit(solution)/shard_map/all_gather | solution.py:395
  27.5 0.0 copy-done
  27.5 0.0 copy-done.1
  27.5 0.0 copy-done.2
  27.5 0.0 copy-done.3
  27.5 4.2 %coefficients.1.matrix_there = bf16[256,1792]{1,0:T(8,128)(2,1)} custom-call(f32[8,6]{1,0:T(8,128)S(1)} %copy-done.1, s32[4,2]{1,0:T(4,128)S(1)} %bitcast.18, s32[256]{0:T(256)S(1)} %copy-done.2, s32[2]{0:T(128)S(1)} %pad_add_fusion.place, f32[1,640]{1,0:T(1,128)S(1)} %copy-done.3, s32[3,640]{1,0:T(4,128)S(1)} %copy-done), custom_call_target="tpu_custom_call" | custom-call | tf_op jit(solution)/shard_map/coefficients/pallas_call | solution.py:418
  31.7 59.7 %all-to-all-done = f32[64,96,128]{2,1,0:T(8,128)S(1)} async-done(((f32[64,96,128]{2,1,0:T(8,128)}), f32[64,96,128]{2,1,0:T(8,128)S(1)}, u32[]{:S(2)}, u32[]{:S(2)}) %all-to-all-start) | async-done | bytes 3145760 | tf_op jit(solution)/shard_map/all_to_all | solution.py:416
  91.5 15.2 %server.1 = (f32[512,128]{1,0:T(8,128)}, f32[512,128]{1,0:T(8,128)}, f32[6,512,128]{2,1,0:T(8,128)}, f32[6,512,128]{2,1,0:T(8,128)}) custom-call(f32[6144,128]{1,0:T(8,128)S(1)} %bitcast.17, bf16[256,1792]{1,0:T(8,128)(2,1)} %coefficients.1.matrix_there), custom_call_target="tpu_custom_call" | custom-call | tf_op jit(solution)/shard_map/server/pallas_call | solution.py:429
Async XLA Ops:
  4.4 13.2 %copy-start.4 = (s32[1,2]{1,0:T(1,128)S(1)}, s32[1,2]{1,0:T(1,128)}, u32[]{:S(2)}) copy-start(s32[1,2]{1,0:T(1,128)} %param.10) | copy-start | bytes 28
  4.4 23.0 %copy-start = (s32[3,640]{1,0:T(4,128)S(1)}, s32[3,640]{1,0:T(4,128)}, u32[]{:S(2)}) copy-start(s32[3,640]{1,0:T(4,128)} %constant.16.clone.which) | copy-start | bytes 23044
  4.5 23.0 %copy-start.1 = (f32[8,6]{1,0:T(8,128)S(1)}, f32[8,6]{1,0:T(8,128)}, u32[]{:S(2)}) copy-start(f32[8,6]{1,0:T(8,128)} %table.1) | copy-start | bytes 580
  4.5 23.0 %copy-start.2 = (s32[256]{0:T(256)S(1)}, s32[256]{0:T(256)}, u32[]{:S(2)}) copy-start(s32[256]{0:T(256)} %owner.1) | copy-start | bytes 3076
  4.5 23.0 %copy-start.3 = (f32[1,640]{1,0:T(1,128)S(1)}, f32[1,640]{1,0:T(1,128)}, u32[]{:S(2)}) copy-start(f32[1,640]{1,0:T(1,128)} %constant.15.clone.factor) | copy-start | bytes 7684
  4.5 87.0 %all-to-all-start = ((f32[64,96,128]{2,1,0:T(8,128)}), f32[64,96,128]{2,1,0:T(8,128)S(1)}, u32[]{:S(2)}, u32[]{:S(2)}) async-start(f32[64,96,128]{2,1,0:T(8,128)} %pack.1), calls=%async_computation | async-start | bytes 6291456 | tf_op jit(solution)/shard_map/all_to_all | solution.py:416

commit v7 on v6

--- a/solution.py
+++ b/solution.py
@@ -85,7 +85,7 @@
     for ref in (padded_u, padded_s):
         for x in range(8):
             ref[x, :PAD] = jnp.zeros((PAD, 128), jnp.float32)
-            ref[x, PAD + count :] = jnp.zeros((PAD, 128), jnp.float32)
+            ref[x, PAD + count :] = jnp.zeros((2 * PAD, 128), jnp.float32)
     group = place[0]
     listed.wait()
 
@@ -116,11 +116,11 @@
     def fill_far(s, carry):
         p = inverse[group * servers + s] + PAD
         for k, (ref, step) in enumerate(((flat_u, -3), (flat_u, 3), (flat_s, -2), (flat_s, 2))):
-            ready[s, 64 + 8 * k : 72 + 8 * k, :] = ref[pl.ds(p + step, 8, stride=count + 2 * PAD), :]
-        return carry
-
-    flat_u = padded_u.reshape(8 * (count + 2 * PAD), 128)
-    flat_s = padded_s.reshape(8 * (count + 2 * PAD), 128)
+            ready[s, 64 + 8 * k : 72 + 8 * k, :] = ref[pl.ds(p + step, 8, stride=count + 3 * PAD), :]
+        return carry
+
+    flat_u = padded_u.reshape(8 * (count + 3 * PAD), 128)
+    flat_s = padded_s.reshape(8 * (count + 3 * PAD), 128)
     lax.fori_loop(0, servers, fill_far, 0, unroll=4)
     here = pl.ds(64, 32)
     sent.append(pltpu.make_async_copy(ready.at[:, here], send.at[:, here], out_sems.at[STAGES]))
@@ -402,8 +402,8 @@
         in_specs=[smem, hbm, hbm, hbm],
         out_specs=hbm,
         scratch_shapes=[
-            pltpu.VMEM((8, rows_y + 2 * PAD, cells_z), jnp.float32),
-            pltpu.VMEM((8, rows_y + 2 * PAD, cells_z), jnp.float32),
+            pltpu.VMEM((8, rows_y + 3 * PAD, cells_z), jnp.float32),
+            pltpu.VMEM((8, rows_y + 3 * PAD, cells_z), jnp.float32),
             pltpu.VMEM((servers, HELD, cells_z), jnp.float32),
             pltpu.SMEM((rows_y,), jnp.int32),
             pltpu.SMEM((rows_y,), jnp.int32),

time: 107 us -> 107 us (level)
  no operation moved by 1% of the time
where the time goes in v7:
time: 107 us
  waiting for transfers between devices  59.7 us (56%)
  Pallas kernels  23.1 us (22%)
  starting transfers between devices  13.1 us (12%)
  blocking collectives  9.84 us (9%)
    all_to_all x1, waiting for transfers between devices, local(): lax.all_to_all(send, 'space', split_axis=0, concat_axis=0, tiled=True)  59.7 us
    pallas_call x1, Pallas kernels, local(): pl.pallas_call(server_kernel, out_shape=(flat, flat, six, six), in_specs=...  15.3 us
    all_to_all x1, starting transfers between devices, local(): lax.all_to_all(send, 'space', split_axis=0, concat_axis=0, tiled=True)  13.1 us
    all_gather x1, blocking collectives, local(): all_pairs = lax.all_gather(pairs, 'group', axis=0, tiled=True)  9.84 us
    pallas_call x1, Pallas kernels, local(): pl.pallas_call(coefficient_kernel, out_shape=pltpu.HBM((256, DEPTH), jnp....  4.25 us
    pallas_call x1, Pallas kernels, local(): pl.pallas_call(pack_kernel, out_shape=pltpu.HBM((servers, HELD, cells_z),...  3.58 us
  transfers between devices with their start and end apart: 1, of which 1 were waited for; matrix products, arithmetic and copies ran while one was open for 0% of the time, Pallas kernels for 4%

profile of v7, /device:TPU:6, one launch (start us, length us, event | category | flops | bytes accessed | tf_op | source)
XLA Modules:
  0.0 106.6 jit_solution(14959605090049290614)
XLA Ops:
  0.6 0.1 pad_add_fusion.place
  0.7 3.6 %pack.1 = f32[64,96,128]{2,1,0:T(8,128)} custom-call(s32[2]{0:T(128)S(1)} %pad_add_fusion.place, s32[256]{0:T(256)} %owner.1, f32[8,256,128]{2,1,0:T(8,128)} %initial.1, f32[8,256,128]{2,1,0:T(8,128)} %source.1), custom_call_target="tpu_custom_call" | custom-call | tf_op jit(solution)/shard_map/pack/pallas_call | solution.py:399
  4.3 0.0 copy-start.4
  4.3 0.0 copy-start
  4.3 0.0 copy-start.1
  4.3 0.0 copy-start.2
  4.3 0.0 copy-start.3
  4.4 13.1 %all-to-all-start = ((f32[64,96,128]{2,1,0:T(8,128)}), f32[64,96,128]{2,1,0:T(8,128)S(1)}, u32[]{:S(2)}, u32[]{:S(2)}) async-start(f32[64,96,128]{2,1,0:T(8,128)} %pack.1), calls=%async_computation | async-start | bytes 6291456 | tf_op jit(solution)/shard_map/all_to_all | solution.py:416
  17.5 0.0 copy-done.4
  17.5 9.8 %all-gather = s32[4,1,2]{2,1,0:T(1,128)S(1)} all-gather(s32[1,1,2]{2,1,0:T(1,128)S(1)} %bitcast.19), channel_id=1, replica_groups=mesh['group'=4,'space'=64] {'group'}, dimensions={0}, use_global_device_ids=true | all-gather | bytes 40 | tf_op jit(solution)/shard_map/all_gather | solution.py:395
  27.3 0.0 copy-done
  27.3 0.0 copy-done.1
  27.3 0.0 copy-done.2
  27.3 0.0 copy-done.3
  27.3 4.2 %coefficients.1.matrix_there = bf16[256,1792]{1,0:T(8,128)(2,1)} custom-call(f32[8,6]{1,0:T(8,128)S(1)} %copy-done.1, s32[4,2]{1,0:T(4,128)S(1)} %bitcast.18, s32[256]{0:T(256)S(1)} %copy-done.2, s32[2]{0:T(128)S(1)} %pad_add_fusion.place, f32[1,640]{1,0:T(1,128)S(1)} %copy-done.3, s32[3,640]{1,0:T(4,128)S(1)} %copy-done), custom_call_target="tpu_custom_call" | custom-call | tf_op jit(solution)/shard_map/coefficients/pallas_call | solution.py:418
  31.6 59.7 %all-to-all-done = f32[64,96,128]{2,1,0:T(8,128)S(1)} async-done(((f32[64,96,128]{2,1,0:T(8,128)}), f32[64,96,128]{2,1,0:T(8,128)S(1)}, u32[]{:S(2)}, u32[]{:S(2)}) %all-to-all-start) | async-done | bytes 3145760 | tf_op jit(solution)/shard_map/all_to_all | solution.py:416
  91.3 15.3 %server.1 = (f32[512,128]{1,0:T(8,128)}, f32[512,128]{1,0:T(8,128)}, f32[6,512,128]{2,1,0:T(8,128)}, f32[6,512,128]{2,1,0:T(8,128)}) custom-call(f32[6144,128]{1,0:T(8,128)S(1)} %bitcast.17, bf16[256,1792]{1,0:T(8,128)(2,1)} %coefficients.1.matrix_there), custom_call_target="tpu_custom_call" | custom-call | tf_op jit(solution)/shard_map/server/pallas_call | solution.py:429
Async XLA Ops:
  4.3 13.2 %copy-start.4 = (s32[1,2]{1,0:T(1,128)S(1)}, s32[1,2]{1,0:T(1,128)}, u32[]{:S(2)}) copy-start(s32[1,2]{1,0:T(1,128)} %param.10) | copy-start | bytes 28
  4.3 23.0 %copy-start = (s32[3,640]{1,0:T(4,128)S(1)}, s32[3,640]{1,0:T(4,128)}, u32[]{:S(2)}) copy-start(s32[3,640]{1,0:T(4,128)} %constant.16.clone.which) | copy-start | bytes 23044
  4.3 23.0 %copy-start.1 = (f32[8,6]{1,0:T(8,128)S(1)}, f32[8,6]{1,0:T(8,128)}, u32[]{:S(2)}) copy-start(f32[8,6]{1,0:T(8,128)} %table.1) | copy-start | bytes 580
  4.3 23.0 %copy-start.2 = (s32[256]{0:T(256)S(1)}, s32[256]{0:T(256)}, u32[]{:S(2)}) copy-start(s32[256]{0:T(256)} %owner.1) | copy-start | bytes 3076
  4.3 23.0 %copy-start.3 = (f32[1,640]{1,0:T(1,128)S(1)}, f32[1,640]{1,0:T(1,128)}, u32[]{:S(2)}) copy-start(f32[1,640]{1,0:T(1,128)} %constant.15.clone.factor) | copy-start | bytes 7684
  4.4 87.0 %all-to-all-start = ((f32[64,96,128]{2,1,0:T(8,128)}), f32[64,96,128]{2,1,0:T(8,128)S(1)}, u32[]{:S(2)}, u32[]{:S(2)}) async-start(f32[64,96,128]{2,1,0:T(8,128)} %pack.1), calls=%async_computation | async-start | bytes 6291456 | tf_op jit(solution)/shard_map/all_to_all | solution.py:416
